TPU v7x, 32 devices: a whole 2x2x4 slice. The times are simulated.
32 devices in a mesh: dp: 8 (over z, y), expert: 2 (over core), col: 2 (over x).
Axes of the slice: x: 2, y: 2, z: 4, core: 2. Of those that a mesh axis runs over, the one named last changes fastest.
Arguments:
- tokens: bfloat16 [8192, 1536], P(('dp', 'expert'), 'col'), may hold values from -6 to 6
- gain_attn: float32 [1536], P('col'), may hold values from 0.5 to 1.5
- w_query: bfloat16 [1536, 1536], P('col', 'expert'), may hold values from -0.625 to 0.625
- key_matrix: bfloat16 [1536, 512], P('col', 'expert'), may hold values from -0.625 to 0.625
- value_matrix: bfloat16 [1536, 512], P('col', 'expert'), may hold values from -0.15625 to 0.15625
- w_out: bfloat16 [1536, 1536], P('expert', 'col'), may hold values from -2.5 to 2.5
- gain_moe: float32 [1536], P('col'), may hold values from 0.5 to 1.5
- w_router: bfloat16 [1536, 40], P('col'), may hold values from -0.078125 to 0.078125
- w_gate: bfloat16 [40, 1536, 512], P('expert', 'col'), may hold values from -0.15625 to 0.15625
- w_up: bfloat16 [40, 1536, 512], P('expert', 'col'), may hold values from -0.15625 to 0.15625
- w_down: bfloat16 [40, 512, 1536], P('expert', None, 'col'), may hold values from -4 to 4
- segments: int32 [16, 512], P('dp'), may hold values from 0 to 3, never falling along the last dimension, each value on 1 to 256 neighbouring positions
- routes: int32 [8192, 8], P(('dp', 'expert')), may hold values from 0 to 39, all different within a row; in each aligned block of 512 rows (0 to 511, 512 to 1023, ...) at most 192 rows name the same one
- cotangent: bfloat16 [8192, 1536], P(('dp', 'expert'), 'col'), may hold values from -6 to 6
Outputs:
- output: float32 [8192, 1536], P(('dp', 'expert'), 'col')
- grad_tokens: float32 [8192, 1536], P(('dp', 'expert'), 'col')
- grad_gain_attn: float32 [1536], P('col')
- grad_query: float32 [1536, 1536], P('col', 'expert')
- grad_key: float32 [1536, 512], P('col', 'expert')
- grad_value: float32 [1536, 512], P('col', 'expert')
- grad_out: float32 [1536, 1536], P('expert', 'col')
- grad_gain_moe: float32 [1536], P('col')
- grad_router: float32 [1536, 40], P('col')
- grad_gate: float32 [40, 1536, 512], P('expert', 'col', 'dp')
- grad_up: float32 [40, 1536, 512], P('expert', 'col', 'dp')
- grad_down: float32 [40, 512, 1536], P('expert', 'dp', 'col')
Inputs may be any that keep to these rules, and one draw needn't show every extreme that they name: `routes`: in each aligned block of 512 rows (one sequence) no expert is named by more than 192 rows, and one expert is named by exactly 192 rows in some blocks. `segments`: never falls along a sequence; a document has 1 to 256 tokens, one of them exactly that many.
All inputs are finite; a program needn't handle non-finite values.
Results may differ from a plain program's by a relative error of at most 0.017.
Values may be sent and summed in bfloat16 or wider, within the bound.
A program may use at most 384 MiB of HBM per device.

v0:
```python
import math

import jax
import jax.numpy as jnp
from jax import lax
from jax.sharding import PartitionSpec as P

HEAD_WIDTH = 64
CAP = 192


EPS = 1e-06
RESIDUAL = 0.22
SCORE_SCALE = 0.015625
THETA = 10000.0
NEG = -1000000000.0
HIGHEST = lax.Precision.HIGHEST


def doc_positions(seg_row):
    length_total = seg_row.shape[0]
    index = jnp.arange(length_total, dtype=jnp.int32)
    before = jnp.concatenate([jnp.full((1,), -1, jnp.int32), seg_row[:-1]])
    starts = jnp.where(seg_row != before, index, 0)
    return index - lax.cummax(starts, axis=0)


def rope_tables(positions, head_size):
    half = head_size // 2
    freq = jnp.exp(jnp.arange(half, dtype=jnp.float32) * (-2.0 * math.log(THETA) / head_size))
    angle = positions.astype(jnp.float32)[:, None] * freq[None, :]
    return (jnp.cos(angle)[:, None, :], jnp.sin(angle)[:, None, :])


def apply_rotation(heads, cosine_table, sine_table):
    half = heads.shape[-1] // 2
    first = heads[..., :half]
    second = heads[..., half:]
    return jnp.concatenate(
        [first * cosine_table - second * sine_table, second * cosine_table + first * sine_table], -1
    )


def unrotate(grads, cosine_table, sine_table):
    half = grads.shape[-1] // 2
    first = grads[..., :half]
    second = grads[..., half:]
    return jnp.concatenate(
        [first * cosine_table + second * sine_table, second * cosine_table - first * sine_table], -1
    )


def slot_targets(route_rows, capacity, count):
    flat = route_rows.reshape(-1)
    onehot = (flat[:, None] == jnp.arange(count, dtype=jnp.int32)[None, :]).astype(jnp.int32)
    before = jnp.cumsum(onehot, 0) - onehot
    slot = jnp.sum(before * onehot, 1)
    return flat * capacity + slot


def allowed_mask(seg_row, start, block):
    length_total = seg_row.shape[0]
    query_index = start + jnp.arange(block)
    key_index = jnp.arange(length_total)
    same = seg_row[:, None] == seg_row[None, :]
    return same & (key_index[None, :] <= query_index[:, None])


def block_scores(q_part, key_rows, seg_row, start, block):
    scores = (
        jnp.einsum("qkgd,skd->kgqs", q_part, key_rows, preferred_element_type=jnp.float32)
        * SCORE_SCALE
    )
    return jnp.where(allowed_mask(seg_row, start, block), scores, NEG)


def attend_forward(query_rows, key_rows, value_rows, seg_row, block):
    scores = block_scores(query_rows, key_rows, seg_row, 0, block)
    peak = jnp.max(scores, -1, keepdims=True)
    expo = jnp.exp(scores - peak)
    total = jnp.sum(expo, -1, keepdims=True)
    probs = (expo / total).astype(jnp.bfloat16)
    outputs = jnp.einsum("kgqs,skd->qkgd", probs, value_rows, preferred_element_type=jnp.float32)
    totals = peak + jnp.log(total)
    return (outputs, totals)


def attend_backward(query_rows, key_rows, value_rows, seg_row, block, totals, grad_mixed):
    scores = block_scores(query_rows, key_rows, seg_row, 0, block)
    probs = jnp.exp(scores - totals)
    slope = jnp.einsum("qkgd,skd->kgqs", grad_mixed, value_rows, preferred_element_type=jnp.float32)
    delta = jnp.sum(probs * slope, -1, keepdims=True)
    dscore = (probs * (slope - delta)).astype(jnp.bfloat16)
    grad_queries = (
        jnp.einsum("kgqs,skd->qkgd", dscore, key_rows, preferred_element_type=jnp.float32)
        * SCORE_SCALE
    )
    grad_keys = (
        jnp.einsum("kgqs,qkgd->skd", dscore, query_rows, preferred_element_type=jnp.float32)
        * SCORE_SCALE
    )
    grad_values = jnp.einsum(
        "kgqs,qkgd->skd", probs.astype(jnp.bfloat16), grad_mixed, preferred_element_type=jnp.float32
    )
    return (grad_queries, grad_keys, grad_values)


def grid_rows(inputs, matrix, rows):
    gathered = lax.all_gather(inputs, "expert", axis=0, tiled=True)

    def product_term(start, count):
        return jnp.dot(gathered, matrix, preferred_element_type=jnp.float32)

    return (
        gathered,
        lax.psum_scatter(
            product_term(jnp.int32(0), rows * lax.axis_size("col")),
            "col",
            scatter_dimension=0,
            tiled=True,
        ),
    )


def grid_cols(inputs, matrix, rows):
    gathered = lax.all_gather(inputs, "col", axis=0, tiled=True)

    def product_term(start, count):
        return jnp.dot(gathered, matrix, preferred_element_type=jnp.float32)

    return (
        gathered,
        lax.psum_scatter(
            product_term(jnp.int32(0), rows * lax.axis_size("expert")),
            "expert",
            scatter_dimension=0,
            tiled=True,
        ),
    )


def across_col(value):
    return lax.psum(value, "col")


def to_experts(buffer):
    return lax.all_to_all(buffer, "expert", split_axis=0, concat_axis=0, tiled=True)


def from_experts(buffer):
    return lax.all_to_all(buffer, "expert", split_axis=0, concat_axis=0, tiled=True)


def share_sum(product_term, rows):
    return lax.psum_scatter(
        product_term(jnp.int32(0), rows * lax.axis_size("col")),
        "col",
        scatter_dimension=0,
        tiled=True,
    )


def share_gather(value_rows):
    return lax.all_gather(value_rows, "col", axis=0, tiled=True)


def spread_expert_grads(grad_gate, grad_up, grad_down):
    return (
        lax.psum_scatter(grad_gate, "dp", scatter_dimension=2, tiled=True),
        lax.psum_scatter(grad_up, "dp", scatter_dimension=2, tiled=True),
        lax.psum_scatter(grad_down, "dp", scatter_dimension=1, tiled=True),
    )


def on_device(
    tokens,
    gain_attn,
    w_query,
    key_matrix,
    value_matrix,
    w_out,
    gain_moe,
    w_router,
    w_gate,
    w_up,
    w_down,
    segments,
    routes,
    cotangent,
):
    inputs = tokens.astype(jnp.float32)
    length_total, part = inputs.shape
    width = part * lax.axis_size("col")
    inv_first = lax.rsqrt(across_col(jnp.sum(inputs * inputs, 1)) / width + EPS)
    normalized_input = (inputs * inv_first[:, None] * gain_attn).astype(jnp.bfloat16)
    w_qkv = jnp.concatenate([w_query, key_matrix, value_matrix], 1)
    q_width = w_query.shape[1]
    kv_width = key_matrix.shape[1]
    q_heads = q_width // HEAD_WIDTH
    kv_heads = kv_width // HEAD_WIDTH
    group_size = q_heads // kv_heads
    normed_rows, qkv = grid_rows(normalized_input, w_qkv, length_total)
    seg_row = lax.dynamic_index_in_dim(segments, lax.axis_index("col"), 0, keepdims=False)
    cosine_table, sine_table = rope_tables(doc_positions(seg_row), HEAD_WIDTH)
    query_rows = apply_rotation(
        qkv[:, :q_width].reshape(length_total, q_heads, HEAD_WIDTH), cosine_table, sine_table
    )
    query_rows = query_rows.astype(jnp.bfloat16).reshape(
        length_total, kv_heads, group_size, HEAD_WIDTH
    )
    key_rows = apply_rotation(
        qkv[:, q_width : q_width + kv_width].reshape(length_total, kv_heads, HEAD_WIDTH),
        cosine_table,
        sine_table,
    ).astype(jnp.bfloat16)
    value_rows = (
        qkv[:, q_width + kv_width :]
        .reshape(length_total, kv_heads, HEAD_WIDTH)
        .astype(jnp.bfloat16)
    )
    block = min(512, length_total)
    mixed, totals = attend_forward(query_rows, key_rows, value_rows, seg_row, block)
    mixed = mixed.reshape(length_total, q_width).astype(jnp.bfloat16)
    mixed_rows, attn = grid_cols(mixed, w_out, length_total)
    middle = inputs + RESIDUAL * attn
    inv_second = lax.rsqrt(across_col(jnp.sum(middle * middle, 1)) / width + EPS)
    normed_moe = (middle * inv_second[:, None] * gain_moe).astype(jnp.bfloat16)
    logits = across_col(jnp.dot(normed_moe, w_router, preferred_element_type=jnp.float32))
    gates = jax.nn.softmax(jnp.take_along_axis(logits, routes, 1), axis=-1)
    top = routes.shape[1]
    local = w_gate.shape[0]
    groups = lax.axis_size("expert")
    experts = local * groups
    ffn = w_gate.shape[2]
    targets = slot_targets(routes, CAP, experts)
    send = (
        jnp.zeros((experts * CAP, part), jnp.bfloat16)
        .at[targets]
        .set(jnp.repeat(normed_moe, top, 0))
    )
    received = to_experts(send.reshape(groups, local, CAP, part))
    received_rows = received.reshape(-1, part)
    share = received_rows.shape[0] // lax.axis_size("col")
    w_pair = jnp.concatenate([w_gate, w_up], 2)

    def pair_term(start, count):
        piece = received_rows.reshape(-1, local, CAP, part)
        return jnp.einsum(
            "nlcd,ldf->nlcf", piece, w_pair, preferred_element_type=jnp.float32
        ).reshape(count, 2 * ffn)

    pair = share_sum(pair_term, share)
    gate_val = pair[:, :ffn]
    up_val = pair[:, ffn:]
    sigma = jax.nn.sigmoid(gate_val)
    hidden_share = (gate_val * sigma * up_val).astype(jnp.bfloat16)
    hidden = share_gather(hidden_share).reshape(groups, local, CAP, ffn)
    expert_out = jnp.einsum(
        "nlcf,lfd->nlcd", hidden, w_down, preferred_element_type=jnp.float32
    ).astype(jnp.bfloat16)
    returned = (
        from_experts(expert_out)
        .reshape(experts * CAP, part)[targets]
        .reshape(length_total, top, part)
    )
    moe = jnp.sum(gates[:, :, None] * returned, 1)
    output = middle + RESIDUAL * moe
    grad_final = cotangent.astype(jnp.float32)
    grad_moe = RESIDUAL * grad_final
    grad_gates = across_col(jnp.sum(grad_moe[:, None, :] * returned, 2))
    grad_sel = gates * (grad_gates - jnp.sum(gates * grad_gates, 1, keepdims=True))
    chosen = routes[:, :, None] == jnp.arange(experts, dtype=jnp.int32)[None, None, :]
    grad_logits = jnp.sum(jnp.where(chosen, grad_sel[:, :, None], 0.0), 1)
    grad_normed_moe = jnp.dot(grad_logits, w_router.astype(jnp.float32).T, precision=HIGHEST)
    grad_router = jnp.dot(normed_moe.astype(jnp.float32).T, grad_logits, precision=HIGHEST)
    slot_grads = (
        (gates[:, :, None] * grad_moe[:, None, :])
        .astype(jnp.bfloat16)
        .reshape(length_total * top, part)
    )
    send_grads = jnp.zeros((experts * CAP, part), jnp.bfloat16).at[targets].set(slot_grads)
    got_grads = to_experts(send_grads.reshape(groups, local, CAP, part))
    grad_down = jnp.einsum("nlcf,nlcd->lfd", hidden, got_grads, preferred_element_type=jnp.float32)
    got_rows = got_grads.reshape(-1, part)

    def hidden_term(start, count):
        piece = got_rows.reshape(-1, local, CAP, part)
        return jnp.einsum(
            "nlcd,lfd->nlcf", piece, w_down, preferred_element_type=jnp.float32
        ).reshape(count, ffn)

    grad_hidden = share_sum(hidden_term, share)
    grad_gate_val = grad_hidden * up_val * sigma * (1.0 + gate_val * (1.0 - sigma))
    grad_up_val = grad_hidden * gate_val * sigma
    slopes = jnp.concatenate([grad_gate_val, grad_up_val], 1).astype(jnp.bfloat16)
    slopes = share_gather(slopes).reshape(groups, local, CAP, 2 * ffn)
    grad_pair = jnp.einsum("nlcd,nlcf->ldf", received, slopes, preferred_element_type=jnp.float32)
    back_rows = jnp.einsum(
        "nlcf,ldf->nlcd", slopes, w_pair, preferred_element_type=jnp.float32
    ).astype(jnp.bfloat16)
    back = (
        from_experts(back_rows)
        .reshape(experts * CAP, part)[targets]
        .reshape(length_total, top, part)
    )
    grad_normed_moe = grad_normed_moe + jnp.sum(back.astype(jnp.float32), 1)
    grad_gate = grad_pair[:, :, :ffn]
    grad_up = grad_pair[:, :, ffn:]
    scaled_moe = grad_normed_moe * gain_moe
    grad_gain_moe = jnp.sum(grad_normed_moe * middle * inv_second[:, None], 0)
    inner_moe = across_col(jnp.sum(middle * scaled_moe, 1))
    grad_middle = (
        grad_final
        + inv_second[:, None] * scaled_moe
        - middle * (inv_second**3 * inner_moe / width)[:, None]
    )
    grad_attn = (RESIDUAL * grad_middle).astype(jnp.bfloat16)
    grad_rows, grad_mixed = grid_rows(grad_attn, w_out.T, length_total)
    grad_out_w = jnp.einsum("rh,rd->hd", mixed_rows, grad_rows, preferred_element_type=jnp.float32)
    grad_mixed = grad_mixed.astype(jnp.bfloat16).reshape(
        length_total, kv_heads, group_size, HEAD_WIDTH
    )
    grad_queries, grad_keys, grad_values = attend_backward(
        query_rows, key_rows, value_rows, seg_row, block, totals, grad_mixed
    )
    grad_queries = unrotate(
        grad_queries.reshape(length_total, q_heads, HEAD_WIDTH), cosine_table, sine_table
    ).reshape(length_total, q_width)
    grad_keys = unrotate(grad_keys, cosine_table, sine_table).reshape(length_total, kv_width)
    grad_qkv = jnp.concatenate(
        [grad_queries, grad_keys, grad_values.reshape(length_total, kv_width)], 1
    ).astype(jnp.bfloat16)
    grad_qkv_rows, grad_normed = grid_cols(grad_qkv, w_qkv.T, length_total)
    grad_qkv_w = jnp.einsum(
        "rd,rf->df", normed_rows, grad_qkv_rows, preferred_element_type=jnp.float32
    )
    scaled_attn = grad_normed * gain_attn
    grad_gain_attn = jnp.sum(grad_normed * inputs * inv_first[:, None], 0)
    inner_attn = across_col(jnp.sum(inputs * scaled_attn, 1))
    grad_tokens = (
        grad_middle
        + inv_first[:, None] * scaled_attn
        - inputs * (inv_first**3 * inner_attn / width)[:, None]
    )
    grad_gain_attn, grad_gain_moe, grad_router = lax.psum(
        (grad_gain_attn, grad_gain_moe, grad_router), ("dp", "expert")
    )
    grad_qkv_w, grad_out_w = lax.psum((grad_qkv_w, grad_out_w), "dp")
    grad_gate, grad_up, grad_down = spread_expert_grads(grad_gate, grad_up, grad_down)
    return (
        output,
        grad_tokens,
        grad_gain_attn,
        grad_qkv_w[:, :q_width],
        grad_qkv_w[:, q_width : q_width + kv_width],
        grad_qkv_w[:, q_width + kv_width :],
        grad_out_w,
        grad_gain_moe,
        grad_router,
        grad_gate,
        grad_up,
        grad_down,
    )


def solution(mesh):
    in_specs = (
        P(("dp", "expert"), "col"),
        P("col"),
        P("col", "expert"),
        P("col", "expert"),
        P("col", "expert"),
        P("expert", "col"),
        P("col"),
        P("col", None),
        P("expert", "col", None),
        P("expert", "col", None),
        P("expert", None, "col"),
        P("dp", None),
        P(("dp", "expert"), None),
        P(("dp", "expert"), "col"),
    )
    out_specs = (
        P(("dp", "expert"), "col"),
        P(("dp", "expert"), "col"),
        P("col"),
        P("col", "expert"),
        P("col", "expert"),
        P("col", "expert"),
        P("expert", "col"),
        P("col"),
        P("col", None),
        P("expert", "col", "dp"),
        P("expert", "col", "dp"),
        P("expert", "dp", "col"),
    )
    return jax.shard_map(
        on_device, mesh=mesh, in_specs=in_specs, out_specs=out_specs, check_vma=False
    )
```

profile of v0, /device:TPU:0, one launch (start us, length us, event | category | flops | bytes accessed | tf_op | source)
XLA Modules:
  0.0 3451.5 jit_solution(4386420728271806502)
XLA Ops:
  37.2 65.0 %reduce-scatter.10.cloned.1.call-done = f32[512,1280]{1,0:T(8,128)} async-done(((f32[1024,1280]{1,0:T(8,128)}), f32[512,1280]{1,0:T(8,128)}) %reduce-scatter.10.cloned.1.call-update) | async-done | bytes 2621456 | tf_op jit(solution)/shard_map/reduce_scatter | solution.py:116
  123.5 27.1 all-gather.9.cloned.1.call-done
  213.1 47.7 %gather_fusion.2 = f32[4096]{0:T(1024)} fusion(f32[512,40]{0,1:T(8,128)} %all-reduce.6.cloned.1.call-done, s32[4096]{0:T(1024)S(1)} %reshape.323), kind=kCustom, calls=%fused_computation.2 | custom fusion | bytes 65536 | tf_op jit(solution)/shard_map/jit(take_along_axis)/gather | solution.py:229
  268.3 27.1 scatter_custom_fusion.1
  351.7 25.1 scatter_custom_fusion
  400.6 30.7 fusion.7
  454.5 75.1 %reduce-scatter.16.cloned.1.call-done = f32[3840,512]{1,0:T(8,128)} async-done(((f32[7680,512]{1,0:T(8,128)}), f32[3840,512]{1,0:T(8,128)}) %reduce-scatter.16.cloned.1.call-update) | async-done | bytes 7864336 | tf_op jit(solution)/shard_map/reduce_scatter | solution.py:155
  529.6 349.2 %reduce-scatter.14.cloned.1.call-done = f32[3840,1024]{1,0:T(8,128)} async-done(((f32[7680,1024]{1,0:T(8,128)}), f32[3840,1024]{1,0:T(8,128)}) %reduce-scatter.14.cloned.1.call-update) | async-done | bytes 15728656 | tf_op jit(solution)/shard_map/reduce_scatter | solution.py:155
  902.1 90.0 %all-gather.11.cloned.1.call-done = bf16[7680,512]{1,0:T(8,128)(2,1)} async-done(((bf16[3840,512]{1,0:T(8,128)(2,1)}), bf16[7680,512]{1,0:T(8,128)(2,1)}) %all-gather.11.cloned.1.call-update) | async-done | bytes 7864336 | tf_op jit(solution)/shard_map/all_gather | solution.py:164
  1031.1 25.2 gather_fusion
  1075.0 106.1 %all-gather.13.cloned.1.call-done = bf16[7680,1024]{1,0:T(8,128)(2,1)} async-done(((bf16[3840,1024]{1,0:T(8,128)(2,1)}), bf16[7680,1024]{1,0:T(8,128)(2,1)}) %all-gather.13.cloned.1.call-update) | async-done | bytes 15728656 | tf_op jit(solution)/shard_map/all_gather | solution.py:164
  1226.1 25.0 gather_fusion.1
  1285.3 44.4 %reduce-scatter.18.cloned.1.call-done = f32[512,768]{1,0:T(8,128)} async-done(((f32[1024,768]{1,0:T(8,128)}), f32[512,768]{1,0:T(8,128)}) %reduce-scatter.18.cloned.1.call-update) | async-done | bytes 1572880 | tf_op jit(solution)/shard_map/reduce_scatter | solution.py:116
  1366.0 34.5 all-gather.17.cloned.1.call-done
  1413.7 35.3 %convolution_bitcast_fusion = f32[20,768,1024]{2,1,0:T(8,128)} fusion(bf16[2,20,192,768]{3,2,1,0:T(8,128)(2,1)} %all_to_all.21, bf16[2,20,192,1024]{3,2,1,0:T(8,128)(2,1)} %bitcast.208), kind=kOutput, calls=%fused_computation.6 | convolution fusion | flops 12079595520 | bytes 90439680 | tf_op jit(solution)/shard_map/nlcd,nlcf->ldf/dot_general | solution.py:297
  1449.0 41.5 %fusion.85 = (f32[20,768,512]{2,1,0:T(8,128)}, f32[20,768,512]{2,1,0:T(8,128)}) fusion(f32[20,768,1024]{2,1,0:T(8,128)} %convolution_bitcast_fusion), kind=kLoop, calls=%fused_computation.158 | loop fusion | bytes 125829120 | tf_op jit(solution)/shard_map/slice | solution.py:308
  1490.5 35.6 %copy.200 = f32[20,768,512]{1,0,2:T(8,128)} copy(f32[20,768,512]{2,1,0:T(8,128)} %get-tuple-element.96) | data formatting | bytes 62914560 | tf_op jit(solution)/shard_map/slice | solution.py:308
  1526.1 35.5 %copy.199 = f32[20,768,512]{1,0,2:T(8,128)} copy(f32[20,768,512]{2,1,0:T(8,128)} %get-tuple-element.97) | data formatting | bytes 62914560 | tf_op jit(solution)/shard_map/slice | solution.py:307
  1585.1 33.8 all-reduce.10.cloned.1.call-done
  1634.2 36.9 %all-reduce = (f32[768]{0:T(1024)}, f32[768]{0:T(1024)}) all-reduce(f32[768]{0:T(1024)} %get-tuple-element.88, f32[768]{0:T(1024)} %get-tuple-element.86), channel_id=1, replica_groups=mesh['dp'=8,'expert'=2,'col'=2] {'dp','expert'}, use_global_device_ids=true, to_apply=%region_34.35 | all-reduce | flops 1536 | bytes 12288 | tf_op jit(solution)/shard_map/psum | solution.py:345
  1685.5 556.1 %reduce-scatter.24.cloned.1.call-done = f32[20,768,64]{1,0,2:T(8,128)} async-done(((f32[20,768,512]{1,0,2:T(8,128)}), f32[20,768,64]{1,0,2:T(8,128)}) %reduce-scatter.24.cloned.1.call-update) | async-done | bytes 3932176 | tf_op jit(solution)/shard_map/reduce_scatter | solution.py:170
  2247.1 603.2 %reduce-scatter.22.cloned.1.call-done = f32[20,768,64]{1,0,2:T(8,128)} async-done(((f32[20,768,512]{1,0,2:T(8,128)}), f32[20,768,64]{1,0,2:T(8,128)}) %reduce-scatter.22.cloned.1.call-update) | async-done | bytes 3932176 | tf_op jit(solution)/shard_map/reduce_scatter | solution.py:169
  2855.8 84.3 %all-reduce.8.cloned.1.call-done = f32[768,40]{0,1:T(8,128)} async-done(((f32[768,40]{0,1:T(8,128)}), f32[768,40]{0,1:T(8,128)}) %all-reduce.8.cloned.1.call-update) | async-done | bytes 122896 | tf_op jit(solution)/shard_map/psum | solution.py:345
  2940.1 501.2 %reduce-scatter.26.cloned.1.call-done = f32[20,64,768]{2,1,0:T(8,128)} async-done(((f32[20,512,768]{2,1,0:T(8,128)}), f32[20,64,768]{2,1,0:T(8,128)}) %reduce-scatter.26.cloned.1.call-update) | async-done | bytes 3932176 | tf_op jit(solution)/shard_map/reduce_scatter | solution.py:171
  (284 shorter events, 500.4 us)
Async XLA Ops:
  7.2 143.4 %copy-start = (bf16[768,768]{1,0:T(8,128)(2,1)S(1)}, bf16[768,768]{1,0:T(8,128)(2,1)}, u32[]{:S(2)}) copy-start(bf16[768,768]{1,0:T(8,128)(2,1)} %param.19) | copy-start | bytes 3538948
  7.2 22.0 all-gather.7.cloned.1.call-start
  17.5 84.7 %reduce-scatter.10.cloned.1.call-start = ((), (), s32[]{:S(2)}) async-start(), calls=%async_computation.14 | async-start | bytes 7864320 | tf_op jit(solution)/shard_map/reduce_scatter | solution.py:116
  35.2 115.4 %all-gather.9.cloned.1.call-start = ((), (), s32[]{:S(2)}) async-start(), calls=%async_computation.15 | async-start | bytes 2359296 | tf_op jit(solution)/shard_map/all_gather | solution.py:126
  123.2 59.3 %reduce-scatter.12.cloned.1.call-start = ((), (), s32[]{:S(2)}) async-start(), calls=%async_computation.16 | async-start | bytes 4718592 | tf_op jit(solution)/shard_map/reduce_scatter | solution.py:133
  155.1 58.0 %all-reduce.6.cloned.1.call-start = ((), (), s32[]{:S(2)}) async-start(), calls=%async_computation.17 | async-start | bytes 163840 | tf_op jit(solution)/shard_map/psum | solution.py:143
  190.1 161.2 %copy-start.10 = (bf16[512,768]{1,0:T(8,128)(2,1)}, bf16[512,768]{1,0:T(8,128)(2,1)S(1)}, u32[]{:S(2)}) copy-start(bf16[512,768]{1,0:T(8,128)(2,1)S(1)} %multiply_convert_fusion.4) | copy-start | bytes 2359300
  192.1 337.5 %reduce-scatter.16.cloned.1.call-start = ((), (), s32[]{:S(2)}) async-start(), calls=%async_computation.20 | async-start | bytes 23592960 | tf_op jit(solution)/shard_map/reduce_scatter | solution.py:155
  351.1 527.8 %reduce-scatter.14.cloned.1.call-start = ((), (), s32[]{:S(2)}) async-start(), calls=%async_computation.18 | async-start | bytes 47185920 | tf_op jit(solution)/shard_map/reduce_scatter | solution.py:155
  454.3 537.8 %all-gather.11.cloned.1.call-start = ((), (), s32[]{:S(2)}) async-start(), calls=%async_computation.19 | async-start | bytes 11796480 | tf_op jit(solution)/shard_map/all_gather | solution.py:164
  893.8 287.3 %all-gather.13.cloned.1.call-start = ((), (), s32[]{:S(2)}) async-start(), calls=%async_computation.21 | async-start | bytes 23592960 | tf_op jit(solution)/shard_map/all_gather | solution.py:164
  902.0 378.5 %all-gather.15.cloned.1.call-start = ((), (), s32[]{:S(2)}) async-start(), calls=%async_computation.22 | async-start | bytes 2359296 | tf_op jit(solution)/shard_map/all_gather | solution.py:109
  1270.6 59.1 %reduce-scatter.18.cloned.1.call-start = ((), (), s32[]{:S(2)}) async-start(), calls=%async_computation.23 | async-start | bytes 4718592 | tf_op jit(solution)/shard_map/reduce_scatter | solution.py:116
  1285.1 115.4 %all-gather.17.cloned.1.call-start = ((), (), s32[]{:S(2)}) async-start(), calls=%async_computation.24 | async-start | bytes 3932160 | tf_op jit(solution)/shard_map/all_gather | solution.py:126
  1361.3 257.6 %all-reduce.10.cloned.1.call-start = ((), (), s32[]{:S(2)}) async-start(), calls=%async_computation.30 | async-start | bytes 12582912 | tf_op jit(solution)/shard_map/psum | solution.py:348
  1406.4 225.2 %reduce-scatter.20.cloned.1.call-start = ((), (), s32[]{:S(2)}) async-start(), calls=%async_computation.25 | async-start | bytes 4718592 | tf_op jit(solution)/shard_map/reduce_scatter | solution.py:133
  1413.7 827.9 %reduce-scatter.24.cloned.1.call-start = ((), (), s32[]{:S(2)}) async-start(), calls=%async_computation.28 | async-start | bytes 42467328 | tf_op jit(solution)/shard_map/reduce_scatter | solution.py:170
  1526.1 1324.2 %reduce-scatter.22.cloned.1.call-start = ((), (), s32[]{:S(2)}) async-start(), calls=%async_computation.27 | async-start | bytes 42467328 | tf_op jit(solution)/shard_map/reduce_scatter | solution.py:169
  1561.7 1378.5 %all-reduce.8.cloned.1.call-start = ((), (), s32[]{:S(2)}) async-start(), calls=%async_computation.26 | async-start | bytes 245760 | tf_op jit(solution)/shard_map/psum | solution.py:345
  1563.9 1877.4 %reduce-scatter.26.cloned.1.call-start = ((), (), s32[]{:S(2)}) async-start(), calls=%async_computation.29 | async-start | bytes 35389440 | tf_op jit(solution)/shard_map/reduce_scatter | solution.py:171
  1585.1 95.2 %copy-start.5 = (f32[512,768]{1,0:T(8,128)S(1)}, f32[512,768]{1,0:T(8,128)}, u32[]{:S(2)}) copy-start(f32[512,768]{1,0:T(8,128)} %copy-done.3) | copy-start | bytes 4718596
  1585.1 95.2 %copy-start.46 = (f32[768]{0:T(1024)S(1)}, f32[768]{0:T(1024)}, u32[]{:S(2)}) copy-start(f32[768]{0:T(1024)} %param.20) | copy-start | bytes 9220
  1585.1 95.1 %copy-start.50 = (f32[512]{0:T(512)S(1)}, f32[512]{0:T(512)}, u32[]{:S(2)}) copy-start(f32[512]{0:T(512)} %copy-done.48) | copy-start | bytes 6148
  2247.1 1194.2 %copy-start.18 = (f32[768,768]{1,0:T(8,128)S(1)}, f32[768,768]{1,0:T(8,128)}, u32[]{:S(2)}) copy-start(f32[768,768]{1,0:T(8,128)} %get-tuple-element.126) | copy-start | bytes 7077892
  (58 other events, 860.4 us)
Sparse Core Ops, SparseCore 0:
  17.6 11.6 all-gather.6
  35.3 66.8 reduce-scatter.9
  123.3 27.2 all-gather.8
  155.3 10.7 reduce-scatter.11
  192.2 20.8 all-reduce.5
  351.2 178.3 reduce-scatter.15
  531.9 346.8 reduce-scatter.13
  894.0 98.0 all-gather.10
  993.7 187.3 all-gather.12
  1270.7 9.8 all-gather.14
  1285.2 44.4 reduce-scatter.17
  1361.4 39.0 all-gather.16
  1406.6 212.3 all-reduce.9
  1621.6 9.9 reduce-scatter.19
  1635.9 605.6 reduce-scatter.23
  2245.3 604.9 reduce-scatter.21
  2854.5 85.5 all-reduce.7
  2944.9 496.3 reduce-scatter.25
where the time goes:
time: 3470 us; the launch traced here: 3450 us
  waiting for transfers between devices  2620 us (76%)
  local copies, waits for them, and re-layouts  335 us (10%)
  matrix products  209 us (6%)
  blocking collectives  144 us (4%)
  other arithmetic  129 us (4%)
    reduce_scatter x1, waiting for transfers between devices, spread_expert_grads(): lax.psum_scatter(grad_gate, 'dp', scatter_dimension=2, tiled=True)  603 us
    reduce_scatter x1, waiting for transfers between devices, spread_expert_grads(): lax.psum_scatter(grad_up, 'dp', scatter_dimension=2, tiled=True)  556 us
    reduce_scatter x1, waiting for transfers between devices, spread_expert_grads(): lax.psum_scatter(grad_down, 'dp', scatter_dimension=1, tiled=True)  501 us
    reduce_scatter x2, waiting for transfers between devices, share_sum(): lax.psum_scatter(product_term(jnp.int32(0), rows * lax.axis_size('col')),...  424 us
    all_gather x2, waiting for transfers between devices, share_gather(): return lax.all_gather(value_rows, 'col', axis=0, tiled=True)  196 us
    reduce_scatter x2, waiting for transfers between devices, grid_rows(): lax.psum_scatter(product_term(jnp.int32(0), rows * lax.axis_size('col')),...  109 us
    psum x1, waiting for transfers between devices, on_device(): lax.psum((grad_gain_attn, grad_gain_moe, grad_router), ('dp', 'expert'))  84.3 us
    slice x2, local copies, waits for them, and re-layouts, on_device(): grad_up = grad_pair[:, :, ffn:]  77 us
  transfers between devices with their start and end apart: 18, of which 17 were waited for; matrix products, arithmetic and copies ran while one was open for 11% of the time, Pallas kernels for 0%

commit v1 on v0

v1 whole, which is shorter than its diff:
```python
import math

import jax
import jax.numpy as jnp
from jax import lax
from jax.experimental import pallas as pl
from jax.experimental.pallas import tpu as pltpu
from jax.sharding import PartitionSpec as P

HEAD_WIDTH = 64
ZPARTS = 4
LANES = 128
TILE = 512

EPS = 1e-06
RESIDUAL = 0.22
SCORE_SCALE = 0.015625
THETA = 10000.0
NEG = -1000000000.0


def doc_positions(seg_row):
    length_total = seg_row.shape[0]
    index = jnp.arange(length_total, dtype=jnp.int32)
    before = jnp.concatenate([jnp.full((1,), -1, jnp.int32), seg_row[:-1]])
    starts = jnp.where(seg_row != before, index, 0)
    return index - lax.cummax(starts, axis=0)


def rope_tables(positions, head_size):
    half = head_size // 2
    freq = jnp.exp(jnp.arange(half, dtype=jnp.float32) * (-2.0 * math.log(THETA) / head_size))
    angle = positions.astype(jnp.float32)[:, None] * freq[None, :]
    return (jnp.cos(angle)[:, None, :], jnp.sin(angle)[:, None, :])


def apply_rotation(heads, cosine_table, sine_table):
    half = heads.shape[-1] // 2
    first = heads[..., :half]
    second = heads[..., half:]
    return jnp.concatenate(
        [first * cosine_table - second * sine_table, second * cosine_table + first * sine_table], -1
    )


def unrotate(grads, cosine_table, sine_table):
    half = grads.shape[-1] // 2
    first = grads[..., :half]
    second = grads[..., half:]
    return jnp.concatenate(
        [first * cosine_table + second * sine_table, second * cosine_table - first * sine_table], -1
    )


def allowed_mask(seg_rows):
    index = jnp.arange(seg_rows.shape[1])
    same = seg_rows[:, :, None] == seg_rows[:, None, :]
    return same & (index[None, None, :] <= index[None, :, None])


def block_scores(query_rows, key_rows, allowed):
    scores = (
        jnp.einsum("bqkgd,bskd->bkgqs", query_rows, key_rows, preferred_element_type=jnp.float32)
        * SCORE_SCALE
    )
    return jnp.where(allowed[:, None, None], scores, NEG)


def attend_forward(query_rows, key_rows, value_rows, allowed):
    scores = block_scores(query_rows, key_rows, allowed)
    peak = jnp.max(scores, -1, keepdims=True)
    expo = jnp.exp(scores - peak)
    total = jnp.sum(expo, -1, keepdims=True)
    probs = (expo / total).astype(jnp.bfloat16)
    outputs = jnp.einsum("bkgqs,bskd->bqkgd", probs, value_rows, preferred_element_type=jnp.float32)
    totals = peak + jnp.log(total)
    return (outputs, totals)


def attend_backward(query_rows, key_rows, value_rows, allowed, totals, grad_mixed):
    scores = block_scores(query_rows, key_rows, allowed)
    probs = jnp.exp(scores - totals)
    slope = jnp.einsum(
        "bqkgd,bskd->bkgqs", grad_mixed, value_rows, preferred_element_type=jnp.float32
    )
    delta = jnp.sum(probs * slope, -1, keepdims=True)
    dscore = (probs * (slope - delta)).astype(jnp.bfloat16)
    grad_queries = (
        jnp.einsum("bkgqs,bskd->bqkgd", dscore, key_rows, preferred_element_type=jnp.float32)
        * SCORE_SCALE
    )
    grad_keys = (
        jnp.einsum("bkgqs,bqkgd->bskd", dscore, query_rows, preferred_element_type=jnp.float32)
        * SCORE_SCALE
    )
    grad_values = jnp.einsum(
        "bkgqs,bqkgd->bskd",
        probs.astype(jnp.bfloat16),
        grad_mixed,
        preferred_element_type=jnp.float32,
    )
    return (grad_queries, grad_keys, grad_values)


def flip(value, axis, mask=1):
    size = lax.axis_size(axis)
    return lax.ppermute(value, axis, [(i, i ^ mask) for i in range(size)])


def across(value):
    return flip(value, "col")


def sibling(value):
    return flip(value, "expert")


def dot_nn(a, b):
    return jnp.dot(a, b, preferred_element_type=jnp.float32)


def dot_nt(a, b):
    return lax.dot_general(a, b, (((1,), (1,)), ((), ())), preferred_element_type=jnp.float32)


def dot_tn(a, b):
    return lax.dot_general(a, b, (((0,), (0,)), ((), ())), preferred_element_type=jnp.float32)


def moe_kernel(
    base_ref,
    routes_ref,
    h_own,
    h_far,
    c_own,
    c_far,
    pair_own,
    pair_far,
    down_own,
    down_far,
    router_own,
    router_far,
    moe_own,
    moe_far,
    back_own,
    back_far,
    hidden_ref,
    slopes_ref,
    dlog_ref,
):
    experts = down_own.shape[0] // LANES
    rows = h_own.shape[0]
    lane = lax.broadcasted_iota(jnp.int32, (rows, LANES), 1)
    chosen = lane == routes_ref[:, 0:1]
    for k in range(1, routes_ref.shape[1]):
        chosen = chosen | (lane == routes_ref[:, k : k + 1])
    logits = dot_nn(h_own[...], router_own[...]) + dot_nn(h_far[...], router_far[...])
    peak = jnp.max(jnp.where(chosen, logits, -jnp.inf), axis=1, keepdims=True)
    expo = jnp.where(chosen, jnp.exp(logits - peak), 0.0)
    gates = expo / jnp.sum(expo, axis=1, keepdims=True)
    grad_gates = jnp.zeros((rows, LANES), jnp.float32)
    for e in range(experts):
        here = lane == base_ref[0] + e
        gate = jnp.sum(jnp.where(here, gates, 0.0), axis=1, keepdims=True)
        pair_rows = pl.ds(2 * LANES * e, 2 * LANES)
        down_rows = pl.ds(LANES * e, LANES)
        pair = dot_nt(h_own[...], pair_own[pair_rows, :]) + dot_nt(
            h_far[...], pair_far[pair_rows, :]
        )
        slope = dot_nt(c_own[...], down_own[down_rows, :]) + dot_nt(
            c_far[...], down_far[down_rows, :]
        )
        slope = RESIDUAL * slope
        gate_val = pair[:, :LANES]
        up_val = pair[:, LANES:]
        sigma = jax.nn.sigmoid(gate_val)
        silu = gate_val * sigma
        hidden = silu * up_val
        dgate = jnp.sum(hidden * slope, axis=1, keepdims=True)
        grad_gates = jnp.where(here, dgate, grad_gates)
        dz = gate * slope
        hidden_ref[:, LANES * e : LANES * (e + 1)] = (gate * hidden).astype(jnp.bfloat16)
        slopes_ref[:, 2 * LANES * e : 2 * LANES * e + LANES] = (
            dz * up_val * (sigma + silu * (1.0 - sigma))
        ).astype(jnp.bfloat16)
        slopes_ref[:, 2 * LANES * e + LANES : 2 * LANES * (e + 1)] = (dz * silu).astype(
            jnp.bfloat16
        )
    dlog = gates * (grad_gates - jnp.sum(gates * grad_gates, axis=1, keepdims=True))
    dlog_high = dlog.astype(jnp.bfloat16)
    dlog_low = (dlog - dlog_high.astype(jnp.float32)).astype(jnp.bfloat16)
    dlog_ref[:, :LANES] = dlog_high
    dlog_ref[:, LANES:] = dlog_low
    moe_own[...] = dot_nn(hidden_ref[...], down_own[...]).astype(jnp.bfloat16)
    moe_far[...] = dot_nn(hidden_ref[...], down_far[...]).astype(jnp.bfloat16)
    for out, pair, router in ((back_own, pair_own, router_own), (back_far, pair_far, router_far)):
        total = dot_nt(dlog_high, router[...]) + dot_nt(dlog_low, router[...])
        out[...] = (total + dot_nn(slopes_ref[...], pair[...])).astype(jnp.bfloat16)


def moe_chunk(base, routes, h_own, h_far, c_own, c_far, weights):
    rows, part = h_own.shape
    experts = weights[2].shape[0] // LANES
    by_row = lambda width: pl.BlockSpec((TILE, width), lambda i, *_: (i, 0))
    whole = lambda a: pl.BlockSpec(
        a.shape, lambda i, *_: (0,) * a.ndim, pipeline_mode=pl.Buffered(1)
    )
    outs = [part, part, part, part, experts * LANES, 2 * experts * LANES, 2 * LANES]
    flops = 2 * rows * 2 * part * experts * LANES * 6
    return pl.pallas_call(
        moe_kernel,
        out_shape=[jax.ShapeDtypeStruct((rows, w), jnp.bfloat16) for w in outs],
        grid_spec=pltpu.PrefetchScalarGridSpec(
            num_scalar_prefetch=1,
            grid=(rows // TILE,),
            in_specs=[by_row(routes.shape[1])]
            + [by_row(part)] * 4
            + [whole(w) for w in weights],
            out_specs=[by_row(w) for w in outs],
        ),
        compiler_params=pltpu.CompilerParams(vmem_limit_bytes=56 * 1024 * 1024),
        cost_estimate=pl.CostEstimate(
            flops=flops, bytes_accessed=40_000_000, transcendentals=rows * experts * LANES
        ),
        name="moe_rows",
    )(base, routes, h_own, h_far, c_own, c_far, *weights)


def weight_kernel(side_ref, *refs):
    chunks = (len(refs) - 4) // 6
    hidden = refs[:chunks]
    slopes = refs[chunks : 2 * chunks]
    h_own, h_far, c_own, c_far = (
        refs[(2 + i) * chunks : (3 + i) * chunks] for i in range(4)
    )
    outs = refs[6 * chunks :]
    half = LANES // 2
    first = side_ref[0] == 0
    for keep, send, rows_h, rows_c in (
        (outs[0], outs[2], h_own, c_own),
        (outs[1], outs[3], h_far, c_far),
    ):
        pair = sum(dot_tn(s[...], h[...]) for s, h in zip(slopes, rows_h))
        down = sum(dot_tn(s[...], c[...]) for s, c in zip(hidden, rows_c)) * RESIDUAL
        for i, block in enumerate((pair[:LANES], pair[LANES:], down)):
            low, high = block[:half], block[half:]
            keep[0, half * i : half * (i + 1), :] = jnp.where(first, low, high)
            send[0, half * i : half * (i + 1), :] = jnp.where(first, high, low).astype(
                jnp.bfloat16
            )


def weight_grads(side, start, count, hidden, slopes, h_own, h_far, c_own, c_far):
    rows, part = h_own[0].shape
    whole = pl.BlockSpec((rows, part), lambda e, *_: (0, 0), pipeline_mode=pl.Buffered(1))
    out = pl.BlockSpec((1, 3 * LANES // 2, part), lambda e, *_: (e, 0, 0))
    n = len(hidden)
    shape = (count, 3 * LANES // 2, part)
    return pl.pallas_call(
        weight_kernel,
        out_shape=[jax.ShapeDtypeStruct(shape, jnp.float32)] * 2
        + [jax.ShapeDtypeStruct(shape, jnp.bfloat16)] * 2,
        grid_spec=pltpu.PrefetchScalarGridSpec(
            num_scalar_prefetch=1,
            grid=(count,),
            in_specs=[pl.BlockSpec((rows, LANES), lambda e, *_: (0, e + start))] * n
            + [pl.BlockSpec((rows, 2 * LANES), lambda e, *_: (0, e + start))] * n
            + [whole] * (4 * n),
            out_specs=[out] * 4,
        ),
        compiler_params=pltpu.CompilerParams(vmem_limit_bytes=60 * 1024 * 1024),
        cost_estimate=pl.CostEstimate(
            flops=2 * n * rows * 2 * part * count * LANES * 3,
            bytes_accessed=40_000_000,
            transcendentals=0,
        ),
        name="expert_weight_grads",
    )(side, *hidden, *slopes, *h_own, *h_far, *c_own, *c_far)


def gather_tokens(value, step, relay):
    far = across(value)
    chunks = [(value, far), (flip(value, "dp", step), flip(far, "dp", step))]
    for k in range(2, ZPARTS):
        got = flip(value, "dp", k * step)
        chunks.append((got, across(got) if relay else flip(far, "dp", k * step)))
    return [
        tuple(jnp.concatenate([piece, sibling(piece)], 0) for piece in pair) for pair in chunks
    ]


def add_wide(*parts):
    return sum(p.astype(jnp.float32) for p in parts)


def scatter_tokens(chunks, step):
    own, far, later = 0.0, 0.0, []
    for k, (p_own, p_far) in enumerate(chunks):
        rows = p_own.shape[0] // 2
        s_own = add_wide(p_own[:rows], sibling(p_own[rows:]))
        s_far = add_wide(p_far[:rows], sibling(p_far[rows:]))
        if k == 0:
            own, far = s_own, s_far
        elif k == 1:
            own = own + flip(s_own.astype(jnp.bfloat16), "dp", step).astype(jnp.float32)
            far = far + flip(s_far.astype(jnp.bfloat16), "dp", step).astype(jnp.float32)
        else:
            piece = s_own + across(s_far.astype(jnp.bfloat16)).astype(jnp.float32)
            later.append(flip(piece.astype(jnp.bfloat16), "dp", k * step))
    return add_wide(own, across(far.astype(jnp.bfloat16)), *later)


def halve(value, index, mask, axis):
    low, high = jnp.split(value, 2, axis)
    upper = (index & mask) != 0
    send = jnp.where(upper, low, high).astype(jnp.bfloat16)
    return jnp.where(upper, high, low) + flip(send, "dp", mask).astype(jnp.float32)


def sum_over_dp(value, index):
    size = lax.axis_size("dp")
    masks = []
    while 1 << len(masks) < size:
        masks.append(1 << len(masks))
    for mask in masks:
        value = halve(value, index, mask, 0)
    value = value.astype(jnp.bfloat16)
    for mask in masks[::-1]:
        got = flip(value, "dp", mask)
        upper = (index & mask) != 0
        value = jnp.concatenate([jnp.where(upper, got, value), jnp.where(upper, value, got)], 0)
    return value.astype(jnp.float32)


def sum_small(value):
    value = value + sibling(value)
    mask = 1
    while mask < lax.axis_size("dp"):
        value = value + flip(value, "dp", mask)
        mask *= 2
    return value


def on_device(
    tokens,
    gain_attn,
    w_query,
    key_matrix,
    value_matrix,
    w_out,
    gain_moe,
    w_router,
    w_gate,
    w_up,
    w_down,
    segments,
    routes,
    cotangent,
):
    col = lax.axis_index("col")
    core = lax.axis_index("expert")
    group = lax.axis_index("dp")
    step = lax.axis_size("dp") // ZPARTS
    zed, member = group // step, group % step

    local, part, ffn = w_gate.shape
    width = part * lax.axis_size("col")
    mine = local // 2
    units = ffn // ZPARTS
    experts = local * lax.axis_size("expert")

    def cut_pair(which):
        def cut(w):
            piece = lax.dynamic_slice(w, (which * mine, 0, zed * units), (mine, part, units))
            return jnp.swapaxes(piece, 1, 2)

        return jnp.concatenate([cut(w_gate), cut(w_up)], 1)

    def cut_down(which):
        return lax.dynamic_slice(w_down, (which * mine, zed * units, 0), (mine, units, part))

    side = member & 1
    split = mine // 2

    def fetch(cut):
        whole = cut(1 - col)
        half = lax.dynamic_slice_in_dim(whole, side * split, split, 0)
        got = across(half)
        other = flip(got, "dp", 1)
        first = jnp.where(side == 0, got, other)
        second = jnp.where(side == 0, other, got)
        return jnp.concatenate([first, second], 0).reshape(-1, part)

    pair_far = fetch(cut_pair)
    down_far = fetch(cut_down)
    pair_own = cut_pair(col).reshape(-1, part)
    down_own = cut_down(col).reshape(-1, part)
    router_own = jnp.pad(w_router, ((0, 0), (0, LANES - experts)))
    router_far = across(router_own)
    weights = [pair_own, pair_far, down_own, down_far, router_own, router_far]

    route_rows = routes.T
    route_rows = jnp.concatenate([route_rows, sibling(route_rows)], 1)
    route_chunks = [route_rows] + [flip(route_rows, "dp", k * step) for k in range(1, ZPARTS)]
    route_chunks = [r.T for r in route_chunks]
    c_chunks = gather_tokens(cotangent, step, False)

    def both(own):
        return jnp.concatenate([own, sibling(own)], 0)

    length_total = tokens.shape[0]
    rows_own, rows_far = both(tokens), both(across(tokens))
    gain_far = across(gain_attn)
    wide_own, wide_far = rows_own.astype(jnp.float32), rows_far.astype(jnp.float32)
    square = jnp.sum(wide_own * wide_own, 1) + jnp.sum(wide_far * wide_far, 1)
    inv_rows = lax.rsqrt(square / width + EPS)
    normed_own = (wide_own * inv_rows[:, None] * gain_attn).astype(jnp.bfloat16)
    normed_far = (wide_far * inv_rows[:, None] * gain_far).astype(jnp.bfloat16)
    inputs, inv_first = wide_own[:length_total], inv_rows[:length_total]

    q_width = w_query.shape[1] // 2
    kv_width = key_matrix.shape[1] // 2
    qkv_width = q_width + 2 * kv_width
    kv_heads = kv_width // HEAD_WIDTH
    group_size = q_width // kv_width

    def qkv_columns(which):
        def cut(w):
            return lax.dynamic_slice_in_dim(w, which * (w.shape[1] // 2), w.shape[1] // 2, 1)

        return jnp.concatenate([cut(w_query), cut(key_matrix), cut(value_matrix)], 1)

    def out_rows(which):
        return lax.dynamic_slice_in_dim(w_out, which * q_width, q_width, 0)

    qkv_here, qkv_there = qkv_columns(col), qkv_columns(1 - col)
    qkv_far = across(qkv_there)
    out_here, out_there = out_rows(col), out_rows(1 - col)
    out_far = across(out_there)

    qkv = dot_nn(normed_own, qkv_here) + dot_nn(normed_far, qkv_far)
    seg_rows = jnp.where(core == 0, segments, segments[::-1])
    allowed = allowed_mask(seg_rows)
    positions = jax.vmap(doc_positions)(seg_rows).reshape(-1)
    cosine_table, sine_table = rope_tables(positions, HEAD_WIDTH)

    def heads(value, *count):
        return value.reshape(2, length_total, *count, HEAD_WIDTH)

    query_rows = apply_rotation(
        qkv[:, :q_width].reshape(2 * length_total, -1, HEAD_WIDTH), cosine_table, sine_table
    )
    query_rows = heads(query_rows.astype(jnp.bfloat16), kv_heads, group_size)
    key_rows = apply_rotation(
        qkv[:, q_width : q_width + kv_width].reshape(2 * length_total, -1, HEAD_WIDTH),
        cosine_table,
        sine_table,
    )
    key_rows = heads(key_rows.astype(jnp.bfloat16), kv_heads)
    value_rows = heads(qkv[:, q_width + kv_width :].astype(jnp.bfloat16), kv_heads)
    mixed, totals = attend_forward(query_rows, key_rows, value_rows, allowed)
    mixed = mixed.reshape(2 * length_total, q_width).astype(jnp.bfloat16)
    mixed_far = across(mixed)
    attn = dot_nn(mixed, out_here) + dot_nn(mixed_far, out_there)
    attn = attn[:length_total] + sibling(attn[length_total:])
    middle = inputs + RESIDUAL * attn
    square = jnp.sum(middle * middle, 1)
    inv_second = lax.rsqrt((square + across(square)) / width + EPS)
    normed_moe = (middle * inv_second[:, None] * gain_moe).astype(jnp.bfloat16)

    h_chunks = gather_tokens(normed_moe, step, True)
    base = (core * local + col * mine).astype(jnp.int32).reshape(1)
    results = [
        moe_chunk(base, r, h[0], h[1], c[0], c[1], weights)
        for r, h, c in zip(route_chunks, h_chunks, c_chunks)
    ]
    moe = scatter_tokens([(r[0], r[1]) for r in results], step)
    output = middle + RESIDUAL * moe
    grad_normed_moe = scatter_tokens([(r[2], r[3]) for r in results], step)
    hidden = [r[4] for r in results]
    slopes = [r[5] for r in results]
    h_own, h_far = [h[0] for h in h_chunks], [h[1] for h in h_chunks]
    c_own, c_far = [c[0] for c in c_chunks], [c[1] for c in c_chunks]

    half_mask = step // 2
    upper = ((member & half_mask) != 0).astype(jnp.int32).reshape(1)
    own_parts, far_parts = [], []
    for start in range(0, mine, split):
        keep_own, keep_far, send_own, send_far = weight_grads(
            upper, start, split, hidden, slopes, h_own, h_far, c_own, c_far
        )
        keep_own = keep_own + flip(send_own, "dp", half_mask).astype(jnp.float32)
        keep_far = keep_far + flip(send_far, "dp", half_mask).astype(jnp.float32)
        shape = (split, 3, units // 2, part)
        keep_own, keep_far = keep_own.reshape(shape), keep_far.reshape(shape)
        mask = half_mask // 2
        while mask:
            keep_own = halve(keep_own, member, mask, 2)
            keep_far = halve(keep_far, member, mask, 2)
            mask //= 2
        own_parts.append(keep_own)
        far_parts.append(across(keep_far.astype(jnp.bfloat16)).astype(jnp.float32))
    own_part, far_part = jnp.concatenate(own_parts, 0), jnp.concatenate(far_parts, 0)
    expert_grads = jnp.concatenate(
        [jnp.where(col == 0, own_part, far_part), jnp.where(col == 0, far_part, own_part)], 0
    )
    grad_gate = jnp.swapaxes(expert_grads[:, 0], 1, 2)
    grad_up = jnp.swapaxes(expert_grads[:, 1], 1, 2)
    grad_down = expert_grads[:, 2]

    def router_term(rows):
        both = sum(dot_tn(h, r[6]) for h, r in zip(rows, results))
        return both[:, :experts] + both[:, LANES : LANES + experts]

    grad_router = router_term(h_own) + across(router_term(h_far))

    scaled_moe = grad_normed_moe * gain_moe
    grad_gain_moe = jnp.sum(grad_normed_moe * middle * inv_second[:, None], 0)
    inner_moe = jnp.sum(middle * scaled_moe, 1)
    inner_moe = inner_moe + across(inner_moe)
    grad_final = cotangent.astype(jnp.float32)
    grad_middle = (
        grad_final
        + inv_second[:, None] * scaled_moe
        - middle * (inv_second**3 * inner_moe / width)[:, None]
    )
    grad_attn = (RESIDUAL * grad_middle).astype(jnp.bfloat16)
    da_own, da_far = both(grad_attn), both(across(grad_attn))
    grad_mixed = dot_nt(da_own, out_here) + dot_nt(da_far, out_far)
    grad_out_here = dot_tn(mixed, da_own)
    grad_out_there = dot_tn(mixed_far, da_own)
    grad_mixed = heads(grad_mixed.astype(jnp.bfloat16), kv_heads, group_size)
    grad_queries, grad_keys, grad_values = attend_backward(
        query_rows, key_rows, value_rows, allowed, totals, grad_mixed
    )
    grad_queries = unrotate(
        grad_queries.reshape(2 * length_total, -1, HEAD_WIDTH), cosine_table, sine_table
    )
    grad_keys = unrotate(
        grad_keys.reshape(2 * length_total, -1, HEAD_WIDTH), cosine_table, sine_table
    )
    grad_qkv = jnp.concatenate(
        [g.reshape(2 * length_total, -1) for g in (grad_queries, grad_keys, grad_values)], 1
    ).astype(jnp.bfloat16)
    grad_qkv_far = across(grad_qkv)
    grad_normed = dot_nt(grad_qkv, qkv_here) + dot_nt(grad_qkv_far, qkv_there)
    grad_normed = grad_normed[:length_total] + sibling(grad_normed[length_total:])
    grad_qkv_w = jnp.concatenate(
        [dot_tn(normed_own, grad_qkv), dot_tn(normed_own, grad_qkv_far)], 1
    )
    scaled_attn = grad_normed * gain_attn
    grad_gain_attn = jnp.sum(grad_normed * inputs * inv_first[:, None], 0)
    inner_attn = jnp.sum(inputs * scaled_attn, 1)
    inner_attn = inner_attn + across(inner_attn)
    grad_tokens = (
        grad_middle
        + inv_first[:, None] * scaled_attn
        - inputs * (inv_first**3 * inner_attn / width)[:, None]
    )
    grad_router = sum_small(grad_router.T).T
    grad_gain_moe = sum_small(grad_gain_moe)
    grad_gain_attn = sum_small(grad_gain_attn)
    grad_out_w = sum_over_dp(jnp.concatenate([grad_out_here, grad_out_there], 0), group)
    grad_out_w = jnp.where(
        col == 0, grad_out_w, jnp.concatenate([grad_out_w[q_width:], grad_out_w[:q_width]], 0)
    )
    grad_qkv_w = sum_over_dp(grad_qkv_w, group)
    grad_here, grad_there = grad_qkv_w[:, :qkv_width], grad_qkv_w[:, qkv_width:]

    def columns(start, stop):
        here, there = grad_here[:, start:stop], grad_there[:, start:stop]
        return jnp.where(
            col == 0,
            jnp.concatenate([here, there], 1),
            jnp.concatenate([there, here], 1),
        )

    return (
        output,
        grad_tokens,
        grad_gain_attn,
        columns(0, q_width),
        columns(q_width, q_width + kv_width),
        columns(q_width + kv_width, qkv_width),
        grad_out_w,
        grad_gain_moe,
        grad_router,
        grad_gate,
        grad_up,
        grad_down,
    )


def solution(mesh):
    in_specs = (
        P(("dp", "expert"), "col"),
        P("col"),
        P("col", "expert"),
        P("col", "expert"),
        P("col", "expert"),
        P("expert", "col"),
        P("col"),
        P("col", None),
        P("expert", "col", None),
        P("expert", "col", None),
        P("expert", None, "col"),
        P("dp", None),
        P(("dp", "expert"), None),
        P(("dp", "expert"), "col"),
    )
    out_specs = (
        P(("dp", "expert"), "col"),
        P(("dp", "expert"), "col"),
        P("col"),
        P("col", "expert"),
        P("col", "expert"),
        P("col", "expert"),
        P("expert", "col"),
        P("col"),
        P("col", None),
        P("expert", "col", "dp"),
        P("expert", "col", "dp"),
        P("expert", "dp", "col"),
    )
    return jax.shard_map(
        on_device, mesh=mesh, in_specs=in_specs, out_specs=out_specs, check_vma=False
    )
```

time: 3470 us -> 1100 us (0.32)
  waiting for transfers between devices: 2620 us -> 452 us
  Pallas kernels: 0 us -> 235 us
  local copies, waits for them, and re-layouts: 335 us -> 117 us
  blocking collectives: 144 us -> 0 us
  matrix products: 209 us -> 66.5 us
  starting transfers between devices: 1.98 us -> 136 us
  other arithmetic: 129 us -> 80.9 us
    reduce_scatter x9 -> x0, waiting for transfers between devices: 2200 us -> none  [the longest x1 603 us: spread_expert_grads(): lax.psum_scatter(grad_gate, 'dp', scatter_dimension=2, tiled=True)]
    ppermute x0 -> x116, waiting for transfers between devices: none -> 452 us  [flip(): return lax.ppermute(value, axis, [(i, i ^ mask) for i in range(size)])]
    all_gather x6 -> x0, waiting for transfers between devices: 277 us -> none  [the longest x2 196 us: share_gather(): return lax.all_gather(value_rows, 'col', axis=0, tiled=True)]
    pallas_call x0 -> x6, Pallas kernels: none -> 235 us  [the longest x4 162 us: moe_chunk(): pl.pallas_call(moe_kernel, out_shape=[jax.ShapeDtypeStruct((rows, w), jnp...]
    dot_general x21 -> x26, matrix products: 209 us -> 66.5 us  [the longest x12 19.2 us: dot_tn(): lax.dot_general(a, b, (((0,), (0,)), ((), ())), preferred_element_type=jn...]
    psum x3 -> x0, waiting for transfers between devices: 136 us -> none  [the longest x1 84.3 us: on_device(): lax.psum((grad_gain_attn, grad_gain_moe, grad_router), ('dp', 'expert'))]
    ppermute x0 -> x116, starting transfers between devices: none -> 136 us  [flip(): return lax.ppermute(value, axis, [(i, i ^ mask) for i in range(size)])]
    slice x14 -> x26, local copies, waits for them, and re-layouts: 126 us -> 10.3 us  [the longest x8 5.25 us: scatter_tokens(): s_far = add_wide(p_far[:rows], sibling(p_far[rows:]))]
  transfers between devices with their start and end apart: 18 -> 116, of which waited for: 17 -> 37; matrix products, arithmetic and copies ran while one was open for 11% -> 21% of each run, Pallas kernels for 0% -> 18%
where the time goes in v1:
time: 1100 us; the launch traced here: 1090 us
  waiting for transfers between devices  452 us (41%)
  Pallas kernels  235 us (21%)
  starting transfers between devices  136 us (12%)
  local copies, waits for them, and re-layouts  117 us (11%)
  other arithmetic  80.9 us (7%)
  matrix products  66.5 us (6%)
    ppermute x116, waiting for transfers between devices, flip(): return lax.ppermute(value, axis, [(i, i ^ mask) for i in range(size)])  452 us
    pallas_call x4, Pallas kernels, moe_chunk(): pl.pallas_call(moe_kernel, out_shape=[jax.ShapeDtypeStruct((rows, w), jnp...  162 us
    ppermute x116, starting transfers between devices, flip(): return lax.ppermute(value, axis, [(i, i ^ mask) for i in range(size)])  136 us
    pallas_call x2, Pallas kernels, weight_grads(): pl.pallas_call(weight_kernel, out_shape=[jax.ShapeDtypeStruct(shape, jnp....  73.6 us
    unnamed x309, local copies, waits for them, and re-layouts  45.7 us
  transfers between devices with their start and end apart: 116, of which 37 were waited for; matrix products, arithmetic and copies ran while one was open for 21% of the time, Pallas kernels for 18%

profile of v1, /device:TPU:0, one launch (start us, length us, event | category | flops | bytes accessed | tf_op | source)
XLA Modules:
  0.0 1091.3 jit_solution(3066181734922708430)
XLA Ops:
  49.1 12.3 %collective-permute-done.3 = f32[768]{0:T(1024)S(1)} collective-permute-done((f32[768]{0:T(1024)S(1)}, f32[768]{0:T(1024)S(1)}, u32[]{:S(2)}, u32[]{:S(2)}) %collective-permute-start.3) | collective-permute-done | bytes 3104 | tf_op jit(solution)/shard_map/ppermute | solution.py:107
  115.7 33.4 %collective-permute-start.43 = (bf16[512,768]{1,0:T(8,128)(2,1)}, bf16[512,768]{1,0:T(8,128)(2,1)S(1)}, u32[]{:S(2)}, u32[]{:S(2)}) collective-permute-start(bf16[512,768]{1,0:T(8,128)(2,1)} %collective-permute-done.13), channel_id=1, source_target_pairs={{0,16},{4,20},{8,24},{12,28},{16,0},{20,4},{24,8},{28,12},{1,17},{... | collective-permute-start | bytes 2359304 | tf_op jit(solution)/shard_map/ppermute | solution.py:107
  154.4 34.1 %collective-permute-done.43 = bf16[512,768]{1,0:T(8,128)(2,1)S(1)} collective-permute-done((bf16[512,768]{1,0:T(8,128)(2,1)}, bf16[512,768]{1,0:T(8,128)(2,1)S(1)}, u32[]{:S(2)}, u32[]{:S(2)}) %collective-permute-start.43) | collective-permute-done | bytes 786464 | tf_op jit(solution)/shard_map/ppermute | solution.py:107
  198.0 18.6 %collective-permute-done.18 = bf16[5,128,768]{2,1,0:T(8,128)(2,1)S(1)} collective-permute-done((bf16[5,128,768]{2,1,0:T(8,128)(2,1)}, bf16[5,128,768]{2,1,0:T(8,128)(2,1)S(1)}, u32[]{:S(2)}, u32[]{:S(2)}) %collective-permute-start.18) | collective-permute-done | bytes 983072 | tf_op jit(solution)/shard_map/ppermute | solution.py:107
  227.7 30.2 %collective-permute-done.16 = bf16[5,256,768]{1,2,0:T(8,128)(2,1)S(1)} collective-permute-done((bf16[5,256,768]{1,2,0:T(8,128)(2,1)S(1)}, bf16[5,256,768]{1,2,0:T(8,128)(2,1)S(1)}, u32[]{:S(2)}, u32[]{:S(2)}) %collective-permute-start.16) | collective-permute-done | bytes 1966112 | tf_op jit(solution)/shard_map/ppermute | solution.py:107
  275.6 19.4 %collective-permute-done.37 = bf16[512,768]{1,0:T(8,128)(2,1)} collective-permute-done((bf16[512,768]{1,0:T(8,128)(2,1)S(1)}, bf16[512,768]{1,0:T(8,128)(2,1)}, u32[]{:S(2)}, u32[]{:S(2)}) %collective-permute-start.37) | collective-permute-done | bytes 786464 | tf_op jit(solution)/shard_map/ppermute | solution.py:107
  303.2 40.3 %moe_rows.4 = (bf16[1024,768]{1,0:T(8,128)(2,1)}, bf16[1024,768]{1,0:T(8,128)(2,1)}, bf16[1024,768]{1,0:T(8,128)(2,1)}, bf16[1024,768]{1,0:T(8,128)(2,1)}, bf16[...) custom-call(s32[1]{0:T(128)} %bitcast.8.base_ref, s32[1024,8]{1,0:T(8,128)} %bitcast.10.routes_ref, ...), custom_call_target="tpu_custom_call" | custom-call | flops 24159191040 | bytes 40000000 | tf_op jit(solution)/shard_map/moe_rows/pallas_call | solution.py:210
  363.7 40.6 %moe_rows.7 = (bf16[1024,768]{1,0:T(8,128)(2,1)}, bf16[1024,768]{1,0:T(8,128)(2,1)}, bf16[1024,768]{1,0:T(8,128)(2,1)}, bf16[1024,768]{1,0:T(8,128)(2,1)}, bf16[...) custom-call(s32[1]{0:T(128)} %bitcast.8.base_ref, s32[1024,8]{1,0:T(8,128)} %bitcast.21.routes_ref, ...), custom_call_target="tpu_custom_call" | custom-call | flops 24159191040 | bytes 40000000 | tf_op jit(solution)/shard_map/moe_rows/pallas_call | solution.py:210
  407.8 40.3 %moe_rows.5 = (bf16[1024,768]{1,0:T(8,128)(2,1)}, bf16[1024,768]{1,0:T(8,128)(2,1)}, bf16[1024,768]{1,0:T(8,128)(2,1)}, bf16[1024,768]{1,0:T(8,128)(2,1)}, bf16[...) custom-call(s32[1]{0:T(128)} %bitcast.8.base_ref, s32[1024,8]{1,0:T(8,128)} %bitcast.19.routes_ref, ...), custom_call_target="tpu_custom_call" | custom-call | flops 24159191040 | bytes 40000000 | tf_op jit(solution)/shard_map/moe_rows/pallas_call | solution.py:210
  455.1 40.6 %moe_rows.6 = (bf16[1024,768]{1,0:T(8,128)(2,1)}, bf16[1024,768]{1,0:T(8,128)(2,1)}, bf16[1024,768]{1,0:T(8,128)(2,1)}, bf16[1024,768]{1,0:T(8,128)(2,1)}, bf16[...) custom-call(s32[1]{0:T(128)} %bitcast.8.base_ref, s32[1024,8]{1,0:T(8,128)} %bitcast.20.routes_ref, ...), custom_call_target="tpu_custom_call" | custom-call | flops 24159191040 | bytes 40000000 | tf_op jit(solution)/shard_map/moe_rows/pallas_call | solution.py:210
  516.0 17.4 %collective-permute-start.108 = (f32[40,768]{1,0:T(8,128)S(1)}, f32[40,768]{1,0:T(8,128)S(1)}, u32[]{:S(2)}, u32[]{:S(2)}) collective-permute-start(f32[40,768]{1,0:T(8,128)S(1)} %add.405), channel_id=1, source_target_pairs={{0,8},{4,12},{8,0},{12,4},{16,24},{20,28},{24,16},{28,20},{1,9},{5... | collective-permute-start | bytes 368648 | tf_op jit(solution)/shard_map/ppermute | solution.py:107
  533.5 36.7 %expert_weight_grads.3 = (f32[5,192,768]{2,1,0:T(8,128)}, f32[5,192,768]{2,1,0:T(8,128)}, bf16[5,192,768]{2,1,0:T(8,128)(2,1)}, bf16[5,192,768]{2,1,0:T(8,128)(2,1)}) custom-call(s32[1]{0:T(128)} %bitcast.36.side_ref, bf16[1024,1280]{1,0:T(8,128)(2,1)} %get-tuple-element.68.refs_0_, bf16[1024,1280]{1,0:T(8,128)(2,1)} %get-tuple-element.69.refs_1_, ...), custom_call_target="tpu_custom_call" | custom-call | flops 24159191040 | bytes 40000000 | tf_op jit(solution)/shard_map/expert_weight_grads/pallas_call | solution.py:259
  571.6 36.9 %expert_weight_grads.2 = (f32[5,192,768]{2,1,0:T(8,128)}, f32[5,192,768]{2,1,0:T(8,128)}, bf16[5,192,768]{2,1,0:T(8,128)(2,1)}, bf16[5,192,768]{2,1,0:T(8,128)(2,1)}) custom-call(s32[1]{0:T(128)} %bitcast.36.side_ref, bf16[1024,1280]{1,0:T(8,128)(2,1)} %get-tuple-element.68.refs_0_, bf16[1024,1280]{1,0:T(8,128)(2,1)} %get-tuple-element.69.refs_1_, ...), custom_call_target="tpu_custom_call" | custom-call | flops 24159191040 | bytes 40000000 | tf_op jit(solution)/shard_map/expert_weight_grads/pallas_call | solution.py:259
  625.7 15.4 %collective-permute-done.75 = bf16[512,768]{1,0:T(8,128)(2,1)S(1)} collective-permute-done((bf16[512,768]{1,0:T(8,128)(2,1)S(1)}, bf16[512,768]{1,0:T(8,128)(2,1)S(1)}, u32[]{:S(2)}, u32[]{:S(2)}) %collective-permute-start.75) | collective-permute-done | bytes 786464 | tf_op jit(solution)/shard_map/ppermute | solution.py:107
  641.1 16.0 %collective-permute-done.71 = bf16[512,768]{1,0:T(8,128)(2,1)S(1)} collective-permute-done((bf16[512,768]{1,0:T(8,128)(2,1)S(1)}, bf16[512,768]{1,0:T(8,128)(2,1)S(1)}, u32[]{:S(2)}, u32[]{:S(2)}) %collective-permute-start.71) | collective-permute-done | bytes 786464 | tf_op jit(solution)/shard_map/ppermute | solution.py:107
  667.3 11.9 %collective-permute-done.64 = bf16[512,768]{1,0:T(8,128)(2,1)S(1)} collective-permute-done((bf16[512,768]{1,0:T(8,128)(2,1)S(1)}, bf16[512,768]{1,0:T(8,128)(2,1)S(1)}, u32[]{:S(2)}, u32[]{:S(2)}) %collective-permute-start.64) | collective-permute-done | bytes 786464 | tf_op jit(solution)/shard_map/ppermute | solution.py:107
  681.8 15.8 %collective-permute-done.76 = bf16[512,768]{1,0:T(8,128)(2,1)S(1)} collective-permute-done((bf16[512,768]{1,0:T(8,128)(2,1)S(1)}, bf16[512,768]{1,0:T(8,128)(2,1)S(1)}, u32[]{:S(2)}, u32[]{:S(2)}) %collective-permute-start.76) | collective-permute-done | bytes 786464 | tf_op jit(solution)/shard_map/ppermute | solution.py:107
  697.6 35.2 %collective-permute-done.72 = bf16[512,768]{1,0:T(8,128)(2,1)S(1)} collective-permute-done((bf16[512,768]{1,0:T(8,128)(2,1)S(1)}, bf16[512,768]{1,0:T(8,128)(2,1)S(1)}, u32[]{:S(2)}, u32[]{:S(2)}) %collective-permute-start.72) | collective-permute-done | bytes 786464 | tf_op jit(solution)/shard_map/ppermute | solution.py:107
  741.8 26.3 %collective-permute-done.110 = bf16[5,192,768]{2,1,0:T(8,128)(2,1)S(1)} collective-permute-done((bf16[5,192,768]{2,1,0:T(8,128)(2,1)S(1)}, bf16[5,192,768]{2,1,0:T(8,128)(2,1)S(1)}, u32[]{:S(2)}, u32[]{:S(2)}) %collective-permute-start.110) | collective-permute-done | bytes 1474592 | tf_op jit(solution)/shard_map/ppermute | solution.py:107
  771.5 26.8 %collective-permute-done.112 = bf16[5,192,768]{2,1,0:T(8,128)(2,1)S(1)} collective-permute-done((bf16[5,192,768]{2,1,0:T(8,128)(2,1)S(1)}, bf16[5,192,768]{2,1,0:T(8,128)(2,1)S(1)}, u32[]{:S(2)}, u32[]{:S(2)}) %collective-permute-start.112) | collective-permute-done | bytes 1474592 | tf_op jit(solution)/shard_map/ppermute | solution.py:107
  821.4 16.8 %collective-permute-done.79 = bf16[512,768]{1,0:T(8,128)(2,1)S(1)} collective-permute-done((bf16[512,768]{1,0:T(8,128)(2,1)S(1)}, bf16[512,768]{1,0:T(8,128)(2,1)S(1)}, u32[]{:S(2)}, u32[]{:S(2)}) %collective-permute-start.79) | collective-permute-done | bytes 786464 | tf_op jit(solution)/shard_map/ppermute | solution.py:107
  936.3 22.3 %collective-permute-done.113 = bf16[5,3,64,768]{3,2,0,1:T(8,128)(2,1)S(1)} collective-permute-done((bf16[5,3,64,768]{3,2,0,1:T(8,128)(2,1)S(1)}, bf16[5,3,64,768]{3,2,0,1:T(8,128)(2,1)S(1)}, u32[]{:S(2)}, u32[]{:S(2)}) %collective-permute-start.113) | collective-permute-done | bytes 1474592 | tf_op jit(solution)/shard_map/ppermute | solution.py:107
  991.9 43.0 %collective-permute-done.92 = bf16[96,1280]{1,0:T(8,128)(2,1)S(1)} collective-permute-done((bf16[96,1280]{1,0:T(8,128)(2,1)S(1)}, bf16[96,1280]{1,0:T(8,128)(2,1)S(1)}, u32[]{:S(2)}, u32[]{:S(2)}) %collective-permute-start.92) | collective-permute-done | bytes 245792 | tf_op jit(solution)/shard_map/ppermute | solution.py:107
  1051.4 10.8 collective-permute-done.84
  (722 shorter events, 446.5 us)
Async XLA Ops:
  3.8 83.6 %collective-permute-start.41 = (bf16[512,768]{1,0:T(8,128)(2,1)}, bf16[512,768]{1,0:T(8,128)(2,1)}, u32[]{:S(2)}, u32[]{:S(2)}) collective-permute-start(bf16[512,768]{1,0:T(8,128)(2,1)} %param.27), channel_id=1, source_target_pairs={{0,16},{4,20},{8,24},{12,28},{16,0},{20,4},{24,8},{28,12},{1,17},{... | collective-permute-start | bytes 2359304 | tf_op jit(solution)/shard_map/ppermute | solution.py:107
  6.4 108.7 %collective-permute-start.26 = (bf16[512,768]{1,0:T(8,128)(2,1)}, bf16[512,768]{1,0:T(8,128)(2,1)}, u32[]{:S(2)}, u32[]{:S(2)}) collective-permute-start(bf16[512,768]{1,0:T(8,128)(2,1)} %param.27), channel_id=1, source_target_pairs={{0,8},{4,12},{8,0},{12,4},{16,24},{20,28},{24,16},{28,20},{1,9},{5... | collective-permute-start | bytes 2359304 | tf_op jit(solution)/shard_map/ppermute | solution.py:107
  87.3 62.9 %collective-permute-start.17 = (bf16[5,128,768]{2,1,0:T(8,128)(2,1)}, bf16[5,128,768]{2,1,0:T(8,128)(2,1)}, u32[]{:S(2)}, u32[]{:S(2)}) collective-permute-start(bf16[5,128,768]{2,1,0:T(8,128)(2,1)} %constant_dynamic-slice_fusion), channel_id=1, source_target_pairs={{0,1},{1,0},{2,3},{3,2},{4,5},{5,4},{6,7},{7,6},{8,9},{9,8},{10,11... | collective-permute-start | bytes 2949128 | tf_op jit(solution)/shard_map/ppermute | solution.py:107
  115.1 81.6 %collective-permute-start.15 = (bf16[5,256,768]{1,2,0:T(8,128)(2,1)S(1)}, bf16[5,256,768]{1,2,0:T(8,128)(2,1)S(1)}, u32[]{:S(2)}, u32[]{:S(2)}) collective-permute-start(bf16[5,256,768]{1,2,0:T(8,128)(2,1)S(1)} %copy-done.55), channel_id=1, source_target_pairs={{0,1},{1,0},{2,3},{3,2},{4,5},{5,4},{6,7},{7,6},{8,9},{9,8},{10,11... | collective-permute-start | bytes 5898248 | tf_op jit(solution)/shard_map/ppermute | solution.py:107
  115.7 72.8 %collective-permute-start.43 = (bf16[512,768]{1,0:T(8,128)(2,1)}, bf16[512,768]{1,0:T(8,128)(2,1)S(1)}, u32[]{:S(2)}, u32[]{:S(2)}) collective-permute-start(bf16[512,768]{1,0:T(8,128)(2,1)} %collective-permute-done.13), channel_id=1, source_target_pairs={{0,16},{4,20},{8,24},{12,28},{16,0},{20,4},{24,8},{28,12},{1,17},{... | collective-permute-start | bytes 2359304 | tf_op jit(solution)/shard_map/ppermute | solution.py:107
  227.5 67.4 %collective-permute-start.37 = (bf16[512,768]{1,0:T(8,128)(2,1)S(1)}, bf16[512,768]{1,0:T(8,128)(2,1)}, u32[]{:S(2)}, u32[]{:S(2)}) collective-permute-start(bf16[512,768]{1,0:T(8,128)(2,1)S(1)} %multiply_convert_fusion.2), channel_id=1, source_target_pairs={{0,16},{4,20},{8,24},{12,28},{16,0},{20,4},{24,8},{28,12},{1,17},{... | collective-permute-start | bytes 2359304 | tf_op jit(solution)/shard_map/ppermute | solution.py:107
  272.5 77.1 %collective-permute-start.52 = (bf16[512,768]{1,0:T(8,128)(2,1)}, bf16[512,768]{1,0:T(8,128)(2,1)S(1)}, u32[]{:S(2)}, u32[]{:S(2)}) collective-permute-start(bf16[512,768]{1,0:T(8,128)(2,1)} %collective-permute-done.50), channel_id=1, source_target_pairs={{0,1},{1,0},{2,3},{3,2},{4,5},{5,4},{6,7},{7,6},{8,9},{9,8},{10,11... | collective-permute-start | bytes 2359304 | tf_op jit(solution)/shard_map/ppermute | solution.py:107
  350.5 103.4 %collective-permute-start.36 = (s32[8,1024]{0,1:T(8,128)}, s32[8,1024]{0,1:T(8,128)}, u32[]{:S(2)}, u32[]{:S(2)}) collective-permute-start(s32[8,1024]{0,1:T(8,128)} %copy.131), channel_id=1, source_target_pairs={{0,16},{4,20},{8,24},{12,28},{16,0},{20,4},{24,8},{28,12},{1,17},{... | collective-permute-start | bytes 98312 | tf_op jit(solution)/shard_map/ppermute | solution.py:107
  356.3 95.7 %collective-permute-start.40 = (bf16[512,768]{1,0:T(8,128)(2,1)}, bf16[512,768]{1,0:T(8,128)(2,1)}, u32[]{:S(2)}, u32[]{:S(2)}) collective-permute-start(bf16[512,768]{1,0:T(8,128)(2,1)} %collective-permute-done.39), channel_id=1, source_target_pairs={{0,2},{2,0},{1,3},{3,1},{4,6},{6,4},{5,7},{7,5},{8,10},{10,8},{9,1... | collective-permute-start | bytes 2359304 | tf_op jit(solution)/shard_map/ppermute | solution.py:107
  513.0 107.1 %collective-permute-start.65 = (bf16[512,768]{1,0:T(8,128)(2,1)}, bf16[512,768]{1,0:T(8,128)(2,1)}, u32[]{:S(2)}, u32[]{:S(2)}) collective-permute-start(bf16[512,768]{1,0:T(8,128)(2,1)} %slice.244), channel_id=1, source_target_pairs={{0,2},{2,0},{1,3},{3,1},{4,6},{6,4},{5,7},{7,5},{8,10},{10,8},{9,1... | collective-permute-start | bytes 2359304 | tf_op jit(solution)/shard_map/ppermute | solution.py:107
  514.6 102.3 %collective-permute-start.74 = (bf16[512,768]{1,0:T(8,128)(2,1)}, bf16[512,768]{1,0:T(8,128)(2,1)}, u32[]{:S(2)}, u32[]{:S(2)}) collective-permute-start(bf16[512,768]{1,0:T(8,128)(2,1)} %slice.254), channel_id=1, source_target_pairs={{0,2},{2,0},{1,3},{3,1},{4,6},{6,4},{5,7},{7,5},{8,10},{10,8},{9,1... | collective-permute-start | bytes 2359304 | tf_op jit(solution)/shard_map/ppermute | solution.py:107
  515.5 103.2 %collective-permute-start.70 = (bf16[512,768]{1,0:T(8,128)(2,1)}, bf16[512,768]{1,0:T(8,128)(2,1)}, u32[]{:S(2)}, u32[]{:S(2)}) collective-permute-start(bf16[512,768]{1,0:T(8,128)(2,1)} %slice.250), channel_id=1, source_target_pairs={{0,2},{2,0},{1,3},{3,1},{4,6},{6,4},{5,7},{7,5},{8,10},{10,8},{9,1... | collective-permute-start | bytes 2359304 | tf_op jit(solution)/shard_map/ppermute | solution.py:107
  658.8 77.1 %collective-permute-start.111 = (bf16[5,192,768]{2,1,0:T(8,128)(2,1)S(1)}, bf16[5,192,768]{2,1,0:T(8,128)(2,1)S(1)}, u32[]{:S(2)}, u32[]{:S(2)}) collective-permute-start(bf16[5,192,768]{2,1,0:T(8,128)(2,1)S(1)} %copy-done.139), channel_id=1, source_target_pairs={{0,4},{4,0},{8,12},{12,8},{16,20},{20,16},{24,28},{28,24},{1,5},{5... | collective-permute-start | bytes 4423688 | tf_op jit(solution)/shard_map/ppermute | solution.py:107
  664.0 68.9 %collective-permute-start.72 = (bf16[512,768]{1,0:T(8,128)(2,1)S(1)}, bf16[512,768]{1,0:T(8,128)(2,1)S(1)}, u32[]{:S(2)}, u32[]{:S(2)}) collective-permute-start(bf16[512,768]{1,0:T(8,128)(2,1)S(1)} %add_convert_fusion.5), channel_id=1, source_target_pairs={{0,16},{4,20},{8,24},{12,28},{16,0},{20,4},{24,8},{28,12},{1,17},{... | collective-permute-start | bytes 2359304 | tf_op jit(solution)/shard_map/ppermute | solution.py:107
  664.5 69.7 %collective-permute-start.68 = (bf16[512,768]{1,0:T(8,128)(2,1)S(1)}, bf16[512,768]{1,0:T(8,128)(2,1)S(1)}, u32[]{:S(2)}, u32[]{:S(2)}) collective-permute-start(bf16[512,768]{1,0:T(8,128)(2,1)S(1)} %add_convert_fusion.7), channel_id=1, source_target_pairs={{0,1},{1,0},{2,3},{3,2},{4,5},{5,4},{6,7},{7,6},{8,9},{9,8},{10,11... | collective-permute-start | bytes 2359304 | tf_op jit(solution)/shard_map/ppermute | solution.py:107
  697.6 108.3 %collective-permute-start.58 = (bf16[512,768]{1,0:T(8,128)(2,1)S(1)}, bf16[512,768]{1,0:T(8,128)(2,1)S(1)}, u32[]{:S(2)}, u32[]{:S(2)}) collective-permute-start(bf16[512,768]{1,0:T(8,128)(2,1)S(1)} %slice.236), channel_id=1, source_target_pairs={{0,2},{2,0},{1,3},{3,1},{4,6},{6,4},{5,7},{7,5},{8,10},{10,8},{9,1... | collective-permute-start | bytes 2359304 | tf_op jit(solution)/shard_map/ppermute | solution.py:107
  734.1 64.2 %collective-permute-start.112 = (bf16[5,192,768]{2,1,0:T(8,128)(2,1)S(1)}, bf16[5,192,768]{2,1,0:T(8,128)(2,1)S(1)}, u32[]{:S(2)}, u32[]{:S(2)}) collective-permute-start(bf16[5,192,768]{2,1,0:T(8,128)(2,1)S(1)} %copy-done.136), channel_id=1, source_target_pairs={{0,4},{4,0},{8,12},{12,8},{16,20},{20,16},{24,28},{28,24},{1,5},{5... | collective-permute-start | bytes 4423688 | tf_op jit(solution)/shard_map/ppermute | solution.py:107
  739.6 71.6 %collective-permute-start.45 = (bf16[512,768]{1,0:T(8,128)(2,1)S(1)}, bf16[512,768]{1,0:T(8,128)(2,1)S(1)}, u32[]{:S(2)}, u32[]{:S(2)}) collective-permute-start(bf16[512,768]{1,0:T(8,128)(2,1)S(1)} %slice.232), channel_id=1, source_target_pairs={{0,2},{2,0},{1,3},{3,1},{4,6},{6,4},{5,7},{7,5},{8,10},{10,8},{9,1... | collective-permute-start | bytes 2359304 | tf_op jit(solution)/shard_map/ppermute | solution.py:107
  811.1 87.8 %collective-permute-start.32 = (bf16[512,768]{1,0:T(8,128)(2,1)}, bf16[512,768]{1,0:T(8,128)(2,1)}, u32[]{:S(2)}, u32[]{:S(2)}) collective-permute-start(bf16[512,768]{1,0:T(8,128)(2,1)} %slice.228), channel_id=1, source_target_pairs={{0,2},{2,0},{1,3},{3,1},{4,6},{6,4},{5,7},{7,5},{8,10},{10,8},{9,1... | collective-permute-start | bytes 2359304 | tf_op jit(solution)/shard_map/ppermute | solution.py:107
  839.5 204.2 %collective-permute-start.20 = (bf16[512,768]{1,0:T(8,128)(2,1)}, bf16[512,768]{1,0:T(8,128)(2,1)}, u32[]{:S(2)}, u32[]{:S(2)}) collective-permute-start(bf16[512,768]{1,0:T(8,128)(2,1)} %slice.224), channel_id=1, source_target_pairs={{0,2},{2,0},{1,3},{3,1},{4,6},{6,4},{5,7},{7,5},{8,10},{10,8},{9,1... | collective-permute-start | bytes 2359304 | tf_op jit(solution)/shard_map/ppermute | solution.py:107
  850.5 83.7 %collective-permute-start.115 = (bf16[5,3,64,768]{3,2,0,1:T(8,128)(2,1)}, bf16[5,3,64,768]{3,2,0,1:T(8,128)(2,1)}, u32[]{:S(2)}, u32[]{:S(2)}) collective-permute-start(bf16[5,3,64,768]{3,2,0,1:T(8,128)(2,1)} %copy.153), channel_id=1, source_target_pairs={{0,1},{1,0},{2,3},{3,2},{4,5},{5,4},{6,7},{7,6},{8,9},{9,8},{10,11... | collective-permute-start | bytes 4423688 | tf_op jit(solution)/shard_map/ppermute | solution.py:107
  918.9 149.9 %collective-permute-start.31 = (bf16[512,768]{1,0:T(8,128)(2,1)}, bf16[512,768]{1,0:T(8,128)(2,1)}, u32[]{:S(2)}, u32[]{:S(2)}) collective-permute-start(bf16[512,768]{1,0:T(8,128)(2,1)} %add_convert_fusion.16), channel_id=1, source_target_pairs={{0,8},{4,12},{8,0},{12,4},{16,24},{20,28},{24,16},{28,20},{1,9},{5... | collective-permute-start | bytes 2359304 | tf_op jit(solution)/shard_map/ppermute | solution.py:107
  971.3 63.8 %collective-permute-start.83 = (f32[512,768]{1,0:T(8,128)S(1)}, f32[512,768]{1,0:T(8,128)S(1)}, u32[]{:S(2)}, u32[]{:S(2)}) collective-permute-start(f32[512,768]{1,0:T(8,128)S(1)} %slice.294), channel_id=1, source_target_pairs={{0,2},{2,0},{1,3},{3,1},{4,6},{6,4},{5,7},{7,5},{8,10},{10,8},{9,1... | collective-permute-start | bytes 4718600 | tf_op jit(solution)/shard_map/ppermute | solution.py:107
  990.7 78.3 %collective-permute-start.61 = (bf16[512,768]{1,0:T(8,128)(2,1)}, bf16[512,768]{1,0:T(8,128)(2,1)S(1)}, u32[]{:S(2)}, u32[]{:S(2)}) collective-permute-start(bf16[512,768]{1,0:T(8,128)(2,1)} %add_convert_fusion.10), channel_id=1, source_target_pairs={{0,24},{4,28},{8,16},{12,20},{16,8},{20,12},{24,0},{28,4},{1,25},{... | collective-permute-start | bytes 2359304 | tf_op jit(solution)/shard_map/ppermute | solution.py:107
  (237 other events, 4151.6 us)

commit v2 on v0

v2 whole, which is shorter than its diff:
```python
import functools
import math

import jax
import jax.numpy as jnp
from jax import lax
from jax.experimental import pallas as pl
from jax.experimental.pallas import tpu as pltpu
from jax.sharding import PartitionSpec as P

HEAD_WIDTH = 64
(
    COT,
    TOK,
    DOWN,
    QKV,
    GATE,
    UP,
    ROUTER,
    GAIN,
    ROUTES,
    MIXED,
    ATTN,
    SQUARE,
    H,
    BACK,
    DA,
    DQKV,
    INNER,
    GRADS,
    MOE,
    SMALL,
    SUM,
) = range(21)
X, C, Y, Z, FAR_X, FAR_C, FAR_Z = range(7)
ZPARTS = 4
LANES = 128


EPS = 1e-06
RESIDUAL = 0.22
SCORE_SCALE = 0.015625
THETA = 10000.0
NEG = -1000000000.0


def doc_positions(seg_row):
    length_total = seg_row.shape[0]
    index = jnp.arange(length_total, dtype=jnp.int32)
    before = jnp.concatenate([jnp.full((1,), -1, jnp.int32), seg_row[:-1]])
    starts = jnp.where(seg_row != before, index, 0)
    return index - lax.cummax(starts, axis=0)


def flip(value, axis, mask=1):
    size = lax.axis_size(axis)
    return lax.ppermute(value, axis, [(i, i ^ mask) for i in range(size)])


def dot_nn(a, b):
    return jnp.dot(a, b, preferred_element_type=jnp.float32)


def dot_nt(a, b):
    return lax.dot_general(a, b, (((1,), (1,)), ((), ())), preferred_element_type=jnp.float32)


def dot_tn(a, b):
    return lax.dot_general(a, b, (((0,), (0,)), ((), ())), preferred_element_type=jnp.float32)


def add_wide(*parts):
    return sum(p.astype(jnp.float32) for p in parts)


def low(value):
    return value.astype(jnp.bfloat16)


class Place:
    def __init__(self):
        self.col = lax.axis_index("col")
        self.core = lax.axis_index("expert")
        group = lax.axis_index("dp")
        self.step = lax.axis_size("dp") // ZPARTS
        self.zed, self.member = group // self.step, group % self.step
        self.half = self.step // 2
        self.side = (self.member // self.half) % 2

    def x(self):
        return {"col": 1 - self.col}

    def c(self):
        return {"expert": 1 - self.core}

    def y(self):
        return {"dp": self.zed * self.step + self.member + self.half * (1 - 2 * self.side)}

    def z(self, k):
        zed = self.zed
        other = (zed + 1 - 2 * (zed % 2), (zed + 2) % ZPARTS, ZPARTS - 1 - zed)[k - 1]
        return {"dp": other * self.step + self.member}

    def bits(self):
        levels = []
        mask = self.half
        while mask:
            bit = (self.member // mask) % 2
            partner = self.zed * self.step + self.member + mask * (1 - 2 * bit)
            levels.append(({"dp": partner}, bit))
            mask //= 2
        return levels, [(self.z(1), self.zed % 2), (self.z(2), self.zed // 2)]


def greet(partners):
    barrier = pltpu.get_barrier_semaphore()
    for partner in partners:
        pl.semaphore_signal(
            barrier, inc=1, device_id=partner, device_id_type=pl.DeviceIdType.MESH
        )
    pl.semaphore_wait(barrier, len(partners))


class Transfers:
    def __init__(self, sems):
        self.sems, self.table, self.waited = sems, {}, set()

    def add(self, key, src, dst, partner):
        self.table[key] = (len(self.table), src, dst, partner)

    def copy(self, key):
        i, src, dst, partner = self.table[key]
        return pltpu.make_async_remote_copy(
            src_ref=src,
            dst_ref=dst,
            send_sem=self.sems.at[0, i],
            recv_sem=self.sems.at[1, i],
            device_id=partner,
            device_id_type=pl.DeviceIdType.MESH,
        )

    def start(self, *keys):
        for key in keys:
            self.copy(key).start()

    def arrived(self, *keys):
        for key in keys:
            self.waited.add(key)
            self.copy(key).wait_recv()

    def sent(self, *keys):
        for key in keys:
            self.copy(key).wait_send()

    def finish(self, *sent):
        for key in self.table:
            if key not in sent:
                self.copy(key).wait_send()
        for key in self.table:
            if key not in self.waited:
                self.copy(key).wait_recv()


def moves(sems, *pairs):
    copies = [pltpu.make_async_copy(src, dst, sems.at[i]) for i, (src, dst) in enumerate(pairs)]
    for copy in copies:
        copy.start()
    for copy in copies:
        copy.wait()


ANY = pl.BlockSpec(memory_space=pl.ANY)


def whole_block(a):
    return pl.BlockSpec(a.shape, lambda *_: (0,) * a.ndim, pipeline_mode=pl.Buffered(1))


def turn(block, cosine, sine):
    lane = lax.broadcasted_iota(jnp.int32, block.shape, 1) % HEAD_WIDTH
    ahead = pltpu.roll(block, LANES - HEAD_WIDTH // 2, 1)
    behind = pltpu.roll(block, HEAD_WIDTH // 2, 1)
    return block * cosine + jnp.where(lane < HEAD_WIDTH // 2, ahead, behind) * sine


def score_tiles(rows):
    half = rows // 2
    return ((0, half, half), (half, rows, rows))


def allowed_tile(seg_row, seg_col, across_keys):
    shape = (seg_col.shape[0], seg_row.shape[1])
    down, along = (lax.broadcasted_iota(jnp.int32, shape, axis) for axis in (0, 1))
    order = down <= along if across_keys else along <= down
    return jnp.where((seg_row == seg_col) & order, 1.0, 0.0)


def swap_heads(value):
    return pltpu.roll(value.astype(jnp.float32), HEAD_WIDTH, 1).astype(value.dtype)


def attend_rows(q_ref, keys_ref, values_ref, allowed_ref, out_ref, base, blocks):
    rows = allowed_ref.shape[0]
    group = blocks

    def body(j, carry):
        cols = pl.ds(pl.multiple_of(j * LANES, LANES), LANES)
        for start, stop, keys in score_tiles(rows):
            lane = lax.broadcasted_iota(jnp.int32, (stop - start, LANES), 1)
            query = q_ref[base + start : base + stop, cols]
            allowed = allowed_ref[start:stop, :keys] > 0
            outs = []
            for side, part in enumerate((lane < HEAD_WIDTH, lane >= HEAD_WIDTH)):
                other = (2 * j + side) // group
                other = other + side - 2 * other * side
                key_rows = keys_ref[other, base : base + keys, :]
                scores = dot_nt(jnp.where(part, query, jnp.zeros_like(query)), key_rows)
                scores = jnp.where(allowed, scores * SCORE_SCALE, NEG)
                expo = jnp.exp(scores - jnp.max(scores, axis=1, keepdims=True))
                probs = expo * (1.0 / jnp.sum(expo, axis=1, keepdims=True))
                outs.append(dot_nn(low(probs), values_ref[other, base : base + keys, :]))
            mixed = jnp.where(lane < HEAD_WIDTH, outs[0], outs[1])
            out_ref[base + start : base + stop, cols] = low(mixed)
        return carry

    lax.fori_loop(0, blocks, body, 0)


def weight_slice(ref, which, half, split, zed, wide):
    first = (2 * which + half) * split
    units = pl.ds(pl.multiple_of(zed * LANES, LANES), LANES)
    if wide:
        return ref.at[pl.ds(first, split), units, :]
    return ref.at[pl.ds(first, split), :, units]


def qkv_slices(refs, which):
    widths = [ref.shape[1] // 2 for ref in refs]
    return [
        ref.at[:, pl.ds(pl.multiple_of(which * w, LANES), w)] for ref, w in zip(refs, widths)
    ]


def qkv_targets(target, refs):
    widths = [ref.shape[1] // 2 for ref in refs]
    starts = [sum(widths[:i]) for i in range(len(widths))]
    return [target.at[:, pl.ds(start, w)] for start, w in zip(starts, widths)]


def front_kernel(*refs):
    tokens, cot, w_down, w_gate, w_up, router, routes = refs[:7]
    qkv = refs[7:10]
    gain, gain_moe, w_out, cosine, sine, seg_row, seg_col = refs[10:17]
    (
        down_got,
        down_other,
        gate_got,
        gate_other,
        up_got,
        up_other,
        router_far,
        c_own,
        c_far,
        route_all,
        grad_hidden,
        q_ref,
        keys,
        values,
        mixed,
        mixed_far,
        normed,
        inv_first,
        middle_ref,
        inv_second,
        h2_ref,
    ) = refs[17:38]
    tok, qkv_here, qkv_far, gain_far, normed_far, give, got, square, square_far = refs[38:47]
    own_buf, far_buf, down_own, down_buf, grad_buf, allowed, sems, local = refs[47:]
    place = Place()
    t = Transfers(sems)
    x, c, y = place.x(), place.c(), place.y()
    z = [None] + [place.z(k) for k in range(1, ZPARTS)]
    rows, part = tokens.shape
    ks = range(1, ZPARTS)
    t.add((TOK, X), tokens, tok.at[0], x)
    t.add((TOK, C), tokens, tok.at[1], c)
    t.add((TOK, FAR_C), tok.at[0], tok.at[2], c)
    there = qkv_slices(qkv, 1 - place.col)
    for i, target in enumerate(qkv_targets(qkv_far, qkv)):
        t.add((QKV, X, i), there[i], target, x)
    t.add((GAIN, X), gain, gain_far, x)
    t.add((ROUTER, X), router, router_far, x)
    t.add((COT, X), cot, c_far.at[0, 0], x)
    t.add((COT, C, 0), cot, c_own.at[0, 1], c)
    t.add((COT, FAR_C, 0), c_far.at[0, 0], c_far.at[0, 1], c)
    t.add((ROUTES, C, 0), routes, route_all.at[0, 1], c)
    for k in ks:
        t.add((COT, Z, k), cot, c_own.at[k, 0], z[k])
        t.add((COT, FAR_Z, k), c_far.at[0, 0], c_far.at[k, 0], z[k])
        t.add((COT, C, k), c_own.at[k, 0], c_own.at[k, 1], c)
        t.add((COT, FAR_C, k), c_far.at[k, 0], c_far.at[k, 1], c)
        t.add((ROUTES, Z, k), routes, route_all.at[k, 0], z[k])
        t.add((ROUTES, C, k), route_all.at[k, 0], route_all.at[k, 1], c)
    split = down_got.shape[0]
    for key, ref, land, other in (
        (DOWN, w_down, down_got, down_other),
        (GATE, w_gate, gate_got, gate_other),
        (UP, w_up, up_got, up_other),
    ):
        src = weight_slice(ref, 1 - place.col, place.side, split, place.zed, key == DOWN)
        t.add((key, X), src, land, x)
        t.add((key, Y), land, other, y)
    for i in range(2):
        cut = pl.ds(rows * i, rows)
        t.add((MIXED, X, i), mixed.at[cut], mixed_far.at[cut], x)
    t.add((ATTN, C), give, got, c)
    t.add((SQUARE, X), square, square_far, x)

    greet([x, c, y, *z[1:]])
    t.start((COT, X), (TOK, X), (GAIN, X), *[(QKV, X, i) for i in range(3)], (ROUTER, X))
    t.start((TOK, C), (COT, C, 0), (ROUTES, C, 0), *[(ROUTES, Z, k) for k in ks])
    t.start((COT, Z, 1), (COT, Z, 2), (COT, Z, 3))
    own_cut = functools.partial(weight_slice, w_down, place.col, split=split, zed=place.zed)
    moves(
        local,
        (cot, c_own.at[0, 0]),
        (routes, route_all.at[0, 0]),
        (own_cut(half=place.side, wide=True), down_own.at[pl.ds(0, split)]),
        (own_cut(half=1 - place.side, wide=True), down_own.at[pl.ds(split, split)]),
        *zip(qkv_slices(qkv, place.col), qkv_targets(qkv_here, qkv)),
    )

    def norm(own, far, base):
        own, far = own.astype(jnp.float32), far.astype(jnp.float32)
        total = jnp.sum(own * own, 1, keepdims=True) + jnp.sum(far * far, 1, keepdims=True)
        inv = lax.rsqrt(total / (2 * part) + EPS)
        normed[base : base + rows, :] = (own * inv * gain[...]).astype(jnp.bfloat16)
        normed_far[base : base + rows, :] = (far * inv * gain_far[...]).astype(jnp.bfloat16)
        return inv

    def masks(b):
        allowed[...] = allowed_tile(seg_row[b : b + 1, :], seg_col[:, b : b + 1], False)

    masks(1)
    t.arrived((COT, X))
    t.start((COT, FAR_C, 0), *[(COT, FAR_Z, k) for k in ks])
    t.arrived((TOK, X), (GAIN, X))
    t.start((TOK, FAR_C))
    inv = norm(tokens[...], tok[0], 0)
    inv_first[...] = jnp.broadcast_to(inv, inv_first.shape)
    t.arrived((TOK, C), (TOK, FAR_C))
    norm(tok[1], tok[2], rows)
    for k in ks:
        t.arrived((ROUTES, Z, k))
        t.start((ROUTES, C, k))
    t.arrived((COT, Z, 1))
    t.start((COT, C, 1))
    t.arrived(*[(QKV, X, i) for i in range(3)])
    t.start((DOWN, X))

    width = q_ref.shape[1]
    for base in (rows, 0):
        cut = slice(base, base + rows)
        qkv_rows = dot_nn(normed[cut, :], qkv_here[...])
        qkv_rows = qkv_rows + dot_nn(normed_far[cut, :], qkv_far[...])
        for i in range(width // LANES + 1):
            block = qkv_rows[:, LANES * i : LANES * (i + 1)]
            block = turn(block, cosine[cut, :], sine[cut, :])
            if i < width // LANES:
                q_ref[cut, LANES * i : LANES * (i + 1)] = low(block)
            else:
                keys[0, cut, :] = low(block)
                keys[1, cut, :] = swap_heads(low(block))
        block = low(qkv_rows[:, width + LANES :])
        values[0, cut, :] = block
        values[1, cut, :] = swap_heads(block)
    attend_rows(q_ref, keys, values, allowed, mixed, rows, width // LANES)
    t.start((MIXED, X, 1))
    t.arrived((COT, Z, 2))
    t.start((COT, C, 2))
    masks(0)
    attend_rows(q_ref, keys, values, allowed, mixed, 0, width // LANES)
    t.start((MIXED, X, 0))
    t.arrived((DOWN, X))
    t.start((DOWN, Y), (GATE, X))

    def project(base):
        cut = slice(base, base + rows)
        first = pl.ds(pl.multiple_of(place.col * width, LANES), width)
        second = pl.ds(pl.multiple_of((1 - place.col) * width, LANES), width)
        return dot_nn(mixed[cut, :], w_out[first, :]) + dot_nn(mixed_far[cut, :], w_out[second, :])

    def stored(i):
        out = grad_hidden.at[pl.ds(rows * i, rows)]
        return pltpu.make_async_copy(grad_buf.at[i % 2], out, local.at[8 + i % 2])

    def hidden_grads(i):
        k, p = i // 2, i % 2
        if p == 1:
            t.arrived((COT, C, k), (COT, FAR_C, k))
        moves(local, (c_own.at[k, p], own_buf), (c_far.at[k, p], far_buf))
        if i > 1:
            stored(i - 2).wait()
        size = split * LANES
        for n in range(2):
            own_rows = down_own[split * n : split * (n + 1)].reshape(size, part)
            far_rows = down_buf[n].reshape(size, part)
            total = dot_nt(own_buf[...], own_rows) + dot_nt(far_buf[...], far_rows)
            grad_buf[i % 2, :, size * n : size * (n + 1)] = RESIDUAL * total
        stored(i).start()

    t.arrived((MIXED, X, 1))
    give[...] = project(rows)
    t.start((ATTN, C))
    t.arrived((MIXED, X, 0))
    attn = project(0)
    t.arrived((ATTN, C))
    middle = tokens[...].astype(jnp.float32) + RESIDUAL * (attn + got[...])
    middle_ref[...] = middle
    total = jnp.sum(middle * middle, 1, keepdims=True)
    square[...] = jnp.broadcast_to(total, (rows, LANES)).T[:8, :]
    t.start((SQUARE, X))
    t.arrived((DOWN, Y))
    moves(local, (down_got, down_buf.at[0]), (down_other, down_buf.at[1]))
    t.arrived((SQUARE, X))
    t.start((UP, X))
    total = total + jnp.broadcast_to(square_far[:1, :], (LANES, rows)).T[:, :1]
    inv = lax.rsqrt(total / (2 * part) + EPS)
    inv_second[...] = jnp.broadcast_to(inv, inv_second.shape)
    h2_ref[...] = low(middle_ref[...] * inv * gain_moe[...])

    hidden_grads(0)
    hidden_grads(1)
    t.arrived((COT, FAR_Z, 1))
    t.start((COT, FAR_C, 1))
    hidden_grads(2)
    t.arrived((GATE, X))
    t.start((GATE, Y))
    hidden_grads(3)
    t.arrived((COT, FAR_Z, 2))
    t.start((COT, FAR_C, 2))
    t.arrived((COT, Z, 3))
    t.start((COT, C, 3))
    hidden_grads(4)
    hidden_grads(5)
    t.arrived((COT, FAR_Z, 3))
    t.start((COT, FAR_C, 3))
    hidden_grads(6)
    t.arrived((UP, X))
    t.start((UP, Y))
    hidden_grads(7)
    stored(6).wait()
    stored(7).wait()
    t.finish()


def front(tokens, cot, w_down, w_gate, w_up, router, routes, qkv, *others):
    rows, part = tokens.shape
    gain, w_out = others[0], others[2]
    vmem = pl.BlockSpec(memory_space=pltpu.VMEM)
    shape = lambda dims, dtype=jnp.bfloat16: jax.ShapeDtypeStruct(dims, dtype)
    like = lambda a: shape(a.shape, a.dtype)
    stack = lambda a: shape((ZPARTS, 2, *a.shape), a.dtype)
    mine = w_down.shape[0] // 2
    width, kv = qkv[0].shape[1] // 2, qkv[1].shape[1] // 2
    down, pair = shape((mine // 2, LANES, part)), shape((mine // 2, part, LANES))
    hbm_outs = [down, down, pair, pair, pair, pair, like(router)]
    hbm_outs += [stack(cot), stack(cot), stack(routes)]
    hbm_outs += [shape((2 * ZPARTS * rows, mine * LANES), jnp.float32)]
    vmem_outs = [
        shape((2 * rows, width)),
        shape((2, 2 * rows, kv)),
        shape((2, 2 * rows, kv)),
        shape((2 * rows, width)),
        shape((2 * rows, width)),
        shape((2 * rows, part)),
        shape((rows, LANES), jnp.float32),
        shape((rows, part), jnp.float32),
        shape((rows, LANES), jnp.float32),
        shape((rows, part)),
    ]
    buffer = pltpu.VMEM((rows, part), jnp.bfloat16)
    wide = pltpu.VMEM((rows, part), jnp.float32)
    small = pltpu.VMEM((8, rows), jnp.float32)
    weights = pltpu.VMEM((part, width + 2 * kv), jnp.bfloat16)
    count = 12 + 6 * (ZPARTS - 1) + 6 + 2 + 2
    return pl.pallas_call(
        front_kernel,
        out_shape=hbm_outs + vmem_outs,
        in_specs=[vmem] + [ANY] * 9 + [vmem] * len(others),
        out_specs=[ANY] * len(hbm_outs) + [vmem] * len(vmem_outs),
        scratch_shapes=[
            pltpu.VMEM((3, rows, part), jnp.bfloat16),
            weights,
            weights,
            pltpu.VMEM(gain.shape, jnp.float32),
            pltpu.VMEM((2 * rows, part), jnp.bfloat16),
            wide,
            wide,
            small,
            small,
            buffer,
            buffer,
            pltpu.VMEM((mine, LANES, part), jnp.bfloat16),
            pltpu.VMEM((2, mine // 2, LANES, part), jnp.bfloat16),
            pltpu.VMEM((2, rows, mine * LANES), jnp.float32),
            pltpu.VMEM((rows, rows), jnp.float32),
            pltpu.SemaphoreType.DMA((2, count)),
            pltpu.SemaphoreType.DMA((10,)),
        ],
        compiler_params=pltpu.CompilerParams(
            collective_id=0, has_side_effects=True, vmem_limit_bytes=58 * 1024 * 1024
        ),
        name="front",
    )(tokens, cot, w_down, w_gate, w_up, router, routes, *qkv, *others)


def moe_kernel(*refs):
    routes_ref, grad_ref, router_own, router_far, h2 = refs[:5]
    w_gate, w_up, w_down, gate_got, gate_other, up_got, up_other, down_got, down_other = refs[5:14]
    (
        h_own_all,
        h_far_all,
        moe_own,
        moe_far,
        hidden_ref,
        slopes_ref,
        dlog_ref,
        s0_own,
        s0_far,
        z1_own,
        z1_far,
        piece2,
        s3_own,
        s3_far,
    ) = refs[14:28]
    h_own, h_far, keep_own, keep_far, give_own, give_far, got_own, got_far, got_x = refs[28:37]
    pair_own, pair_far, down_own, down_far, sems, local, fill = refs[37:]
    experts = down_own.shape[0]
    split = experts // 2
    rows = h_own.shape[0]
    place = Place()
    step = pl.program_id(0)
    t = Transfers(sems)
    x, c = place.x(), place.c()
    z = [None] + [place.z(k) for k in range(1, ZPARTS)]
    t.add((H, X), h2, h_far_all.at[0, 0], x)
    t.add((H, C, 0), h2, h_own_all.at[0, 1], c)
    t.add((H, FAR_C, 0), h_far_all.at[0, 0], h_far_all.at[0, 1], c)
    for k in range(1, ZPARTS):
        t.add((H, Z, k), h2, h_own_all.at[k, 0], z[k])
        if k == 1:
            t.add((H, FAR_X, 1), h_far_all.at[0, 0], h_far_all.at[1, 0], z[1])
        else:
            t.add((H, FAR_X, k), h_own_all.at[k, 0], h_far_all.at[k, 0], x)
        t.add((H, C, k), h_own_all.at[k, 0], h_own_all.at[k, 1], c)
        t.add((H, FAR_C, k), h_far_all.at[k, 0], h_far_all.at[k, 1], c)
    for k in range(ZPARTS):
        t.add((BACK, C, k), give_own, got_own.at[k], c)
        t.add((BACK, FAR_C, k), give_far, got_far.at[k], c)
    t.add((BACK, Z), got_own.at[1], z1_own, z[1])
    t.add((BACK, FAR_Z), got_far.at[1], z1_far, z[1])
    t.add((BACK, FAR_X), got_far.at[2], got_x, x)

    def join(k):
        for name in ((BACK, C, k), (BACK, FAR_C, k)):
            t.copy(name).wait_send()
        t.arrived((BACK, C, k), (BACK, FAR_C, k))
        for got, keep in ((got_own, keep_own), (got_far, keep_far)):
            total = got[k].astype(jnp.float32) + keep[...].astype(jnp.float32)
            got[k] = total.astype(jnp.bfloat16)

    @pl.when(step == 0)
    def _():
        greet([x, c, *z[1:]])
        t.start((H, X), (H, C, 0), (H, Z, 1), (H, Z, 2))
        cut = functools.partial(weight_slice, which=place.col, split=split, zed=place.zed)
        fills = []
        for i, half in enumerate((place.side, 1 - place.side)):
            gates = (cut(w_gate, half=half, wide=False), (gate_got, gate_other)[i])
            ups = (cut(w_up, half=half, wide=False), (up_got, up_other)[i])
            downs = (cut(w_down, half=half, wide=True), (down_got, down_other)[i])
            for n, (pair, down) in enumerate(((pair_own, down_own), (pair_far, down_far))):
                for e in range(split):
                    for m, src in enumerate((gates[n], ups[n])):
                        cols = pl.ds(LANES * (2 * e + m), LANES)
                        fills.append((src.at[e], pair.at[i, :, cols]))
                fills.append((downs[n], down.at[pl.ds(split * i, split)]))
        moves(fill, (h2, h_own_all.at[0, 0]), *fills)
        t.arrived((H, X))
        t.start((H, FAR_C, 0), (H, FAR_X, 1))

    @pl.when(step == 1)
    def _():
        t.arrived((H, C, 0), (H, FAR_C, 0), (H, Z, 1))
        t.start((H, C, 1))

    @pl.when(step == 2)
    def _():
        t.start((H, Z, 3))
        t.arrived((H, FAR_X, 1))
        t.start((H, FAR_C, 1))
        join(0)
        t.arrived((H, Z, 2))
        t.start((H, FAR_X, 2), (H, C, 2))

    @pl.when(step == 3)
    def _():
        t.arrived((H, C, 1), (H, FAR_C, 1))

    @pl.when(step == 4)
    def _():
        join(1)
        t.start((BACK, Z), (BACK, FAR_Z))
        t.arrived((H, FAR_X, 2))
        t.start((H, FAR_C, 2))
        t.arrived((H, Z, 3))
        t.start((H, FAR_X, 3), (H, C, 3))

    @pl.when(step == 5)
    def _():
        t.arrived((H, C, 2), (H, FAR_C, 2))

    @pl.when(step == 6)
    def _():
        join(2)
        t.start((BACK, FAR_X))
        t.arrived((H, FAR_X, 3))
        t.start((H, FAR_C, 3))

    @pl.when(step == 7)
    def _():
        t.arrived((H, C, 3), (H, FAR_C, 3))
        t.arrived((BACK, FAR_X))
        total = got_own[2].astype(jnp.float32) + got_x[...].astype(jnp.float32)
        got_own[2] = total.astype(jnp.bfloat16)

    for k in range(ZPARTS):
        for p in range(2):

            @pl.when(step == 2 * k + p)
            def _():
                moves(local, (h_own_all.at[k, p], h_own), (h_far_all.at[k, p], h_far))

    first = (place.core * 2 + place.col) * experts
    lane = lax.broadcasted_iota(jnp.int32, (rows, LANES), 1)
    chosen = lane == routes_ref[:, 0:1]
    for k in range(1, routes_ref.shape[1]):
        chosen = chosen | (lane == routes_ref[:, k : k + 1])
    logits = dot_nn(h_own[...], router_own[...]) + dot_nn(h_far[...], router_far[...])
    peak = jnp.max(jnp.where(chosen, logits, -jnp.inf), axis=1, keepdims=True)
    expo = jnp.where(chosen, jnp.exp(logits - peak), 0.0)
    gates = expo / jnp.sum(expo, axis=1, keepdims=True)
    grad_gates = jnp.zeros((rows, LANES), jnp.float32)
    for e in range(experts):
        here = lane == first + (e + place.side * split) % experts
        gate = jnp.sum(jnp.where(here, gates, 0.0), axis=1, keepdims=True)
        cols = slice(2 * LANES * (e % split), 2 * LANES * (e % split + 1))
        pair = dot_nn(h_own[...], pair_own[e // split, :, cols]) + dot_nn(
            h_far[...], pair_far[e // split, :, cols]
        )
        slope = grad_ref[:, LANES * e : LANES * (e + 1)]
        gate_val = pair[:, :LANES]
        up_val = pair[:, LANES:]
        sigma = jax.nn.sigmoid(gate_val)
        silu = gate_val * sigma
        hidden = silu * up_val
        dgate = jnp.sum(hidden * slope, axis=1, keepdims=True)
        grad_gates = jnp.where(here, dgate, grad_gates)
        dz = gate * slope
        hidden_ref[:, LANES * e : LANES * (e + 1)] = (gate * hidden).astype(jnp.bfloat16)
        slopes_ref[:, 2 * LANES * e : 2 * LANES * e + LANES] = (
            dz * up_val * (sigma + silu * (1.0 - sigma))
        ).astype(jnp.bfloat16)
        slopes_ref[:, 2 * LANES * e + LANES : 2 * LANES * (e + 1)] = (dz * silu).astype(
            jnp.bfloat16
        )
    dlog = gates * (grad_gates - jnp.sum(gates * grad_gates, axis=1, keepdims=True))
    dlog_high = dlog.astype(jnp.bfloat16)
    dlog_low = (dlog - dlog_high.astype(jnp.float32)).astype(jnp.bfloat16)
    dlog_ref[:, :LANES] = dlog_high
    dlog_ref[:, LANES:] = dlog_low

    def back(pairs, router):
        total = dot_nt(dlog_high, router[...]) + dot_nt(dlog_low, router[...])
        for i in range(2):
            cols = slice(2 * LANES * split * i, 2 * LANES * split * (i + 1))
            total = total + dot_nt(slopes_ref[:, cols], pairs[i])
        return total.astype(jnp.bfloat16)

    back_own, back_far = back(pair_own, router_own), back(pair_far, router_far)
    last = pl.num_programs(0) - 1

    @pl.when(step % 2 == 0)
    def _():
        keep_own[...] = back_own
        keep_far[...] = back_far

    @pl.when(step % 2 == 1)
    def _():
        give_own[...] = back_own
        give_far[...] = back_far

    for k in range(ZPARTS):

        @pl.when(step == 2 * k + 1)
        def _():
            t.start((BACK, C, k), (BACK, FAR_C, k))

    part = h_own.shape[1]
    moe_own[...] = low(dot_nn(hidden_ref[...], down_own[...].reshape(-1, part)))
    moe_far[...] = low(dot_nn(hidden_ref[...], down_far[...].reshape(-1, part)))

    @pl.when(step == last)
    def _():
        join(ZPARTS - 1)
        moves(
            local,
            (got_own.at[0], s0_own),
            (got_far.at[0], s0_far),
            (got_own.at[2], piece2),
            (got_own.at[3], s3_own),
            (got_far.at[3], s3_far),
        )
        t.finish(*[(BACK, hop, k) for hop in (C, FAR_C) for k in range(ZPARTS)])


def moe_layer(routes, grad_hidden, routers, h2, weights):
    tile, part = h2.shape
    rows = grad_hidden.shape[0]
    experts = grad_hidden.shape[1] // LANES
    by_row = lambda width: pl.BlockSpec((tile, width), lambda i: (i, 0))
    stack = jax.ShapeDtypeStruct((ZPARTS, 2, tile, part), jnp.bfloat16)
    one = jax.ShapeDtypeStruct((tile, part), jnp.bfloat16)
    widths = [part, part, experts * LANES, 2 * experts * LANES, 2 * LANES]
    buffer = pltpu.VMEM((tile, part), jnp.bfloat16)
    stacked = pltpu.VMEM((ZPARTS, tile, part), jnp.bfloat16)
    pair = pltpu.VMEM((2, part, experts * LANES), jnp.bfloat16)
    down = pltpu.VMEM((experts, LANES, part), jnp.bfloat16)
    count = 3 + 4 * (ZPARTS - 1) + 2 * ZPARTS + 3
    return pl.pallas_call(
        moe_kernel,
        out_shape=[stack, stack]
        + [jax.ShapeDtypeStruct((rows, w), jnp.bfloat16) for w in widths]
        + [one] * 7,
        grid=(rows // tile,),
        in_specs=[by_row(routes.shape[1]), by_row(experts * LANES)]
        + [whole_block(r) for r in routers]
        + [ANY] * (1 + len(weights)),
        out_specs=[ANY, ANY] + [by_row(w) for w in widths] + [ANY] * 7,
        scratch_shapes=[buffer] * 6
        + [stacked] * 2
        + [buffer, pair, pair, down, down]
        + [
            pltpu.SemaphoreType.DMA((2, count)),
            pltpu.SemaphoreType.DMA((5,)),
            pltpu.SemaphoreType.DMA((5 + 4 * experts,)),
        ],
        compiler_params=pltpu.CompilerParams(
            collective_id=1, has_side_effects=True, vmem_limit_bytes=60 * 1024 * 1024
        ),
        name="moe_layer",
    )(routes, grad_hidden, *routers, h2, *weights)


def weight_kernel(cargo, n_cargo, *refs):
    h_own, h_far, c_own, c_far, hidden, slopes = refs[:6]
    sources = refs[6 : 6 + n_cargo]
    outs = refs[6 + n_cargo : 10 + n_cargo]
    landed = refs[10 + n_cargo : 10 + 2 * n_cargo]
    sems = refs[-1]
    place = Place()
    step = pl.program_id(0)
    t = Transfers(sems)
    partners = {X: place.x(), Y: place.y(), C: place.c()}
    partners.update({(Z, k): place.z(k) for k in range(1, ZPARTS)})
    to = {name: partners[name] for name in cargo}
    for i, name in enumerate(cargo):
        t.add(i, sources[i], landed[i], to[name])

    @pl.when(step == 0)
    def _():
        greet(list(to.values()))
        t.start(*t.table)

    half = LANES // 2
    tile = h_own.shape[2]
    first = place.side == 0
    for keep, give, rows_h, rows_c in (
        (outs[0], outs[2], h_own, c_own),
        (outs[1], outs[3], h_far, c_far),
    ):
        pair, down = 0.0, 0.0
        for i in range(2 * ZPARTS):
            rows = slice(tile * i, tile * (i + 1))
            pair = pair + dot_tn(slopes[rows, :], rows_h[i // 2, i % 2])
            down = down + dot_tn(hidden[rows, :], rows_c[i // 2, i % 2])
        for i, block in enumerate((pair[:LANES], pair[LANES:], RESIDUAL * down)):
            low, high = block[:half], block[half:]
            keep[0, half * i : half * (i + 1), :] = jnp.where(first, low, high)
            give[0, half * i : half * (i + 1), :] = jnp.where(first, high, low).astype(
                jnp.bfloat16
            )

    @pl.when(step == pl.num_programs(0) - 1)
    def _():
        t.finish()


def weight_grads(number, start, count, resident, hidden, slopes, cargo):
    part = resident[0].shape[-1]
    rows = hidden.shape[0]
    out = pl.BlockSpec((1, 3 * LANES // 2, part), lambda e: (e, 0, 0))
    shape = (count, 3 * LANES // 2, part)
    names = tuple(name for name, _ in cargo)
    arrays = [array for _, array in cargo]
    return pl.pallas_call(
        functools.partial(weight_kernel, names, len(names)),
        out_shape=[jax.ShapeDtypeStruct(shape, jnp.float32)] * 2
        + [jax.ShapeDtypeStruct(shape, jnp.bfloat16)] * 2
        + [jax.ShapeDtypeStruct(a.shape, a.dtype) for a in arrays],
        grid=(count,),
        in_specs=[whole_block(a) for a in resident]
        + [
            pl.BlockSpec((rows, LANES), lambda e: (0, e + start)),
            pl.BlockSpec((rows, 2 * LANES), lambda e: (0, e + start)),
        ]
        + [ANY] * len(arrays),
        out_specs=[out] * 4 + [ANY] * len(arrays),
        scratch_shapes=[pltpu.SemaphoreType.DMA((2, len(names)))],
        compiler_params=pltpu.CompilerParams(
            collective_id=2 + number, has_side_effects=True, vmem_limit_bytes=60 * 1024 * 1024
        ),
        name="expert_weight_grads",
    )(*resident, hidden, slopes, *arrays)


def unturn(block, cosine, sine):
    return block * cosine + turn(block, jnp.zeros_like(cosine), -sine)


def attend_back_rows(
    q_ref, keys_ref, values_ref, grad_ref, allowed_ref, out_ref, dk, dv, cosine, sine, base, blocks
):
    rows = allowed_ref.shape[0]
    dk[...] = jnp.zeros_like(dk)
    dv[...] = jnp.zeros_like(dv)

    def body(j, carry):
        cols = pl.ds(pl.multiple_of(j * LANES, LANES), LANES)
        for start, stop, keys in score_tiles(rows):
            cut = slice(base + start, base + stop)
            lane = lax.broadcasted_iota(jnp.int32, (stop - start, LANES), 1)
            query, grad = q_ref[cut, cols], grad_ref[cut, cols]
            allowed = allowed_ref[:keys, start:stop] > 0
            dqs = []
            for side, part in enumerate((lane < HEAD_WIDTH, lane >= HEAD_WIDTH)):
                other = (2 * j + side) // blocks
                other = other + side - 2 * other * side
                key_rows = keys_ref[other, base : base + keys, :]
                value_rows = values_ref[other, base : base + keys, :]
                one_query = jnp.where(part, query, jnp.zeros_like(query))
                one_grad = jnp.where(part, grad, jnp.zeros_like(grad))
                scores = jnp.where(allowed, dot_nt(key_rows, one_query) * SCORE_SCALE, NEG)
                expo = jnp.exp(scores - jnp.max(scores, axis=0, keepdims=True))
                probs = expo * (1.0 / jnp.sum(expo, axis=0, keepdims=True))
                slope = dot_nt(value_rows, one_grad)
                delta = jnp.sum(probs * slope, axis=0, keepdims=True)
                dscore = low(probs * (slope - delta))
                dv[other, :keys, :] = dv[other, :keys, :] + dot_nn(low(probs), one_grad)
                dk[other, :keys, :] = dk[other, :keys, :] + dot_nn(dscore, one_query)
                dqs.append(dot_tn(dscore, key_rows))
            dq = jnp.where(lane < HEAD_WIDTH, dqs[0], dqs[1]) * SCORE_SCALE
            out_ref[cut, cols] = low(unturn(dq, cosine[cut, :], sine[cut, :]))
        return carry

    lax.fori_loop(0, blocks, body, 0)
    cut = slice(base, base + rows)
    width = blocks * LANES
    total = (dk[0] + pltpu.roll(dk[1], HEAD_WIDTH, 1)) * SCORE_SCALE
    out_ref[cut, width : width + LANES] = low(unturn(total, cosine[cut, :], sine[cut, :]))
    out_ref[cut, width + LANES :] = low(dv[0] + pltpu.roll(dv[1], HEAD_WIDTH, 1))


class WholeSum:
    def __init__(self, t, name, ref, levels, stages, lands):
        self.t, self.name, self.ref = t, name, ref
        self.stages, self.lands, self.count = stages, lands, len(levels)
        offset, rows = 0, ref.shape[0]
        self.kept, self.other = [], []
        for i, (partner, bit) in enumerate(levels):
            rows = rows // 2
            self.other.append((offset + (1 - bit) * rows, rows))
            offset = offset + bit * rows
            self.kept.append((offset, rows))
            t.add((SUM, name, i), stages[i], lands[i], partner)
            t.add((SUM, name, 2 * self.count - 1 - i), stages[i], lands[self.count + i], partner)

    def rows(self, place):
        return pl.ds(pl.multiple_of(place[0], 8), place[1])

    def send(self, i):
        j = min(i, 2 * self.count - 1 - i)
        if i >= self.count:
            self.t.sent((SUM, self.name, j))
        place = (self.other if i < self.count else self.kept)[j]
        self.stages[j][...] = low(self.ref[self.rows(place), :])
        self.t.start((SUM, self.name, i))

    def land(self, i):
        self.t.arrived((SUM, self.name, i))
        if i < self.count:
            cut = self.rows(self.kept[i])
            total = self.ref[cut, :] + self.lands[i][...].astype(jnp.float32)
            self.ref[cut, :] = low(total).astype(jnp.float32) if i == self.count - 1 else total
        else:
            j = 2 * self.count - 1 - i
            cut = self.rows(self.other[j])
            self.ref[cut, :] = self.lands[self.count + j][...].astype(jnp.float32)

    def next(self, i):
        self.land(i)
        if i + 1 < 2 * self.count:
            self.send(i + 1)

    def keys(self):
        return [(SUM, self.name, i) for i in range(self.count)]


class SmallSum:
    def __init__(self, t, name, ref, partners, lands):
        self.t, self.name, self.ref, self.lands = t, name, ref, lands
        for i, partner in enumerate(partners):
            t.add((SMALL, name, i), ref, lands.at[i], partner)

    def send(self, i):
        self.t.start((SMALL, self.name, i))

    def land(self, i):
        self.t.sent((SMALL, self.name, i))
        self.t.arrived((SMALL, self.name, i))
        self.ref[...] = self.ref[...] + self.lands[i]

    def next(self, i):
        self.land(i)
        if i + 1 < self.lands.shape[0]:
            self.send(i + 1)

    def keys(self):
        return [(SMALL, self.name, i) for i in range(self.lands.shape[0])]


SUMMED = 40


def back_kernel(count, with_grads, *refs):
    refs = list(refs)
    take = lambda n: [refs.pop(0) for _ in range(n)]
    qkv = take(3)
    moe_srcs = take(4)
    tokens, cot, middle, inv_first, inv_second, gain, gain_moe = take(7)
    parts = take(5)
    q_ref, keys, values, mixed, mixed_far, normed, cosine, sine, seg_row, seg_col = take(10)
    w_out, out_far, small_own, small_there = take(4)
    if with_grads:
        grad_srcs, keep_first = take(4), take(1)[0]
    moe_lands = take(4)
    if with_grads:
        grad_lands = take(4)
    grad_tokens, grad_q, grad_k, grad_v, grad_out, small, small_last = take(7)
    qkv_here, qkv_there, da_own, da_far, grad_mixed, dqkv, dqkv_far, give, got = take(9)
    grad_middle, grad_here, grad_there, allowed, dk, dv, square, square_far = take(8)
    small_land, small_lands, last_lands = take(3)
    stages, lands = [], []
    for _ in range(3):
        stages.append(take(count))
        lands.append(take(2 * count))
    if with_grads:
        first_land, first_sum = take(2)
    sems, local = take(2)
    place = Place()
    t = Transfers(sems)
    x, c, y = place.x(), place.c(), place.y()
    rows, part = tokens.shape
    width = q_ref.shape[1]
    low_levels, high_levels = place.bits()
    partners = [partner for partner, _ in low_levels + high_levels]
    t.add((INNER, 0), square.at[0], square_far.at[0], x)
    t.add((INNER, 1), square.at[1], square_far.at[1], x)
    t.add((SMALL, X), small_there, small_land, x)
    first, second = pl.ds(0, rows), pl.ds(rows, rows)
    t.add((DA, X), da_own.at[first], da_far.at[first], x)
    t.add((DA, C), da_own.at[first], da_own.at[second], c)
    t.add((DA, FAR_C), da_far.at[first], da_far.at[second], c)
    for i, cut in enumerate((first, second)):
        t.add((DQKV, i), dqkv.at[cut], dqkv_far.at[cut], x)
    t.add((ATTN, C), give, got, c)
    for i, partner in enumerate((place.z(1), place.z(2), place.z(3), x)):
        t.add((MOE, i), moe_srcs[i], moe_lands[i], partner)
    if with_grads:
        t.add((GRADS, Y, 0), grad_srcs[0], first_land, y)
        t.add((GRADS, Y, 1), grad_srcs[1], grad_lands[0], y)
        t.add((GRADS, Y, 2), grad_srcs[2], grad_lands[1], y)
        t.add((GRADS, X, 0), grad_srcs[3], grad_lands[2], x)
        t.add((GRADS, X, 1), first_sum, grad_lands[3], x)
    sum_out = WholeSum(t, 0, grad_out, high_levels + low_levels, stages[0], lands[0])
    sum_here = WholeSum(t, 1, grad_here, low_levels + high_levels, stages[1], lands[1])
    sum_there = WholeSum(t, 2, grad_there, high_levels + low_levels, stages[2], lands[2])
    small_sum = SmallSum(t, 0, small, [c] + partners, small_lands)
    last_sum = SmallSum(t, 1, small_last, [c] + partners, last_lands)

    greet([x, c, place.z(3)] + partners)
    t.start((SMALL, X), (MOE, 1), (MOE, 2))
    if with_grads:
        t.start((GRADS, Y, 0))
    here, there = qkv_slices(qkv, place.col), qkv_slices(qkv, 1 - place.col)
    targets = [*qkv_targets(qkv_here, qkv), *qkv_targets(qkv_there, qkv)]
    moves(local, *zip([*here, *there], targets))

    def masks(b):
        allowed[...] = allowed_tile(seg_row[b : b + 1, :], seg_col[:, b : b + 1], True)

    def exchange_sum(i, total):
        square[i] = jnp.broadcast_to(total, (rows, LANES)).T[:8, :]
        t.start((INNER, i))

    def exchanged(i, total):
        t.arrived((INNER, i))
        return total + jnp.broadcast_to(square_far[i, :1, :], (LANES, rows)).T[:, :1]

    def norm_back(grad, value, inv, gain_row, inner):
        return inv * (grad * gain_row) - value * (inv * inv * inv * inner / (2 * part))

    grad = add_wide(*[p[...] for p in parts])
    inv = inv_second[:, :1]
    inner = jnp.sum(middle[...] * grad * gain_moe[...], 1, keepdims=True)
    exchange_sum(0, inner)
    small[...] = small_own[...]
    small[SUMMED : SUMMED + 1, :] = jnp.sum(grad * middle[...] * inv, 0, keepdims=True)
    inner = exchanged(0, inner)
    total = cot[...].astype(jnp.float32)
    total = total + norm_back(grad, middle[...], inv, gain_moe[...], inner)
    grad_middle[...] = total
    da_own[:rows, :] = low(RESIDUAL * total)
    t.start((DA, X), (DA, C))
    masks(1)
    t.arrived((SMALL, X))
    small[...] = small[...] + small_land[...]
    small_sum.send(0)
    t.arrived((DA, C))
    at_here = pl.ds(pl.multiple_of(place.col * width, LANES), width)
    at_there = pl.ds(pl.multiple_of((1 - place.col) * width, LANES), width)
    grad_out[at_here, :] = dot_tn(mixed[...], da_own[...])
    grad_out[at_there, :] = dot_tn(mixed_far[...], da_own[...])
    sum_out.send(0)
    small_sum.next(0)
    t.arrived((DA, X))
    t.start((DA, FAR_C))
    if with_grads:
        t.start((GRADS, X, 0))

    def mixed_back(cut):
        total = dot_nt(da_own[cut, :], w_out[at_here, :]) + dot_nt(da_far[cut, :], out_far[...])
        grad_mixed[cut, :] = low(total)

    mixed_back(slice(0, rows))
    t.arrived((DA, FAR_C))
    mixed_back(slice(rows, 2 * rows))
    attend = functools.partial(
        attend_back_rows, q_ref, keys, values, grad_mixed, allowed, dqkv, dk, dv, cosine, sine
    )
    attend(rows, width // LANES)
    t.start((DQKV, 1))
    sum_out.next(0)
    small_sum.next(1)
    if with_grads:
        t.arrived((GRADS, Y, 0))
        t.start((GRADS, Y, 1))
        first_sum[...] = low(keep_first[...] + first_land[...].astype(jnp.float32))
    t.start((MOE, 0))
    masks(0)
    attend(0, width // LANES)
    t.start((DQKV, 0))
    sum_out.next(1)
    grad_here[...] = dot_tn(normed[...], dqkv[...])
    sum_here.send(0)
    t.arrived((DQKV, 1))

    def tokens_back(cut):
        return dot_nt(dqkv[cut, :], qkv_here[...]) + dot_nt(dqkv_far[cut, :], qkv_there[...])

    give[...] = tokens_back(slice(rows, 2 * rows))
    t.start((ATTN, C))
    if with_grads:
        t.start((GRADS, Y, 2))
    sum_out.next(2)
    small_sum.next(2)
    t.arrived((DQKV, 0))
    t.start((MOE, 3))
    if with_grads:
        t.start((GRADS, X, 1))
    grad_there[...] = dot_tn(normed[...], dqkv_far[...])
    sum_there.send(0)
    grad = tokens_back(slice(0, rows))
    t.arrived((ATTN, C))
    grad = grad + got[...]
    got[...] = grad
    value = tokens[...].astype(jnp.float32)
    inv = inv_first[:, :1]
    inner = jnp.sum(value * grad * gain[...], 1, keepdims=True)
    exchange_sum(1, inner)
    small_last[...] = jnp.zeros_like(small_last)
    small_last[0:1, :] = jnp.sum(grad * value * inv, 0, keepdims=True)
    last_sum.send(0)
    sum_here.next(0)
    sum_out.next(3)
    inner = exchanged(1, inner)
    grad = norm_back(got[...], tokens[...].astype(jnp.float32), inv, gain[...], inner)
    grad_tokens[...] = grad_middle[...] + grad
    last_sum.next(0)
    for i in range(2 * count):
        if i + 4 < 2 * count:
            sum_out.next(i + 4)
        if i + 1 < 2 * count:
            sum_here.next(i + 1)
        sum_there.next(i)
        if i + 3 < small_lands.shape[0]:
            small_sum.next(i + 3)
        if i + 1 < last_lands.shape[0]:
            last_sum.next(i + 1)
    start = 0
    for out in (grad_q, grad_k, grad_v):
        size = out.shape[1] // 2
        cut = slice(start, start + size)
        out[:, pl.ds(pl.multiple_of(place.col * size, LANES), size)] = grad_here[:, cut]
        out[:, pl.ds(pl.multiple_of((1 - place.col) * size, LANES), size)] = grad_there[:, cut]
        start += size
    done = [key for each in (sum_out, sum_here, sum_there, small_sum, last_sum) for key in each.keys()]
    t.finish(*done)


def back(levels, qkv, moe_srcs, vmem_ins, grads):
    tokens, middle, q = vmem_ins[0], vmem_ins[2], vmem_ins[12]
    w_out, small_own = vmem_ins[22], vmem_ins[24]
    rows, part = tokens.shape
    width, kv = q.shape[1], qkv[1].shape[1] // 2
    both = width + 2 * kv
    vmem = pl.BlockSpec(memory_space=pltpu.VMEM)
    bf16, f32 = jnp.bfloat16, jnp.float32
    shape = jax.ShapeDtypeStruct
    like = lambda a: shape(a.shape, a.dtype)
    hbm_outs = [like(a) for a in moe_srcs]
    extra_ins, extra_specs, extra_scratch = [], [], []
    if grads:
        extra_ins = list(grads)
        extra_specs = [ANY] * 4 + [vmem]
        hbm_outs += [like(a) for a in grads[:4]]
        extra_scratch = [pltpu.VMEM(grads[0].shape, bf16)] * 2
    small_last = shape((8, part), f32)
    vmem_outs = [shape((rows, part), f32)]
    vmem_outs += [shape((part, w.shape[1]), f32) for w in qkv]
    vmem_outs += [shape(w_out.shape, f32), like(small_own), small_last]
    twice = lambda w, dtype=bf16: pltpu.VMEM((2 * rows, w), dtype)
    wide = pltpu.VMEM((rows, part), f32)
    pair = pltpu.VMEM((2, rows, LANES), f32)
    flat = pltpu.VMEM((2, 8, rows), f32)
    scratch = [pltpu.VMEM((part, both), bf16)] * 2
    scratch += [twice(part), twice(part), twice(width), twice(both), twice(both), wide, wide]
    scratch += [wide, pltpu.VMEM((part, both), f32), pltpu.VMEM((part, both), f32)]
    scratch += [pltpu.VMEM((rows, rows), f32), pair, pair, flat, flat]
    scratch += [pltpu.VMEM(small_own.shape, f32)]
    scratch += [pltpu.VMEM((levels + 1, *small_own.shape), f32)]
    scratch += [pltpu.VMEM((levels + 1, 8, part), f32)]
    for high, wide_cols in ((w_out.shape[0], part), (part, both), (part, both)):
        sizes = [pltpu.VMEM((high >> (i + 1), wide_cols), bf16) for i in range(levels)]
        scratch += sizes * 3
    scratch += extra_scratch
    count = 9 + 4 + 5 + 3 * 2 * levels + 2 * (levels + 1)
    scratch += [pltpu.SemaphoreType.DMA((2, count)), pltpu.SemaphoreType.DMA((6,))]
    return pl.pallas_call(
        functools.partial(back_kernel, levels, bool(grads)),
        out_shape=hbm_outs + vmem_outs,
        in_specs=[ANY] * (len(qkv) + len(moe_srcs)) + [vmem] * len(vmem_ins) + extra_specs,
        out_specs=[ANY] * len(hbm_outs) + [vmem] * len(vmem_outs),
        scratch_shapes=scratch,
        compiler_params=pltpu.CompilerParams(
            collective_id=4, has_side_effects=True, vmem_limit_bytes=62 * 1024 * 1024
        ),
        name="back",
    )(*qkv, *moe_srcs, *vmem_ins, *extra_ins)


def halve(value, index, mask, axis):
    first, last = jnp.split(value, 2, axis)
    upper = (index & mask) != 0
    send = low(jnp.where(upper, first, last))
    return jnp.where(upper, last, first) + flip(send, "dp", mask).astype(jnp.float32)


def on_device(
    tokens,
    gain_attn,
    w_query,
    key_matrix,
    value_matrix,
    w_out,
    gain_moe,
    w_router,
    w_gate,
    w_up,
    w_down,
    segments,
    routes,
    cotangent,
):
    col = lax.axis_index("col")
    core = lax.axis_index("expert")
    group = lax.axis_index("dp")
    dp_size = lax.axis_size("dp")
    step = dp_size // ZPARTS
    member = group % step
    levels = dp_size.bit_length() - 1
    half_mask = step // 2
    side = (member // half_mask) % 2

    local, part, ffn = w_gate.shape
    split = local // 4
    units = ffn // ZPARTS
    experts = local * lax.axis_size("expert")
    rows = tokens.shape[0]
    width = w_query.shape[1] // 2

    router_own = jnp.pad(w_router, ((0, 0), (0, LANES - experts)))
    seg_rows = jnp.where(core == 0, segments, segments[::-1])
    positions = jax.vmap(doc_positions)(seg_rows).reshape(-1, 1).astype(jnp.float32)
    half = HEAD_WIDTH // 2
    slot = jnp.arange(LANES, dtype=jnp.int32)
    freq = jnp.exp((slot % half).astype(jnp.float32) * (-2.0 * math.log(THETA) / HEAD_WIDTH))
    sign = jnp.where(slot % HEAD_WIDTH < half, -1.0, 1.0)
    cosine, sine = jnp.cos(positions * freq), jnp.sin(positions * freq) * sign
    qkv = [w_query, key_matrix, value_matrix]
    gain, gain_second = gain_attn[None], gain_moe[None]
    (
        down_got,
        down_other,
        gate_got,
        gate_other,
        up_got,
        up_other,
        router_far,
        c_own,
        c_far,
        route_all,
        grad_hidden,
        q,
        keys,
        values,
        mixed,
        mixed_far,
        normed,
        inv_first,
        middle,
        inv_second,
        h2,
    ) = front(
        tokens,
        cotangent,
        w_down,
        w_gate,
        w_up,
        router_own,
        routes.T,
        qkv,
        gain,
        gain_second,
        w_out,
        cosine,
        sine,
        seg_rows,
        seg_rows.T,
    )
    route_rows = jnp.swapaxes(route_all, 2, 3).reshape(2 * ZPARTS * rows, -1)
    (
        h_own,
        h_far,
        moe_own,
        moe_far,
        hidden,
        slopes,
        dlog,
        s0_own,
        s0_far,
        z1_own,
        z1_far,
        piece2,
        s3_own,
        s3_far,
    ) = moe_layer(
        route_rows,
        grad_hidden,
        [router_own, router_far],
        h2,
        [w_gate, w_up, w_down, gate_got, gate_other, up_got, up_other, down_got, down_other],
    )
    resident = [h_own, h_far, c_own, c_far]
    out_there = lax.dynamic_slice_in_dim(w_out, (1 - col) * width, width, 0)
    moe_own, moe_far = (a.reshape(ZPARTS, 2, rows, part) for a in (moe_own, moe_far))
    cargo = [
        ((Z, 2), piece2),
        (X, s3_far),
        (X, low(add_wide(s0_far, z1_far))),
        (X, out_there),
        (C, moe_own[:, 1]),
        (C, moe_far[:, 1]),
    ]
    *first_part, z2_piece, x3_far, x0_far, out_far, sib_own, sib_far = weight_grads(
        0, 0, split, resident, hidden, slopes, cargo
    )
    moe_own = low(add_wide(moe_own[:, 0], sib_own))
    moe_far = low(add_wide(moe_far[:, 0], sib_far))
    cargo = [
        ((Z, 3), low(add_wide(s3_own, x3_far))),
        (Y, first_part[3]),
        (X, moe_far[2:]),
        ((Z, 1), moe_far[1]),
    ]
    *second_part, z3_piece, y_far, moe_x, moe_z1_far = weight_grads(
        1, split, split, resident, hidden, slopes, cargo
    )
    moe_srcs = [
        moe_own[1],
        low(add_wide(moe_own[2], moe_x[0])),
        low(add_wide(moe_own[3], moe_x[1])),
        low(add_wide(moe_far[0], moe_z1_far)),
    ]

    def router_term(h_rows):
        total = dot_tn(dlog, h_rows.reshape(-1, part))
        total = total[:experts] + total[LANES : LANES + experts]
        return jnp.pad(total, ((0, 8), (0, 0)))

    vmem_ins = [
        tokens,
        cotangent,
        middle,
        inv_first,
        inv_second,
        gain,
        gain_second,
        s0_own,
        z1_own,
        z2_piece,
        x0_far,
        z3_piece,
        q,
        keys,
        values,
        mixed,
        mixed_far,
        normed,
        cosine,
        sine,
        seg_rows,
        seg_rows.T,
        w_out,
        out_far,
        router_term(h_own),
        router_term(h_far),
    ]
    swap = lambda a: flip(a, "dp", half_mask)
    plain = half_mask == 1
    grads = []
    if plain:
        second_far = low(add_wide(second_part[1], y_far))
        grads = [second_part[3], first_part[2], second_part[2], second_far, first_part[1]]
    outs = back(levels, qkv, moe_srcs, vmem_ins, grads)
    moe_parts, outs = outs[:4], outs[4:]
    if plain:
        (got_second, got_first, far_second, far_first), outs = outs[:4], outs[4:]
        own_first, own_second = add_wide(first_part[0], got_first), add_wide(
            second_part[0], got_second
        )
    else:

        def finish_grads(kept, got_own, got_far):
            shape = (split, 3, units // 2, part)
            keep_own = add_wide(kept[0], got_own).reshape(shape)
            keep_far = add_wide(kept[1], got_far).reshape(shape)
            mask = half_mask // 2
            while mask:
                keep_own = halve(keep_own, member, mask, 2)
                keep_far = halve(keep_far, member, mask, 2)
                mask //= 2
            return keep_own, flip(low(keep_far), "col")

        own_second, far_second = finish_grads(second_part, swap(first_part[2]), y_far)
        own_first, far_first = finish_grads(
            first_part, swap(second_part[2]), swap(second_part[3])
        )
    grad_tokens, grad_query, grad_key, grad_value, grad_out, small, small_last = outs

    def in_order(a, b, index):
        a, b = a.astype(jnp.float32), b.astype(jnp.float32)
        return jnp.concatenate([jnp.where(index == 0, a, b), jnp.where(index == 0, b, a)], 0)

    expert_grads = in_order(
        in_order(own_first, own_second, side), in_order(far_first, far_second, side), col
    )
    expert_grads = expert_grads.reshape(local, 3, -1, part)
    output = middle + RESIDUAL * add_wide(moe_own[0], *moe_parts)
    return (
        output,
        grad_tokens,
        small_last[0],
        grad_query,
        grad_key,
        grad_value,
        grad_out,
        small[SUMMED],
        small[:experts].T,
        jnp.swapaxes(expert_grads[:, 0], 1, 2),
        jnp.swapaxes(expert_grads[:, 1], 1, 2),
        expert_grads[:, 2],
    )


def solution(mesh):
    in_specs = (
        P(("dp", "expert"), "col"),
        P("col"),
        P("col", "expert"),
        P("col", "expert"),
        P("col", "expert"),
        P("expert", "col"),
        P("col"),
        P("col", None),
        P("expert", "col", None),
        P("expert", "col", None),
        P("expert", None, "col"),
        P("dp", None),
        P(("dp", "expert"), None),
        P(("dp", "expert"), "col"),
    )
    out_specs = (
        P(("dp", "expert"), "col"),
        P(("dp", "expert"), "col"),
        P("col"),
        P("col", "expert"),
        P("col", "expert"),
        P("col", "expert"),
        P("expert", "col"),
        P("col"),
        P("col", None),
        P("expert", "col", "dp"),
        P("expert", "col", "dp"),
        P("expert", "dp", "col"),
    )
    return jax.shard_map(
        on_device, mesh=mesh, in_specs=in_specs, out_specs=out_specs, check_vma=False
    )
```

time: 3470 us -> 773 us (0.22)
  waiting for transfers between devices: 2620 us -> 0 us
  Pallas kernels: 0 us -> 691 us
  local copies, waits for them, and re-layouts: 335 us -> 30.4 us
  matrix products: 209 us -> 6.6 us
  blocking collectives: 144 us -> 0 us
  other arithmetic: 129 us -> 37.3 us
    reduce_scatter x9 -> x0, waiting for transfers between devices: 2200 us -> none  [the longest x1 603 us: spread_expert_grads(): lax.psum_scatter(grad_gate, 'dp', scatter_dimension=2, tiled=True)]
    pallas_call x0 -> x5, Pallas kernels: none -> 691 us  [the longest x1 217 us: back(): pl.pallas_call(functools.partial(back_kernel, levels, bool(grads)), out_s...]
    all_gather x6 -> x0, waiting for transfers between devices: 277 us -> none  [the longest x2 196 us: share_gather(): return lax.all_gather(value_rows, 'col', axis=0, tiled=True)]
    dot_general x21 -> x2, matrix products: 209 us -> 6.6 us  [dot_tn(): lax.dot_general(a, b, (((0,), (0,)), ((), ())), preferred_element_type=jn...]
    psum x3 -> x0, waiting for transfers between devices: 136 us -> none  [the longest x1 84.3 us: on_device(): lax.psum((grad_gain_attn, grad_gain_moe, grad_router), ('dp', 'expert'))]
    slice x14 -> x4, local copies, waits for them, and re-layouts: 126 us -> 3.41 us  [the longest x1 1.34 us: on_device(): small_last[0]]
    gather x7 -> x0, local copies, waits for them, and re-layouts: 102 us -> none  [the longest x5 52.3 us: on_device(): gates = jax.nn.softmax(jnp.take_along_axis(logits, routes, 1), axis=-1)]
    all_to_all x4 -> x0, blocking collectives: 77.2 us -> none  [the longest x2 47.6 us: to_experts(): lax.all_to_all(buffer, 'expert', split_axis=0, concat_axis=0, tiled=True)]
  transfers between devices with their start and end apart: 18 -> 0, of which waited for: 17 -> 0; matrix products, arithmetic and copies ran while one was open for 11% -> 0% of each run, Pallas kernels for 0% -> 0%
where the time goes in v2:
time: 773 us; the launch traced here: 766 us
  Pallas kernels  691 us (89%)
  other arithmetic  37.3 us (5%)
  local copies, waits for them, and re-layouts  30.4 us (4%)
    pallas_call x1, Pallas kernels, back(): pl.pallas_call(functools.partial(back_kernel, levels, bool(grads)), out_s...  217 us
    pallas_call x1, Pallas kernels, front(): pl.pallas_call(front_kernel, out_shape=hbm_outs + vmem_outs, in_specs=[vm...  189 us
    pallas_call x1, Pallas kernels, moe_layer(): pl.pallas_call(moe_kernel, out_shape=[stack, stack] + [jax.ShapeDtypeStru...  177 us
    pallas_call x2, Pallas kernels, weight_grads(): pl.pallas_call(functools.partial(weight_kernel, names, len(names)), out_s...  108 us

profile of v2, /device:TPU:0, one launch (start us, length us, event | category | flops | bytes accessed | tf_op | source)
XLA Modules:
  0.0 766.4 jit_solution(3524630918650209452)
XLA Ops:
  3.3 3.1 fusion.17
  9.1 189.1 %front.1 = (bf16[5,128,768]{2,1,0:T(8,128)(2,1)}, bf16[5,128,768]{2,1,0:T(8,128)(2,1)}, bf16[5,768,128]{2,1,0:T(8,128)(2,1)}, bf16[5,768,128]{2,1,0:T(8,128)(2,1...) custom-call(bf16[512,768]{1,0:T(8,128)(2,1)} %refs_7_.5, ...), custom_call_target="tpu_custom_call" | custom-call | tf_op jit(solution)/shard_map/front/pallas_call | solution.py:487
  198.2 2.8 copy.42
  201.1 176.6 %moe_layer.1 = (bf16[4,2,512,768]{3,2,1,0:T(8,128)(2,1)}, bf16[4,2,512,768]{3,2,1,0:T(8,128)(2,1)}, bf16[4096,768]{1,0:T(8,128)(2,1)}, bf16[4096,768]{1,0:T(8,12...) custom-call(s32[4096,8]{1,0:T(8,128)} %bitcast.86, ...), custom_call_target="tpu_custom_call" | custom-call | tf_op jit(solution)/shard_map/moe_layer/pallas_call | solution.py:741
  377.7 3.9 slice_bitcast_fusion.1.refs_11_
  382.6 1.9 slice_bitcast_fusion.2.refs_10_
  386.5 60.2 %expert_weight_grads.2 = (f32[5,192,768]{2,1,0:T(8,128)}, f32[5,192,768]{2,1,0:T(8,128)}, bf16[5,192,768]{2,1,0:T(8,128)(2,1)}, bf16[5,192,768]{2,1,0:T(8,128)(2...) custom-call(bf16[4,2,512,768]{3,2,1,0:T(8,128)(2,1)} %get-tuple-elem, ...), custom_call_target="tpu_custom_call" | custom-call | tf_op jit(solution)/shard_map/expert_weight_grads/pallas_call | solution.py:817
  446.7 3.6 fusion
  450.3 1.2 slice.113.refs_8_
  453.5 48.1 %expert_weight_grads.3 = (f32[5,192,768]{2,1,0:T(8,128)}, f32[5,192,768]{2,1,0:T(8,128)}, bf16[5,192,768]{2,1,0:T(8,128)(2,1)}, bf16[5,192,768]{2,1,0:T(8,128)(2...) custom-call(bf16[4,2,512,768]{3,2,1,0:T(8,128)(2,1)} %get-tuple-elem, ...), custom_call_target="tpu_custom_call" | custom-call | tf_op jit(solution)/shard_map/expert_weight_grads/pallas_call | solution.py:817
  501.7 3.8 add_convert_fusion.refs_36_
  505.5 4.8 fusion.22
  511.0 1.8 fusion.21
  516.7 1.8 fusion.16
  519.5 216.7 %back.1 = (bf16[512,768]{1,0:T(8,128)(2,1)}, bf16[512,768]{1,0:T(8,128)(2,1)}, bf16[512,768]{1,0:T(8,128)(2,1)}, bf16[512,768]{1,0:T(8,128)(2,1)}, bf16[5,192,76...) custom-call(bf16[768,768]{1,0:T(8,128)(2,1)} %refs_0_.3, ...), custom_call_target="tpu_custom_call" | custom-call | tf_op jit(solution)/shard_map/back/pallas_call | solution.py:1180
  736.3 4.1 convert_select_fusion.1
  741.8 3.2 fusion.8
  745.0 4.3 copy_select_fusion
  749.4 5.2 fusion.6
  754.7 3.0 fusion.14
  758.9 1.3 slice_reduce_fusion.2
  760.2 1.1 copy.68
  761.4 1.4 copy.69
  764.8 1.4 copy.72
  (103 shorter events, 20.4 us)
Async XLA Ops:
  0.6 6.4 copy-start.27
  0.7 7.3 copy-start.28
  0.7 7.9 %copy-start.29 = (f32[768]{0:T(1024)S(1)}, f32[768]{0:T(1024)}, u32[]{:S(2)}) copy-start(f32[768]{0:T(1024)} %param.20) | copy-start | bytes 9220
  1.9 7.2 copy-start.2
  377.7 4.9 copy-start.5
  382.6 3.0 copy-start.3
  501.7 3.9 copy-start
  501.7 9.3 %slice-start = ((s8[6291456]{0:T(1024)(128)(4,1)}), s8[2097152]{0:T(1024)(128)(4,1)S(1)}, s32[]{:S(2)}) async-start(s8[6291456]{0:T(1024)(128)(4,1)} %bitcast.75), calls=%async_computation | async-start | bytes 4194304
  505.5 5.5 slice-start.1
  511.0 3.7 slice-start.2
  511.0 3.7 slice-start.3
  511.0 4.3 copy-start.6
  736.3 4.2 copy-start.7
  736.3 4.2 copy-start.8
  736.3 5.1 copy-start.13
  736.3 5.5 copy-start.14
  749.3 5.3 copy-start.4
  749.3 5.3 copy-start.15
  749.3 5.3 copy-start.16
  749.4 5.3 copy-start.17
  749.4 5.3 copy-start.18
  754.6 5.6 copy-start.11
  757.6 3.8 copy-start.10
  761.4 3.4 copy-start.9
  (10 other events, 22.2 us)

commit v3 on v2

--- a/solution.py
+++ b/solution.py
@@ -31,7 +31,8 @@
     MOE,
     SMALL,
     SUM,
-) = range(21)
+    OUT,
+) = range(22)
 X, C, Y, Z, FAR_X, FAR_C, FAR_Z = range(7)
 ZPARTS = 4
 LANES = 128
@@ -170,6 +171,10 @@
 
 
 ANY = pl.BlockSpec(memory_space=pl.ANY)
+
+
+def like_of(a):
+    return jax.ShapeDtypeStruct(a.shape, a.dtype)
 
 
 def whole_block(a):
@@ -257,7 +262,6 @@
         gate_got,
         gate_other,
         up_got,
-        up_other,
         router_far,
         c_own,
         c_far,
@@ -269,13 +273,14 @@
         mixed,
         mixed_far,
         normed,
+        normed_far,
         inv_first,
         middle_ref,
         inv_second,
         h2_ref,
     ) = refs[17:38]
-    tok, qkv_here, qkv_far, gain_far, normed_far, give, got, square, square_far = refs[38:47]
-    own_buf, far_buf, down_own, down_buf, grad_buf, allowed, sems, local = refs[47:]
+    tok, qkv_here, qkv_far, gain_far, give, got, square, square_far = refs[38:46]
+    own_buf, far_buf, down_own, down_buf, grad_buf, allowed, sems, local = refs[46:]
     place = Place()
     t = Transfers(sems)
     x, c, y = place.x(), place.c(), place.y()
@@ -286,8 +291,10 @@
     t.add((TOK, C), tokens, tok.at[1], c)
     t.add((TOK, FAR_C), tok.at[0], tok.at[2], c)
     there = qkv_slices(qkv, 1 - place.col)
+    mine = pl.ds(pl.multiple_of(place.side * (part // 2), part // 2), part // 2)
     for i, target in enumerate(qkv_targets(qkv_far, qkv)):
-        t.add((QKV, X, i), there[i], target, x)
+        t.add((QKV, X, i), there[i].at[mine], target.at[mine], x)
+        t.add((QKV, Y, i), target.at[mine], target.at[mine], y)
     t.add((GAIN, X), gain, gain_far, x)
     t.add((ROUTER, X), router, router_far, x)
     t.add((COT, X), cot, c_far.at[0, 0], x)
@@ -305,11 +312,12 @@
     for key, ref, land, other in (
         (DOWN, w_down, down_got, down_other),
         (GATE, w_gate, gate_got, gate_other),
-        (UP, w_up, up_got, up_other),
+        (UP, w_up, up_got, None),
     ):
         src = weight_slice(ref, 1 - place.col, place.side, split, place.zed, key == DOWN)
         t.add((key, X), src, land, x)
-        t.add((key, Y), land, other, y)
+        if key != UP:
+            t.add((key, Y), land, other, y)
     for i in range(2):
         cut = pl.ds(rows * i, rows)
         t.add((MIXED, X, i), mixed.at[cut], mixed_far.at[cut], x)
@@ -317,7 +325,7 @@
     t.add((SQUARE, X), square, square_far, x)
 
     greet([x, c, y, *z[1:]])
-    t.start((COT, X), (TOK, X), (GAIN, X), *[(QKV, X, i) for i in range(3)], (ROUTER, X))
+    t.start((TOK, X), (GAIN, X), *[(QKV, X, i) for i in range(3)])
     t.start((TOK, C), (COT, C, 0), (ROUTES, C, 0), *[(ROUTES, Z, k) for k in ks])
     t.start((COT, Z, 1), (COT, Z, 2), (COT, Z, 3))
     own_cut = functools.partial(weight_slice, w_down, place.col, split=split, zed=place.zed)
@@ -342,10 +350,10 @@
         allowed[...] = allowed_tile(seg_row[b : b + 1, :], seg_col[:, b : b + 1], False)
 
     masks(1)
-    t.arrived((COT, X))
-    t.start((COT, FAR_C, 0), *[(COT, FAR_Z, k) for k in ks])
+    t.arrived(*[(QKV, X, i) for i in range(3)])
+    t.start(*[(QKV, Y, i) for i in range(3)])
     t.arrived((TOK, X), (GAIN, X))
-    t.start((TOK, FAR_C))
+    t.start((TOK, FAR_C), (COT, X), (ROUTER, X))
     inv = norm(tokens[...], tok[0], 0)
     inv_first[...] = jnp.broadcast_to(inv, inv_first.shape)
     t.arrived((TOK, C), (TOK, FAR_C))
@@ -355,7 +363,7 @@
         t.start((ROUTES, C, k))
     t.arrived((COT, Z, 1))
     t.start((COT, C, 1))
-    t.arrived(*[(QKV, X, i) for i in range(3)])
+    t.arrived(*[(QKV, Y, i) for i in range(3)])
     t.start((DOWN, X))
 
     width = q_ref.shape[1]
@@ -376,13 +384,16 @@
         values[1, cut, :] = swap_heads(block)
     attend_rows(q_ref, keys, values, allowed, mixed, rows, width // LANES)
     t.start((MIXED, X, 1))
-    t.arrived((COT, Z, 2))
-    t.start((COT, C, 2))
+    t.arrived((COT, X))
+    t.start((COT, FAR_C, 0), (COT, FAR_Z, 1), (COT, FAR_Z, 2))
     masks(0)
     attend_rows(q_ref, keys, values, allowed, mixed, 0, width // LANES)
     t.start((MIXED, X, 0))
+    t.start((GATE, X), (COT, FAR_Z, 3))
+    t.arrived((COT, Z, 2))
+    t.start((COT, C, 2))
     t.arrived((DOWN, X))
-    t.start((DOWN, Y), (GATE, X))
+    t.start((DOWN, Y), (UP, X))
 
     def project(base):
         cut = slice(base, base + rows)
@@ -406,7 +417,7 @@
             own_rows = down_own[split * n : split * (n + 1)].reshape(size, part)
             far_rows = down_buf[n].reshape(size, part)
             total = dot_nt(own_buf[...], own_rows) + dot_nt(far_buf[...], far_rows)
-            grad_buf[i % 2, :, size * n : size * (n + 1)] = RESIDUAL * total
+            grad_buf[i % 2, :, size * n : size * (n + 1)] = low(RESIDUAL * total)
         stored(i).start()
 
     t.arrived((MIXED, X, 1))
@@ -423,7 +434,6 @@
     t.arrived((DOWN, Y))
     moves(local, (down_got, down_buf.at[0]), (down_other, down_buf.at[1]))
     t.arrived((SQUARE, X))
-    t.start((UP, X))
     total = total + jnp.broadcast_to(square_far[:1, :], (LANES, rows)).T[:, :1]
     inv = lax.rsqrt(total / (2 * part) + EPS)
     inv_second[...] = jnp.broadcast_to(inv, inv_second.shape)
@@ -446,8 +456,6 @@
     t.arrived((COT, FAR_Z, 3))
     t.start((COT, FAR_C, 3))
     hidden_grads(6)
-    t.arrived((UP, X))
-    t.start((UP, Y))
     hidden_grads(7)
     stored(6).wait()
     stored(7).wait()
@@ -464,15 +472,16 @@
     mine = w_down.shape[0] // 2
     width, kv = qkv[0].shape[1] // 2, qkv[1].shape[1] // 2
     down, pair = shape((mine // 2, LANES, part)), shape((mine // 2, part, LANES))
-    hbm_outs = [down, down, pair, pair, pair, pair, like(router)]
+    hbm_outs = [down, down, pair, pair, pair, like(router)]
     hbm_outs += [stack(cot), stack(cot), stack(routes)]
-    hbm_outs += [shape((2 * ZPARTS * rows, mine * LANES), jnp.float32)]
+    hbm_outs += [shape((2 * ZPARTS * rows, mine * LANES))]
     vmem_outs = [
         shape((2 * rows, width)),
         shape((2, 2 * rows, kv)),
         shape((2, 2 * rows, kv)),
         shape((2 * rows, width)),
         shape((2 * rows, width)),
+        shape((2 * rows, part)),
         shape((2 * rows, part)),
         shape((rows, LANES), jnp.float32),
         shape((rows, part), jnp.float32),
@@ -483,7 +492,7 @@
     wide = pltpu.VMEM((rows, part), jnp.float32)
     small = pltpu.VMEM((8, rows), jnp.float32)
     weights = pltpu.VMEM((part, width + 2 * kv), jnp.bfloat16)
-    count = 12 + 6 * (ZPARTS - 1) + 6 + 2 + 2
+    count = 15 + 6 * (ZPARTS - 1) + 5 + 2 + 2
     return pl.pallas_call(
         front_kernel,
         out_shape=hbm_outs + vmem_outs,
@@ -494,7 +503,6 @@
             weights,
             weights,
             pltpu.VMEM(gain.shape, jnp.float32),
-            pltpu.VMEM((2 * rows, part), jnp.bfloat16),
             wide,
             wide,
             small,
@@ -503,7 +511,7 @@
             buffer,
             pltpu.VMEM((mine, LANES, part), jnp.bfloat16),
             pltpu.VMEM((2, mine // 2, LANES, part), jnp.bfloat16),
-            pltpu.VMEM((2, rows, mine * LANES), jnp.float32),
+            pltpu.VMEM((2, rows, mine * LANES), jnp.bfloat16),
             pltpu.VMEM((rows, rows), jnp.float32),
             pltpu.SemaphoreType.DMA((2, count)),
             pltpu.SemaphoreType.DMA((10,)),
@@ -517,28 +525,30 @@
 
 def moe_kernel(*refs):
     routes_ref, grad_ref, router_own, router_far, h2 = refs[:5]
-    w_gate, w_up, w_down, gate_got, gate_other, up_got, up_other, down_got, down_other = refs[5:14]
+    w_gate, w_up, w_down, w_out, gate_got, gate_other, up_got, down_got, down_other = refs[5:14]
     (
-        h_own_all,
-        h_far_all,
+        h_own_out,
+        h_far_out,
         moe_own,
         moe_far,
-        hidden_ref,
-        slopes_ref,
+        hidden_out,
+        slopes_out,
         dlog_ref,
+        up_other,
+        out_far,
         s0_own,
-        s0_far,
         z1_own,
-        z1_far,
+        x0_far,
         piece2,
         s3_own,
         s3_far,
-    ) = refs[14:28]
-    h_own, h_far, keep_own, keep_far, give_own, give_far, got_own, got_far, got_x = refs[28:37]
-    pair_own, pair_far, down_own, down_far, sems, local, fill = refs[37:]
+    ) = refs[14:29]
+    h_own_all, h_far_all, keep_own, keep_far, give_own, give_far, got_own, got_far = refs[29:37]
+    got_x, z1_far, pair_own, pair_far, down_own, down_far, hidden_ref, slopes_ref = refs[37:45]
+    sems, local, fill, save = refs[45:]
     experts = down_own.shape[0]
     split = experts // 2
-    rows = h_own.shape[0]
+    rows, part = h2.shape
     place = Place()
     step = pl.program_id(0)
     t = Transfers(sems)
@@ -561,6 +571,11 @@
     t.add((BACK, Z), got_own.at[1], z1_own, z[1])
     t.add((BACK, FAR_Z), got_far.at[1], z1_far, z[1])
     t.add((BACK, FAR_X), got_far.at[2], got_x, x)
+    t.add((BACK, X), got_far.at[0], x0_far, x)
+    t.add((UP, Y), up_got, up_other, place.y())
+    width = out_far.shape[0]
+    there = pl.ds(pl.multiple_of((1 - place.col) * width, LANES), width)
+    t.add((OUT, X), w_out.at[there], out_far, x)
 
     def join(k):
         for name in ((BACK, C, k), (BACK, FAR_C, k)):
@@ -572,10 +587,10 @@
 
     @pl.when(step == 0)
     def _():
-        greet([x, c, *z[1:]])
-        t.start((H, X), (H, C, 0), (H, Z, 1), (H, Z, 2))
+        greet([x, c, place.y(), *z[1:]])
+        t.start((H, X), (H, C, 0), (UP, Y), (H, Z, 1), (H, Z, 2))
         cut = functools.partial(weight_slice, which=place.col, split=split, zed=place.zed)
-        fills = []
+        fills, late = [], []
         for i, half in enumerate((place.side, 1 - place.side)):
             gates = (cut(w_gate, half=half, wide=False), (gate_got, gate_other)[i])
             ups = (cut(w_up, half=half, wide=False), (up_got, up_other)[i])
@@ -584,16 +599,19 @@
                 for e in range(split):
                     for m, src in enumerate((gates[n], ups[n])):
                         cols = pl.ds(LANES * (2 * e + m), LANES)
-                        fills.append((src.at[e], pair.at[i, :, cols]))
+                        into = late if src is up_other else fills
+                        into.append((src.at[e], pair.at[i, :, cols]))
                 fills.append((downs[n], down.at[pl.ds(split * i, split)]))
         moves(fill, (h2, h_own_all.at[0, 0]), *fills)
         t.arrived((H, X))
         t.start((H, FAR_C, 0), (H, FAR_X, 1))
+        t.arrived((UP, Y))
+        moves(fill, *late)
 
     @pl.when(step == 1)
     def _():
         t.arrived((H, C, 0), (H, FAR_C, 0), (H, Z, 1))
-        t.start((H, C, 1))
+        t.start((H, C, 1), (OUT, X))
 
     @pl.when(step == 2)
     def _():
@@ -632,15 +650,37 @@
     def _():
         t.arrived((H, C, 3), (H, FAR_C, 3))
         t.arrived((BACK, FAR_X))
-        total = got_own[2].astype(jnp.float32) + got_x[...].astype(jnp.float32)
-        got_own[2] = total.astype(jnp.bfloat16)
-
-    for k in range(ZPARTS):
-        for p in range(2):
-
-            @pl.when(step == 2 * k + p)
-            def _():
-                moves(local, (h_own_all.at[k, p], h_own), (h_far_all.at[k, p], h_far))
+        got_own[2] = low(add_wide(got_own[2], got_x[...]))
+        t.arrived((BACK, FAR_Z))
+        got_far[0] = low(add_wide(got_far[0], z1_far[...]))
+        t.start((BACK, X))
+
+    def saved(i):
+        k, p = i // 2, i % 2
+        pairs = ((h_own_all, h_own_out), (h_far_all, h_far_out))
+        return [
+            pltpu.make_async_copy(src.at[k, p], dst.at[k, p], save.at[n, i])
+            for n, (src, dst) in enumerate(pairs)
+        ]
+
+    def written(i):
+        cut = pl.ds(rows * i, rows)
+        return [
+            pltpu.make_async_copy(src, dst.at[cut], save.at[2 + n, i])
+            for n, (src, dst) in enumerate(((hidden_ref, hidden_out), (slopes_ref, slopes_out)))
+        ]
+
+    for i in range(2 * ZPARTS):
+
+        @pl.when(step == i)
+        def _():
+            for copy in saved(i):
+                copy.start()
+            if i > 0:
+                for copy in written(i - 1):
+                    copy.wait()
+
+    h_own, h_far = h_own_all.at[step // 2, step % 2], h_far_all.at[step // 2, step % 2]
 
     first = (place.core * 2 + place.col) * experts
     lane = lax.broadcasted_iota(jnp.int32, (rows, LANES), 1)
@@ -659,7 +699,7 @@
         pair = dot_nn(h_own[...], pair_own[e // split, :, cols]) + dot_nn(
             h_far[...], pair_far[e // split, :, cols]
         )
-        slope = grad_ref[:, LANES * e : LANES * (e + 1)]
+        slope = grad_ref[:, LANES * e : LANES * (e + 1)].astype(jnp.float32)
         gate_val = pair[:, :LANES]
         up_val = pair[:, LANES:]
         sigma = jax.nn.sigmoid(gate_val)
@@ -707,7 +747,13 @@
         def _():
             t.start((BACK, C, k), (BACK, FAR_C, k))
 
-    part = h_own.shape[1]
+    for i in range(2 * ZPARTS):
+
+        @pl.when(step == i)
+        def _():
+            for copy in written(i):
+                copy.start()
+
     moe_own[...] = low(dot_nn(hidden_ref[...], down_own[...].reshape(-1, part)))
     moe_far[...] = low(dot_nn(hidden_ref[...], down_far[...].reshape(-1, part)))
 
@@ -717,15 +763,19 @@
         moves(
             local,
             (got_own.at[0], s0_own),
-            (got_far.at[0], s0_far),
             (got_own.at[2], piece2),
             (got_own.at[3], s3_own),
             (got_far.at[3], s3_far),
         )
+        for copy in written(2 * ZPARTS - 1):
+            copy.wait()
+        for i in range(2 * ZPARTS):
+            for copy in saved(i):
+                copy.wait()
         t.finish(*[(BACK, hop, k) for hop in (C, FAR_C) for k in range(ZPARTS)])
 
 
-def moe_layer(routes, grad_hidden, routers, h2, weights):
+def moe_layer(routes, grad_hidden, routers, h2, weights, up_got, width):
     tile, part = h2.shape
     rows = grad_hidden.shape[0]
     experts = grad_hidden.shape[1] // LANES
@@ -735,26 +785,33 @@
     widths = [part, part, experts * LANES, 2 * experts * LANES, 2 * LANES]
     buffer = pltpu.VMEM((tile, part), jnp.bfloat16)
     stacked = pltpu.VMEM((ZPARTS, tile, part), jnp.bfloat16)
+    pieces = pltpu.VMEM((ZPARTS, 2, tile, part), jnp.bfloat16)
     pair = pltpu.VMEM((2, part, experts * LANES), jnp.bfloat16)
     down = pltpu.VMEM((experts, LANES, part), jnp.bfloat16)
-    count = 3 + 4 * (ZPARTS - 1) + 2 * ZPARTS + 3
+    extra = [like_of(up_got), jax.ShapeDtypeStruct((width, part), jnp.bfloat16)]
+    count = 3 + 4 * (ZPARTS - 1) + 2 * ZPARTS + 6
     return pl.pallas_call(
         moe_kernel,
         out_shape=[stack, stack]
         + [jax.ShapeDtypeStruct((rows, w), jnp.bfloat16) for w in widths]
-        + [one] * 7,
+        + extra
+        + [one] * 6,
         grid=(rows // tile,),
         in_specs=[by_row(routes.shape[1]), by_row(experts * LANES)]
         + [whole_block(r) for r in routers]
         + [ANY] * (1 + len(weights)),
-        out_specs=[ANY, ANY] + [by_row(w) for w in widths] + [ANY] * 7,
-        scratch_shapes=[buffer] * 6
+        out_specs=[ANY, ANY, by_row(part), by_row(part), ANY, ANY, by_row(2 * LANES)]
+        + [ANY] * 8,
+        scratch_shapes=[pieces] * 2
+        + [buffer] * 4
         + [stacked] * 2
-        + [buffer, pair, pair, down, down]
+        + [buffer, buffer, pair, pair, down, down]
+        + [pltpu.VMEM((tile, w), jnp.bfloat16) for w in widths[2:4]]
         + [
             pltpu.SemaphoreType.DMA((2, count)),
             pltpu.SemaphoreType.DMA((5,)),
             pltpu.SemaphoreType.DMA((5 + 4 * experts,)),
+            pltpu.SemaphoreType.DMA((4, 2 * ZPARTS)),
         ],
         compiler_params=pltpu.CompilerParams(
             collective_id=1, has_side_effects=True, vmem_limit_bytes=60 * 1024 * 1024
@@ -763,32 +820,41 @@
     )(routes, grad_hidden, *routers, h2, *weights)
 
 
-def weight_kernel(cargo, n_cargo, *refs):
+def weight_kernel(cargo, streamed, *refs):
+    n_cargo = len(cargo)
     h_own, h_far, c_own, c_far, hidden, slopes = refs[:6]
     sources = refs[6 : 6 + n_cargo]
-    outs = refs[6 + n_cargo : 10 + n_cargo]
+    keep_own, keep_far, give_own, rest_far = refs[6 + n_cargo : 10 + n_cargo]
     landed = refs[10 + n_cargo : 10 + 2 * n_cargo]
-    sems = refs[-1]
+    if streamed:
+        far_land = refs[10 + 2 * n_cargo]
+    give_far, sems, local = refs[-3:]
     place = Place()
     step = pl.program_id(0)
     t = Transfers(sems)
     partners = {X: place.x(), Y: place.y(), C: place.c()}
     partners.update({(Z, k): place.z(k) for k in range(1, ZPARTS)})
-    to = {name: partners[name] for name in cargo}
-    for i, name in enumerate(cargo):
-        t.add(i, sources[i], landed[i], to[name])
+    to = {name: partners[name] for name, _ in cargo}
+    for i, (name, views) in enumerate(cargo):
+        for n, view in enumerate(views):
+            t.add((i, n), sources[i].at[view], landed[i].at[n], to[name])
+    first_keys = list(t.table)
+    for e in range(streamed):
+        t.add((GRADS, e), give_far.at[e], far_land.at[e], partners[Y])
+    if streamed:
+        to[Y] = partners[Y]
 
     @pl.when(step == 0)
     def _():
         greet(list(to.values()))
-        t.start(*t.table)
+        t.start(*first_keys)
 
     half = LANES // 2
     tile = h_own.shape[2]
     first = place.side == 0
-    for keep, give, rows_h, rows_c in (
-        (outs[0], outs[2], h_own, c_own),
-        (outs[1], outs[3], h_far, c_far),
+    for keep, give, at, rows_h, rows_c in (
+        (keep_far, give_far, step, h_far, c_far),
+        (keep_own, give_own, 0, h_own, c_own),
     ):
         pair, down = 0.0, 0.0
         for i in range(2 * ZPARTS):
@@ -796,29 +862,45 @@
             pair = pair + dot_tn(slopes[rows, :], rows_h[i // 2, i % 2])
             down = down + dot_tn(hidden[rows, :], rows_c[i // 2, i % 2])
         for i, block in enumerate((pair[:LANES], pair[LANES:], RESIDUAL * down)):
-            low, high = block[:half], block[half:]
-            keep[0, half * i : half * (i + 1), :] = jnp.where(first, low, high)
-            give[0, half * i : half * (i + 1), :] = jnp.where(first, high, low).astype(
-                jnp.bfloat16
-            )
+            begin, end = block[:half], block[half:]
+            cut = slice(half * i, half * (i + 1))
+            keep[0, cut, :] = jnp.where(first, begin, end)
+            give[at, cut, :] = low(jnp.where(first, end, begin))
+        if keep is keep_far:
+            for e in range(streamed):
+
+                @pl.when(step == e)
+                def _():
+                    t.start((GRADS, e))
 
     @pl.when(step == pl.num_programs(0) - 1)
     def _():
+        rest = rest_far.shape[0]
+        moves(local, (give_far.at[pl.ds(streamed, rest)], rest_far))
         t.finish()
 
 
-def weight_grads(number, start, count, resident, hidden, slopes, cargo):
+def weight_grads(number, start, count, streamed, resident, hidden, slopes, cargo):
     part = resident[0].shape[-1]
     rows = hidden.shape[0]
     out = pl.BlockSpec((1, 3 * LANES // 2, part), lambda e: (e, 0, 0))
-    shape = (count, 3 * LANES // 2, part)
-    names = tuple(name for name, _ in cargo)
-    arrays = [array for _, array in cargo]
+    block = (3 * LANES // 2, part)
+    shape = (count, *block)
+    arrays = [array for _, array, _ in cargo]
+    views = tuple((name, tuple(where)) for name, _, where in cargo)
+    landed = []
+    for _, array, where in cargo:
+        dims = (len(where), *array.shape[len(where[0]) :])
+        landed.append(jax.ShapeDtypeStruct(dims, array.dtype))
+    rest = jax.ShapeDtypeStruct((count - streamed, *block), jnp.bfloat16)
+    if streamed:
+        landed.append(jax.ShapeDtypeStruct((streamed, *block), jnp.bfloat16))
+    transfers = sum(len(where) for _, _, where in cargo) + streamed
     return pl.pallas_call(
-        functools.partial(weight_kernel, names, len(names)),
+        functools.partial(weight_kernel, views, streamed),
         out_shape=[jax.ShapeDtypeStruct(shape, jnp.float32)] * 2
-        + [jax.ShapeDtypeStruct(shape, jnp.bfloat16)] * 2
-        + [jax.ShapeDtypeStruct(a.shape, a.dtype) for a in arrays],
+        + [jax.ShapeDtypeStruct(shape, jnp.bfloat16), rest]
+        + landed,
         grid=(count,),
         in_specs=[whole_block(a) for a in resident]
         + [
@@ -826,8 +908,12 @@
             pl.BlockSpec((rows, 2 * LANES), lambda e: (0, e + start)),
         ]
         + [ANY] * len(arrays),
-        out_specs=[out] * 4 + [ANY] * len(arrays),
-        scratch_shapes=[pltpu.SemaphoreType.DMA((2, len(names)))],
+        out_specs=[out] * 3 + [ANY] * (1 + len(landed)),
+        scratch_shapes=[
+            pltpu.VMEM(shape, jnp.bfloat16),
+            pltpu.SemaphoreType.DMA((2, transfers)),
+            pltpu.SemaphoreType.DMA((1,)),
+        ],
         compiler_params=pltpu.CompilerParams(
             collective_id=2 + number, has_side_effects=True, vmem_limit_bytes=60 * 1024 * 1024
         ),
@@ -883,48 +969,64 @@
 
 
 class WholeSum:
-    def __init__(self, t, name, ref, levels, stages, lands):
+    def __init__(self, t, name, ref, levels, stages, lands, swap=None):
         self.t, self.name, self.ref = t, name, ref
         self.stages, self.lands, self.count = stages, lands, len(levels)
         offset, rows = 0, ref.shape[0]
         self.kept, self.other = [], []
+        ways = []
         for i, (partner, bit) in enumerate(levels):
             rows = rows // 2
             self.other.append((offset + (1 - bit) * rows, rows))
             offset = offset + bit * rows
             self.kept.append((offset, rows))
-            t.add((SUM, name, i), stages[i], lands[i], partner)
-            t.add((SUM, name, 2 * self.count - 1 - i), stages[i], lands[self.count + i], partner)
+            ways.append((i, i, self.other[i], self.kept[i], partner))
+        last = self.count - 1
+        back = [
+            (i, self.count + i, self.kept[i], self.other[i], levels[i][0])
+            for i in range(last, -1, -1)
+        ]
+        if swap is not None:
+            ways.append((last, 2 * self.count, self.kept[last], self.kept[last], swap))
+        self.ways = ways + back
+        for i, (stage, land, _, _, partner) in enumerate(self.ways):
+            t.add((SUM, name, i), stages[stage], lands[land], partner)
 
     def rows(self, place):
         return pl.ds(pl.multiple_of(place[0], 8), place[1])
 
     def send(self, i):
-        j = min(i, 2 * self.count - 1 - i)
-        if i >= self.count:
-            self.t.sent((SUM, self.name, j))
-        place = (self.other if i < self.count else self.kept)[j]
-        self.stages[j][...] = low(self.ref[self.rows(place), :])
+        stage, _, place, _, _ = self.ways[i]
+        for j in range(i - 1, -1, -1):
+            if self.ways[j][0] == stage:
+                self.t.sent((SUM, self.name, j))
+                break
+        self.stages[stage][...] = low(self.ref[self.rows(place), :])
         self.t.start((SUM, self.name, i))
 
     def land(self, i):
         self.t.arrived((SUM, self.name, i))
+        _, land, _, place, _ = self.ways[i]
+        cut = self.rows(place)
+        total = self.lands[land][...].astype(jnp.float32)
         if i < self.count:
-            cut = self.rows(self.kept[i])
-            total = self.ref[cut, :] + self.lands[i][...].astype(jnp.float32)
-            self.ref[cut, :] = low(total).astype(jnp.float32) if i == self.count - 1 else total
-        else:
-            j = 2 * self.count - 1 - i
-            cut = self.rows(self.other[j])
-            self.ref[cut, :] = self.lands[self.count + j][...].astype(jnp.float32)
+            total = self.ref[cut, :] + total
+            if i == self.count - 1:
+                total = low(total).astype(jnp.float32)
+        self.ref[cut, :] = total
 
     def next(self, i):
-        self.land(i)
-        if i + 1 < 2 * self.count:
-            self.send(i + 1)
+        if 0 <= i < len(self.ways):
+            self.land(i)
+            if i + 1 < len(self.ways):
+                self.send(i + 1)
 
     def keys(self):
-        return [(SUM, self.name, i) for i in range(self.count)]
+        done = []
+        for i, way in enumerate(self.ways):
+            if any(later[0] == way[0] for later in self.ways[i + 1 :]):
+                done.append((SUM, self.name, i))
+        return done
 
 
 class SmallSum:
@@ -942,9 +1044,10 @@
         self.ref[...] = self.ref[...] + self.lands[i]
 
     def next(self, i):
-        self.land(i)
-        if i + 1 < self.lands.shape[0]:
-            self.send(i + 1)
+        if 0 <= i < self.lands.shape[0]:
+            self.land(i)
+            if i + 1 < self.lands.shape[0]:
+                self.send(i + 1)
 
     def keys(self):
         return [(SMALL, self.name, i) for i in range(self.lands.shape[0])]
@@ -960,13 +1063,14 @@
     moe_srcs = take(4)
     tokens, cot, middle, inv_first, inv_second, gain, gain_moe = take(7)
     parts = take(5)
-    q_ref, keys, values, mixed, mixed_far, normed, cosine, sine, seg_row, seg_col = take(10)
+    q_ref, keys, values, mixed, mixed_far, normed, normed_far = take(7)
+    cosine, sine, seg_row, seg_col = take(4)
     w_out, out_far, small_own, small_there = take(4)
     if with_grads:
-        grad_srcs, keep_first = take(4), take(1)[0]
+        grad_srcs, keep_first = take(3), take(1)[0]
     moe_lands = take(4)
     if with_grads:
-        grad_lands = take(4)
+        grad_lands = take(3)
     grad_tokens, grad_q, grad_k, grad_v, grad_out, small, small_last = take(7)
     qkv_here, qkv_there, da_own, da_far, grad_mixed, dqkv, dqkv_far, give, got = take(9)
     grad_middle, grad_here, grad_there, allowed, dk, dv, square, square_far = take(8)
@@ -974,7 +1078,7 @@
     stages, lands = [], []
     for _ in range(3):
         stages.append(take(count))
-        lands.append(take(2 * count))
+        lands.append(take(2 * count + 1))
     if with_grads:
         first_land, first_sum = take(2)
     sems, local = take(2)
@@ -1000,12 +1104,12 @@
     if with_grads:
         t.add((GRADS, Y, 0), grad_srcs[0], first_land, y)
         t.add((GRADS, Y, 1), grad_srcs[1], grad_lands[0], y)
-        t.add((GRADS, Y, 2), grad_srcs[2], grad_lands[1], y)
-        t.add((GRADS, X, 0), grad_srcs[3], grad_lands[2], x)
-        t.add((GRADS, X, 1), first_sum, grad_lands[3], x)
-    sum_out = WholeSum(t, 0, grad_out, high_levels + low_levels, stages[0], lands[0])
-    sum_here = WholeSum(t, 1, grad_here, low_levels + high_levels, stages[1], lands[1])
-    sum_there = WholeSum(t, 2, grad_there, high_levels + low_levels, stages[2], lands[2])
+        t.add((GRADS, X, 0), grad_srcs[2], grad_lands[1], x)
+        t.add((GRADS, X, 1), first_sum, grad_lands[2], x)
+    up, down = high_levels + low_levels, low_levels + high_levels
+    sum_out = WholeSum(t, 0, grad_out, up, stages[0], lands[0])
+    sum_here = WholeSum(t, 1, grad_here, down, stages[1], lands[1])
+    sum_there = WholeSum(t, 2, grad_there, up, stages[2], lands[2], x)
     small_sum = SmallSum(t, 0, small, [c] + partners, small_lands)
     last_sum = SmallSum(t, 1, small_last, [c] + partners, last_lands)
 
@@ -1081,9 +1185,11 @@
     masks(0)
     attend(0, width // LANES)
     t.start((DQKV, 0))
-    sum_out.next(1)
     grad_here[...] = dot_tn(normed[...], dqkv[...])
     sum_here.send(0)
+    grad_there[...] = dot_tn(normed_far[...], dqkv[...])
+    sum_there.send(0)
+    sum_out.next(1)
     t.arrived((DQKV, 1))
 
     def tokens_back(cut):
@@ -1091,16 +1197,13 @@
 
     give[...] = tokens_back(slice(rows, 2 * rows))
     t.start((ATTN, C))
-    if with_grads:
-        t.start((GRADS, Y, 2))
+    sum_here.next(0)
+    sum_there.next(0)
     sum_out.next(2)
     small_sum.next(2)
     t.arrived((DQKV, 0))
-    t.start((MOE, 3))
     if with_grads:
         t.start((GRADS, X, 1))
-    grad_there[...] = dot_tn(normed[...], dqkv_far[...])
-    sum_there.send(0)
     grad = tokens_back(slice(0, rows))
     t.arrived((ATTN, C))
     grad = grad + got[...]
@@ -1112,22 +1215,23 @@
     small_last[...] = jnp.zeros_like(small_last)
     small_last[0:1, :] = jnp.sum(grad * value * inv, 0, keepdims=True)
     last_sum.send(0)
-    sum_here.next(0)
+    sum_here.next(1)
+    sum_there.next(1)
     sum_out.next(3)
     inner = exchanged(1, inner)
+    t.start((MOE, 3))
     grad = norm_back(got[...], tokens[...].astype(jnp.float32), inv, gain[...], inner)
     grad_tokens[...] = grad_middle[...] + grad
     last_sum.next(0)
-    for i in range(2 * count):
-        if i + 4 < 2 * count:
-            sum_out.next(i + 4)
-        if i + 1 < 2 * count:
-            sum_here.next(i + 1)
+    for i in range(2, 2 * count + 1):
+        sum_here.next(i)
         sum_there.next(i)
-        if i + 3 < small_lands.shape[0]:
-            small_sum.next(i + 3)
-        if i + 1 < last_lands.shape[0]:
-            last_sum.next(i + 1)
+        sum_out.next(i + 2)
+        small_sum.next(i + 1)
+        last_sum.next(i - 1)
+    for i in range(2 * count, small_lands.shape[0]):
+        small_sum.next(i + 1)
+        last_sum.next(i)
     start = 0
     for out in (grad_q, grad_k, grad_v):
         size = out.shape[1] // 2
@@ -1141,7 +1245,7 @@
 
 def back(levels, qkv, moe_srcs, vmem_ins, grads):
     tokens, middle, q = vmem_ins[0], vmem_ins[2], vmem_ins[12]
-    w_out, small_own = vmem_ins[22], vmem_ins[24]
+    w_out, small_own = vmem_ins[23], vmem_ins[25]
     rows, part = tokens.shape
     width, kv = q.shape[1], qkv[1].shape[1] // 2
     both = width + 2 * kv
@@ -1153,8 +1257,8 @@
     extra_ins, extra_specs, extra_scratch = [], [], []
     if grads:
         extra_ins = list(grads)
-        extra_specs = [ANY] * 4 + [vmem]
-        hbm_outs += [like(a) for a in grads[:4]]
+        extra_specs = [ANY] * 3 + [vmem]
+        hbm_outs += [like(a) for a in (*grads[1:3], grads[0])]
         extra_scratch = [pltpu.VMEM(grads[0].shape, bf16)] * 2
     small_last = shape((8, part), f32)
     vmem_outs = [shape((rows, part), f32)]
@@ -1173,9 +1277,9 @@
     scratch += [pltpu.VMEM((levels + 1, 8, part), f32)]
     for high, wide_cols in ((w_out.shape[0], part), (part, both), (part, both)):
         sizes = [pltpu.VMEM((high >> (i + 1), wide_cols), bf16) for i in range(levels)]
-        scratch += sizes * 3
+        scratch += sizes * 3 + sizes[-1:]
     scratch += extra_scratch
-    count = 9 + 4 + 5 + 3 * 2 * levels + 2 * (levels + 1)
+    count = 9 + 4 + 4 + 3 * 2 * levels + 1 + 2 * (levels + 1)
     scratch += [pltpu.SemaphoreType.DMA((2, count)), pltpu.SemaphoreType.DMA((6,))]
     return pl.pallas_call(
         functools.partial(back_kernel, levels, bool(grads)),
@@ -1184,7 +1288,7 @@
         out_specs=[ANY] * len(hbm_outs) + [vmem] * len(vmem_outs),
         scratch_shapes=scratch,
         compiler_params=pltpu.CompilerParams(
-            collective_id=4, has_side_effects=True, vmem_limit_bytes=62 * 1024 * 1024
+            collective_id=4, has_side_effects=True, vmem_limit_bytes=63 * 1024 * 1024
         ),
         name="back",
     )(*qkv, *moe_srcs, *vmem_ins, *extra_ins)
@@ -1246,7 +1350,6 @@
         gate_got,
         gate_other,
         up_got,
-        up_other,
         router_far,
         c_own,
         c_far,
@@ -1258,6 +1361,7 @@
         mixed,
         mixed_far,
         normed,
+        normed_far,
         inv_first,
         middle,
         inv_second,
@@ -1288,10 +1392,11 @@
         hidden,
         slopes,
         dlog,
+        _,
+        out_far,
         s0_own,
-        s0_far,
         z1_own,
-        z1_far,
+        x0_far,
         piece2,
         s3_own,
         s3_far,
@@ -1300,38 +1405,41 @@
         grad_hidden,
         [router_own, router_far],
         h2,
-        [w_gate, w_up, w_down, gate_got, gate_other, up_got, up_other, down_got, down_other],
+        [w_gate, w_up, w_down, w_out, gate_got, gate_other, up_got, down_got, down_other],
+        up_got,
+        width,
     )
     resident = [h_own, h_far, c_own, c_far]
-    out_there = lax.dynamic_slice_in_dim(w_out, (1 - col) * width, width, 0)
     moe_own, moe_far = (a.reshape(ZPARTS, 2, rows, part) for a in (moe_own, moe_far))
+    seconds = tuple((k, 1) for k in range(ZPARTS))
     cargo = [
-        ((Z, 2), piece2),
-        (X, s3_far),
-        (X, low(add_wide(s0_far, z1_far))),
-        (X, out_there),
-        (C, moe_own[:, 1]),
-        (C, moe_far[:, 1]),
+        ((Z, 2), piece2[None], ((0,),)),
+        (X, s3_far[None], ((0,),)),
+        (C, moe_own, seconds),
+        (C, moe_far, seconds),
     ]
-    *first_part, z2_piece, x3_far, x0_far, out_far, sib_own, sib_far = weight_grads(
-        0, 0, split, resident, hidden, slopes, cargo
-    )
+    streamed = split - 1 if half_mask == 1 else 0
+    first_outs = weight_grads(0, 0, split, streamed, resident, hidden, slopes, cargo)
+    first_part, (z2_piece, x3_far, sib_own, sib_far) = first_outs[:4], first_outs[4:8]
+    far_early = first_outs[8:]
     moe_own = low(add_wide(moe_own[:, 0], sib_own))
     moe_far = low(add_wide(moe_far[:, 0], sib_far))
     cargo = [
-        ((Z, 3), low(add_wide(s3_own, x3_far))),
-        (Y, first_part[3]),
-        (X, moe_far[2:]),
-        ((Z, 1), moe_far[1]),
+        ((Z, 3), low(add_wide(s3_own[None], x3_far)), ((0,),)),
+        (Y, first_part[3][None], ((0,),)),
+        (Y, first_part[2][None], ((0,),)),
+        (X, moe_far, ((2,), (3,))),
+        ((Z, 1), moe_far, ((1,),)),
     ]
-    *second_part, z3_piece, y_far, moe_x, moe_z1_far = weight_grads(
-        1, split, split, resident, hidden, slopes, cargo
+    *second_part, z3_piece, far_late, got_second, moe_x, moe_z1_far = weight_grads(
+        1, split, split, 0, resident, hidden, slopes, cargo
     )
+    z2_piece, z3_piece, got_second = z2_piece[0], z3_piece[0], got_second[0]
     moe_srcs = [
         moe_own[1],
         low(add_wide(moe_own[2], moe_x[0])),
         low(add_wide(moe_own[3], moe_x[1])),
-        low(add_wide(moe_far[0], moe_z1_far)),
+        low(add_wide(moe_far[0], moe_z1_far[0])),
     ]
 
     def router_term(h_rows):
@@ -1358,6 +1466,7 @@
         mixed,
         mixed_far,
         normed,
+        normed_far,
         cosine,
         sine,
         seg_rows,
@@ -1370,22 +1479,21 @@
     swap = lambda a: flip(a, "dp", half_mask)
     plain = half_mask == 1
     grads = []
+    y_far = jnp.concatenate([*far_early, far_late[0]], 0)
     if plain:
         second_far = low(add_wide(second_part[1], y_far))
-        grads = [second_part[3], first_part[2], second_part[2], second_far, first_part[1]]
+        grads = [second_part[3], second_part[2], second_far, first_part[1]]
     outs = back(levels, qkv, moe_srcs, vmem_ins, grads)
     moe_parts, outs = outs[:4], outs[4:]
+    own_second = add_wide(second_part[0], got_second)
     if plain:
-        (got_second, got_first, far_second, far_first), outs = outs[:4], outs[4:]
-        own_first, own_second = add_wide(first_part[0], got_first), add_wide(
-            second_part[0], got_second
-        )
+        (got_first, far_second, far_first), outs = outs[:3], outs[3:]
+        own_first = add_wide(first_part[0], got_first)
     else:
 
-        def finish_grads(kept, got_own, got_far):
+        def finish_grads(keep_own, keep_far):
             shape = (split, 3, units // 2, part)
-            keep_own = add_wide(kept[0], got_own).reshape(shape)
-            keep_far = add_wide(kept[1], got_far).reshape(shape)
+            keep_own, keep_far = keep_own.reshape(shape), keep_far.reshape(shape)
             mask = half_mask // 2
             while mask:
                 keep_own = halve(keep_own, member, mask, 2)
@@ -1393,9 +1501,10 @@
                 mask //= 2
             return keep_own, flip(low(keep_far), "col")
 
-        own_second, far_second = finish_grads(second_part, swap(first_part[2]), y_far)
+        own_second, far_second = finish_grads(own_second, add_wide(second_part[1], y_far))
         own_first, far_first = finish_grads(
-            first_part, swap(second_part[2]), swap(second_part[3])
+            add_wide(first_part[0], swap(second_part[2])),
+            add_wide(first_part[1], swap(second_part[3])),
         )
     grad_tokens, grad_query, grad_key, grad_value, grad_out, small, small_last = outs
 

time: 773 us -> 701 us (0.907)
  Pallas kernels: 691 us -> 629 us
    pallas_call x1, Pallas kernels: 217 us -> 193 us  [back(): pl.pallas_call(functools.partial(back_kernel, levels, bool(grads)), out_s...]
    pallas_call x1, Pallas kernels: 177 us -> 154 us  [moe_layer(): pl.pallas_call(moe_kernel, out_shape=[stack, stack] + [jax.ShapeDtypeStru...]
    pallas_call x1, Pallas kernels: 189 us -> 179 us  [front(): pl.pallas_call(front_kernel, out_shape=hbm_outs + vmem_outs, in_specs=[vm...]
where the time goes in v3:
time: 701 us; the launch traced here: 694 us
  Pallas kernels  629 us (90%)
  other arithmetic  33.1 us (5%)
  local copies, waits for them, and re-layouts  23.5 us (3%)
    pallas_call x1, Pallas kernels, back(): pl.pallas_call(functools.partial(back_kernel, levels, bool(grads)), out_s...  193 us
    pallas_call x1, Pallas kernels, front(): pl.pallas_call(front_kernel, out_shape=hbm_outs + vmem_outs, in_specs=[vm...  179 us
    pallas_call x1, Pallas kernels, moe_layer(): pl.pallas_call(moe_kernel, out_shape=[stack, stack] + [jax.ShapeDtypeStru...  154 us
    pallas_call x2, Pallas kernels, weight_grads(): pl.pallas_call(functools.partial(weight_kernel, views, streamed), out_sha...  103 us
    convert_element_type x6, other arithmetic, low(): return value.astype(jnp.bfloat16)  14.2 us

profile of v3, /device:TPU:0, one launch (start us, length us, event | category | flops | bytes accessed | tf_op | source)
XLA Modules:
  0.0 693.7 jit_solution(614021297953164472)
XLA Ops:
  2.4 1.3 broadcast_in_dim.39.refs_10_.refs_12_
  3.6 1.3 broadcast_in_dim.40.refs_11_.refs_13_
  7.5 3.1 fusion.18
  11.2 179.5 %front.1 = (bf16[5,128,768]{2,1,0:T(8,128)(2,1)}, bf16[5,128,768]{2,1,0:T(8,128)(2,1)}, bf16[5,768,128]{2,1,0:T(8,128)(2,1)}, bf16[5,768,128]{2,1,0:T(8,128)(2,1...) custom-call(bf16[512,768]{1,0:T(8,128)(2,1)} %refs_7_.5, ...), custom_call_target="tpu_custom_call" | custom-call | tf_op jit(solution)/shard_map/front/pallas_call | solution.py:496
  190.7 2.8 copy.44
  193.6 154.5 %moe_layer.1 = (bf16[4,2,512,768]{3,2,1,0:T(8,128)(2,1)}, bf16[4,2,512,768]{3,2,1,0:T(8,128)(2,1)}, bf16[4096,768]{1,0:T(8,128)(2,1)}, bf16[4096,768]{1,0:T(8,12...) custom-call(s32[4096,8]{1,0:T(8,128)} %bitcast.93, ...), custom_call_target="tpu_custom_call" | custom-call | tf_op jit(solution)/shard_map/moe_layer/pallas_call | solution.py:793
  348.1 51.1 %expert_weight_grads.2 = (f32[5,192,768]{2,1,0:T(8,128)}, f32[5,192,768]{2,1,0:T(8,128)}, bf16[5,192,768]{2,1,0:T(8,128)(2,1)}, bf16[1,192,768]{2,1,0:T(8,128)(2...) custom-call(bf16[4,2,512,768]{3,2,1,0:T(8,128)(2,1)} %get-tuple-elem, ...), custom_call_target="tpu_custom_call" | custom-call | tf_op jit(solution)/shard_map/expert_weight_grads/pallas_call | solution.py:899
  399.3 3.7 fusion.1
  405.4 1.7 copy-done.3
  407.2 2.5 fusion.refs_9_.refs_10_
  409.7 51.5 %expert_weight_grads.3 = (f32[5,192,768]{2,1,0:T(8,128)}, f32[5,192,768]{2,1,0:T(8,128)}, bf16[5,192,768]{2,1,0:T(8,128)(2,1)}, bf16[5,192,768]{2,1,0:T(8,128)(2...) custom-call(bf16[4,2,512,768]{3,2,1,0:T(8,128)(2,1)} %get-tuple-elem, ...), custom_call_target="tpu_custom_call" | custom-call | tf_op jit(solution)/shard_map/expert_weight_grads/pallas_call | solution.py:899
  461.3 3.0 fusion.16
  464.4 2.4 fusion.17.refs_6_
  466.7 4.8 fusion.22
  472.2 1.8 fusion.23
  474.8 1.5 add_convert_fusion.refs_36_
  476.3 192.7 %back.1 = (bf16[512,768]{1,0:T(8,128)(2,1)}, bf16[512,768]{1,0:T(8,128)(2,1)}, bf16[512,768]{1,0:T(8,128)(2,1)}, bf16[512,768]{1,0:T(8,128)(2,1)}, bf16[5,192,76...) custom-call(bf16[768,768]{1,0:T(8,128)(2,1)} %refs_0_.3, ...), custom_call_target="tpu_custom_call" | custom-call | tf_op jit(solution)/shard_map/back/pallas_call | solution.py:1284
  669.0 4.4 fusion.14
  673.4 1.3 slice_reduce_fusion.2
  676.0 3.5 fusion.8
  680.1 1.2 copy_select_fusion
  681.3 5.1 fusion.6
  688.7 1.4 copy.67
  692.1 1.4 copy.70
  (75 shorter events, 14.9 us)
Async XLA Ops:
  6.2 5.1 copy-start.2
  399.2 5.8 slice-start.2
  399.2 4.7 copy-start.14
  399.2 4.7 copy-start.16
  399.2 6.2 slice-start.3
  403.0 58.3 %copy-start.1 = (bf16[4,512,768]{2,1,0:T(8,128)(2,1)}, bf16[4,512,768]{2,1,0:T(8,128)(2,1)S(1)}, u32[]{:S(2)}) copy-start(bf16[4,512,768]{2,1,0:T(8,128)(2,1)S(1)} %fusion.1) | copy-start | bytes 9437188
  403.0 4.2 copy-start.3
  461.3 3.1 copy-start.15
  461.3 5.4 copy-start
  464.4 7.8 %slice-start = ((s8[6291456]{0:T(1024)(128)(4,1)}), s8[4194304]{0:T(1024)(128)(4,1)S(1)}, s32[]{:S(2)}) async-start(s8[6291456]{0:T(1024)(128)(4,1)} %bitcast.76), calls=%async_computation | async-start | bytes 8388608
  466.7 5.5 slice-start.1
  472.2 2.6 copy-start.5
  472.2 2.6 copy-start.11
  472.2 2.6 copy-start.17
  669.0 5.8 copy-start.18
  669.0 7.0 %copy-start.4 = (f32[5,192,768]{2,1,0:T(8,128)S(1)}, f32[5,192,768]{2,1,0:T(8,128)}, u32[]{:S(2)}) copy-start(f32[5,192,768]{2,1,0:T(8,128)} %get-tuple-element.140) | copy-start | bytes 8847364
  676.0 3.6 copy-start.9
  676.0 3.6 copy-start.10
  681.3 5.1 copy-start.8
  686.4 2.2 copy-start.7
  688.7 1.7 copy-start.13
  688.7 2.5 copy-start.12
  688.7 3.4 copy-start.6

commit v4 on v3

--- a/solution.py
+++ b/solution.py
@@ -35,6 +35,7 @@
 ) = range(22)
 X, C, Y, Z, FAR_X, FAR_C, FAR_Z = range(7)
 ZPARTS = 4
+EARLY = 6
 LANES = 128
 
 
@@ -280,7 +281,7 @@
         h2_ref,
     ) = refs[17:38]
     tok, qkv_here, qkv_far, gain_far, give, got, square, square_far = refs[38:46]
-    own_buf, far_buf, down_own, down_buf, grad_buf, allowed, sems, local = refs[46:]
+    own_buf, far_buf, down_own, down_buf, grad_buf, allowed, pair_stage, qkv_stage, sems, local = refs[46:]
     place = Place()
     t = Transfers(sems)
     x, c, y = place.x(), place.c(), place.y()
@@ -291,10 +292,10 @@
     t.add((TOK, C), tokens, tok.at[1], c)
     t.add((TOK, FAR_C), tok.at[0], tok.at[2], c)
     there = qkv_slices(qkv, 1 - place.col)
-    mine = pl.ds(pl.multiple_of(place.side * (part // 2), part // 2), part // 2)
-    for i, target in enumerate(qkv_targets(qkv_far, qkv)):
-        t.add((QKV, X, i), there[i].at[mine], target.at[mine], x)
-        t.add((QKV, Y, i), target.at[mine], target.at[mine], y)
+    half = part // 2
+    halves = [pl.ds(pl.multiple_of(i * half, half), half) for i in (place.side, 1 - place.side)]
+    t.add((QKV, X), qkv_stage, qkv_far.at[0], x)
+    t.add((QKV, Y), qkv_far.at[0], qkv_far.at[1], y)
     t.add((GAIN, X), gain, gain_far, x)
     t.add((ROUTER, X), router, router_far, x)
     t.add((COT, X), cot, c_far.at[0, 0], x)
@@ -309,12 +310,16 @@
         t.add((ROUTES, Z, k), routes, route_all.at[k, 0], z[k])
         t.add((ROUTES, C, k), route_all.at[k, 0], route_all.at[k, 1], c)
     split = down_got.shape[0]
+    staged = []
     for key, ref, land, other in (
         (DOWN, w_down, down_got, down_other),
         (GATE, w_gate, gate_got, gate_other),
         (UP, w_up, up_got, None),
     ):
         src = weight_slice(ref, 1 - place.col, place.side, split, place.zed, key == DOWN)
+        if key != DOWN:
+            staged.append((src, pair_stage.at[len(staged)]))
+            src = staged[-1][1]
         t.add((key, X), src, land, x)
         if key != UP:
             t.add((key, Y), land, other, y)
@@ -325,7 +330,10 @@
     t.add((SQUARE, X), square, square_far, x)
 
     greet([x, c, y, *z[1:]])
-    t.start((TOK, X), (GAIN, X), *[(QKV, X, i) for i in range(3)])
+    t.start((TOK, X), (GAIN, X))
+    targets = [target.at[pl.ds(0, half)] for target in qkv_targets(qkv_stage, qkv)]
+    moves(local, *[(src.at[halves[0]], target) for src, target in zip(there, targets)])
+    t.start((QKV, X))
     t.start((TOK, C), (COT, C, 0), (ROUTES, C, 0), *[(ROUTES, Z, k) for k in ks])
     t.start((COT, Z, 1), (COT, Z, 2), (COT, Z, 3))
     own_cut = functools.partial(weight_slice, w_down, place.col, split=split, zed=place.zed)
@@ -336,6 +344,7 @@
         (own_cut(half=place.side, wide=True), down_own.at[pl.ds(0, split)]),
         (own_cut(half=1 - place.side, wide=True), down_own.at[pl.ds(split, split)]),
         *zip(qkv_slices(qkv, place.col), qkv_targets(qkv_here, qkv)),
+        *staged,
     )
 
     def norm(own, far, base):
@@ -350,8 +359,8 @@
         allowed[...] = allowed_tile(seg_row[b : b + 1, :], seg_col[:, b : b + 1], False)
 
     masks(1)
-    t.arrived(*[(QKV, X, i) for i in range(3)])
-    t.start(*[(QKV, Y, i) for i in range(3)])
+    t.arrived((QKV, X))
+    t.start((QKV, Y))
     t.arrived((TOK, X), (GAIN, X))
     t.start((TOK, FAR_C), (COT, X), (ROUTER, X))
     inv = norm(tokens[...], tok[0], 0)
@@ -363,14 +372,15 @@
         t.start((ROUTES, C, k))
     t.arrived((COT, Z, 1))
     t.start((COT, C, 1))
-    t.arrived(*[(QKV, Y, i) for i in range(3)])
+    t.arrived((QKV, Y))
     t.start((DOWN, X))
 
     width = q_ref.shape[1]
     for base in (rows, 0):
         cut = slice(base, base + rows)
         qkv_rows = dot_nn(normed[cut, :], qkv_here[...])
-        qkv_rows = qkv_rows + dot_nn(normed_far[cut, :], qkv_far[...])
+        for i in range(2):
+            qkv_rows = qkv_rows + dot_nn(normed_far[cut, halves[i]], qkv_far[i])
         for i in range(width // LANES + 1):
             block = qkv_rows[:, LANES * i : LANES * (i + 1)]
             block = turn(block, cosine[cut, :], sine[cut, :])
@@ -389,11 +399,11 @@
     masks(0)
     attend_rows(q_ref, keys, values, allowed, mixed, 0, width // LANES)
     t.start((MIXED, X, 0))
-    t.start((GATE, X), (COT, FAR_Z, 3))
+    t.start((COT, FAR_Z, 3))
     t.arrived((COT, Z, 2))
     t.start((COT, C, 2))
     t.arrived((DOWN, X))
-    t.start((DOWN, Y), (UP, X))
+    t.start((DOWN, Y))
 
     def project(base):
         cut = slice(base, base + rows)
@@ -403,7 +413,7 @@
 
     def stored(i):
         out = grad_hidden.at[pl.ds(rows * i, rows)]
-        return pltpu.make_async_copy(grad_buf.at[i % 2], out, local.at[8 + i % 2])
+        return pltpu.make_async_copy(grad_buf.at[i % 2], out, local.at[9 + i % 2])
 
     def hidden_grads(i):
         k, p = i // 2, i % 2
@@ -422,8 +432,9 @@
 
     t.arrived((MIXED, X, 1))
     give[...] = project(rows)
-    t.start((ATTN, C))
+    t.start((ATTN, C), (GATE, X))
     t.arrived((MIXED, X, 0))
+    t.start((UP, X))
     attn = project(0)
     t.arrived((ATTN, C))
     middle = tokens[...].astype(jnp.float32) + RESIDUAL * (attn + got[...])
@@ -433,13 +444,13 @@
     t.start((SQUARE, X))
     t.arrived((DOWN, Y))
     moves(local, (down_got, down_buf.at[0]), (down_other, down_buf.at[1]))
+    hidden_grads(0)
     t.arrived((SQUARE, X))
     total = total + jnp.broadcast_to(square_far[:1, :], (LANES, rows)).T[:, :1]
     inv = lax.rsqrt(total / (2 * part) + EPS)
     inv_second[...] = jnp.broadcast_to(inv, inv_second.shape)
     h2_ref[...] = low(middle_ref[...] * inv * gain_moe[...])
 
-    hidden_grads(0)
     hidden_grads(1)
     t.arrived((COT, FAR_Z, 1))
     t.start((COT, FAR_C, 1))
@@ -447,18 +458,14 @@
     t.arrived((GATE, X))
     t.start((GATE, Y))
     hidden_grads(3)
-    t.arrived((COT, FAR_Z, 2))
-    t.start((COT, FAR_C, 2))
-    t.arrived((COT, Z, 3))
-    t.start((COT, C, 3))
+    t.arrived((COT, FAR_Z, 2), (COT, Z, 3))
+    t.start((COT, FAR_C, 2), (COT, C, 3))
     hidden_grads(4)
     hidden_grads(5)
     t.arrived((COT, FAR_Z, 3))
     t.start((COT, FAR_C, 3))
-    hidden_grads(6)
-    hidden_grads(7)
-    stored(6).wait()
-    stored(7).wait()
+    stored(EARLY - 2).wait()
+    stored(EARLY - 1).wait()
     t.finish()
 
 
@@ -474,7 +481,7 @@
     down, pair = shape((mine // 2, LANES, part)), shape((mine // 2, part, LANES))
     hbm_outs = [down, down, pair, pair, pair, like(router)]
     hbm_outs += [stack(cot), stack(cot), stack(routes)]
-    hbm_outs += [shape((2 * ZPARTS * rows, mine * LANES))]
+    hbm_outs += [shape((EARLY * rows, mine * LANES))]
     vmem_outs = [
         shape((2 * rows, width)),
         shape((2, 2 * rows, kv)),
@@ -492,6 +499,7 @@
     wide = pltpu.VMEM((rows, part), jnp.float32)
     small = pltpu.VMEM((8, rows), jnp.float32)
     weights = pltpu.VMEM((part, width + 2 * kv), jnp.bfloat16)
+    half_weights = pltpu.VMEM((part // 2, width + 2 * kv), jnp.bfloat16)
     count = 15 + 6 * (ZPARTS - 1) + 5 + 2 + 2
     return pl.pallas_call(
         front_kernel,
@@ -501,7 +509,7 @@
         scratch_shapes=[
             pltpu.VMEM((3, rows, part), jnp.bfloat16),
             weights,
-            weights,
+            pltpu.VMEM((2, part // 2, width + 2 * kv), jnp.bfloat16),
             pltpu.VMEM(gain.shape, jnp.float32),
             wide,
             wide,
@@ -513,8 +521,10 @@
             pltpu.VMEM((2, mine // 2, LANES, part), jnp.bfloat16),
             pltpu.VMEM((2, rows, mine * LANES), jnp.bfloat16),
             pltpu.VMEM((rows, rows), jnp.float32),
+            pltpu.VMEM((2, *pair.shape), jnp.bfloat16),
+            half_weights,
             pltpu.SemaphoreType.DMA((2, count)),
-            pltpu.SemaphoreType.DMA((10,)),
+            pltpu.SemaphoreType.DMA((11,)),
         ],
         compiler_params=pltpu.CompilerParams(
             collective_id=0, has_side_effects=True, vmem_limit_bytes=58 * 1024 * 1024
@@ -524,8 +534,8 @@
 
 
 def moe_kernel(*refs):
-    routes_ref, grad_ref, router_own, router_far, h2 = refs[:5]
-    w_gate, w_up, w_down, w_out, gate_got, gate_other, up_got, down_got, down_other = refs[5:14]
+    routes_ref, grad_ref, router_own, router_far, h2, c_own, c_far = refs[:7]
+    w_gate, w_up, w_down, w_out, gate_got, gate_other, up_got, down_got, down_other = refs[7:16]
     (
         h_own_out,
         h_far_out,
@@ -542,10 +552,10 @@
         piece2,
         s3_own,
         s3_far,
-    ) = refs[14:29]
-    h_own_all, h_far_all, keep_own, keep_far, give_own, give_far, got_own, got_far = refs[29:37]
-    got_x, z1_far, pair_own, pair_far, down_own, down_far, hidden_ref, slopes_ref = refs[37:45]
-    sems, local, fill, save = refs[45:]
+    ) = refs[16:31]
+    h_own_all, h_far_all, keep_own, keep_far, give_own, give_far, got_own, got_far = refs[31:39]
+    got_x, z1_far, pair_own, pair_far, down_own, down_far, hidden_ref, slopes_ref = refs[39:47]
+    grad_late, sems, local, fill, save = refs[47:]
     experts = down_own.shape[0]
     split = experts // 2
     rows, part = h2.shape
@@ -603,8 +613,20 @@
                         into.append((src.at[e], pair.at[i, :, cols]))
                 fills.append((downs[n], down.at[pl.ds(split * i, split)]))
         moves(fill, (h2, h_own_all.at[0, 0]), *fills)
+
+        def hidden_grads(i):
+            k, p = (EARLY + i) // 2, (EARLY + i) % 2
+            moves(local, (c_own.at[k, p], give_own), (c_far.at[k, p], give_far))
+            total = dot_nt(give_own[...], down_own[...].reshape(-1, part))
+            total = total + dot_nt(give_far[...], down_far[...].reshape(-1, part))
+            grad_late[i] = low(RESIDUAL * total)
+
+        for i in range(ZPARTS - EARLY // 2):
+            hidden_grads(i)
         t.arrived((H, X))
         t.start((H, FAR_C, 0), (H, FAR_X, 1))
+        for i in range(ZPARTS - EARLY // 2, 2 * ZPARTS - EARLY):
+            hidden_grads(i)
         t.arrived((UP, Y))
         moves(fill, *late)
 
@@ -692,6 +714,7 @@
     expo = jnp.where(chosen, jnp.exp(logits - peak), 0.0)
     gates = expo / jnp.sum(expo, axis=1, keepdims=True)
     grad_gates = jnp.zeros((rows, LANES), jnp.float32)
+    at_late = jnp.maximum(step - EARLY, 0)
     for e in range(experts):
         here = lane == first + (e + place.side * split) % experts
         gate = jnp.sum(jnp.where(here, gates, 0.0), axis=1, keepdims=True)
@@ -699,7 +722,9 @@
         pair = dot_nn(h_own[...], pair_own[e // split, :, cols]) + dot_nn(
             h_far[...], pair_far[e // split, :, cols]
         )
-        slope = grad_ref[:, LANES * e : LANES * (e + 1)].astype(jnp.float32)
+        cut = slice(LANES * e, LANES * (e + 1))
+        slope = jnp.where(step < EARLY, grad_ref[:, cut], grad_late[at_late, :, cut])
+        slope = slope.astype(jnp.float32)
         gate_val = pair[:, :LANES]
         up_val = pair[:, LANES:]
         sigma = jax.nn.sigmoid(gate_val)
@@ -775,9 +800,9 @@
         t.finish(*[(BACK, hop, k) for hop in (C, FAR_C) for k in range(ZPARTS)])
 
 
-def moe_layer(routes, grad_hidden, routers, h2, weights, up_got, width):
+def moe_layer(routes, grad_hidden, routers, h2, c_rows, weights, up_got, width):
     tile, part = h2.shape
-    rows = grad_hidden.shape[0]
+    rows = routes.shape[0]
     experts = grad_hidden.shape[1] // LANES
     by_row = lambda width: pl.BlockSpec((tile, width), lambda i: (i, 0))
     stack = jax.ShapeDtypeStruct((ZPARTS, 2, tile, part), jnp.bfloat16)
@@ -797,9 +822,12 @@
         + extra
         + [one] * 6,
         grid=(rows // tile,),
-        in_specs=[by_row(routes.shape[1]), by_row(experts * LANES)]
+        in_specs=[
+            by_row(routes.shape[1]),
+            pl.BlockSpec((tile, experts * LANES), lambda i: (jnp.minimum(i, EARLY - 1), 0)),
+        ]
         + [whole_block(r) for r in routers]
-        + [ANY] * (1 + len(weights)),
+        + [ANY] * (3 + len(weights)),
         out_specs=[ANY, ANY, by_row(part), by_row(part), ANY, ANY, by_row(2 * LANES)]
         + [ANY] * 8,
         scratch_shapes=[pieces] * 2
@@ -807,6 +835,7 @@
         + [stacked] * 2
         + [buffer, buffer, pair, pair, down, down]
         + [pltpu.VMEM((tile, w), jnp.bfloat16) for w in widths[2:4]]
+        + [pltpu.VMEM((2 * ZPARTS - EARLY, tile, widths[2]), jnp.bfloat16)]
         + [
             pltpu.SemaphoreType.DMA((2, count)),
             pltpu.SemaphoreType.DMA((5,)),
@@ -814,10 +843,10 @@
             pltpu.SemaphoreType.DMA((4, 2 * ZPARTS)),
         ],
         compiler_params=pltpu.CompilerParams(
-            collective_id=1, has_side_effects=True, vmem_limit_bytes=60 * 1024 * 1024
+            collective_id=1, has_side_effects=True, vmem_limit_bytes=63 * 1024 * 1024
         ),
         name="moe_layer",
-    )(routes, grad_hidden, *routers, h2, *weights)
+    )(routes, grad_hidden, *routers, h2, *c_rows, *weights)
 
 
 def weight_kernel(cargo, streamed, *refs):
@@ -1106,10 +1135,10 @@
         t.add((GRADS, Y, 1), grad_srcs[1], grad_lands[0], y)
         t.add((GRADS, X, 0), grad_srcs[2], grad_lands[1], x)
         t.add((GRADS, X, 1), first_sum, grad_lands[2], x)
-    up, down = high_levels + low_levels, low_levels + high_levels
-    sum_out = WholeSum(t, 0, grad_out, up, stages[0], lands[0])
-    sum_here = WholeSum(t, 1, grad_here, down, stages[1], lands[1])
-    sum_there = WholeSum(t, 2, grad_there, up, stages[2], lands[2], x)
+    levels = low_levels + high_levels
+    sum_out = WholeSum(t, 0, grad_out, levels, stages[0], lands[0])
+    sum_here = WholeSum(t, 1, grad_here, levels, stages[1], lands[1])
+    sum_there = WholeSum(t, 2, grad_there, levels, stages[2], lands[2], x)
     small_sum = SmallSum(t, 0, small, [c] + partners, small_lands)
     last_sum = SmallSum(t, 1, small_last, [c] + partners, last_lands)
 
@@ -1405,6 +1434,7 @@
         grad_hidden,
         [router_own, router_far],
         h2,
+        [c_own, c_far],
         [w_gate, w_up, w_down, w_out, gate_got, gate_other, up_got, down_got, down_other],
         up_got,
         width,

time: 701 us -> 691 us (0.986)
  Pallas kernels: 629 us -> 619 us
where the time goes in v4:
time: 691 us; the launch traced here: 684 us
  Pallas kernels  619 us (90%)
  other arithmetic  33.3 us (5%)
  local copies, waits for them, and re-layouts  23.4 us (3%)
  matrix products  7.23 us (1%)
    pallas_call x1, Pallas kernels, back(): pl.pallas_call(functools.partial(back_kernel, levels, bool(grads)), out_s...  188 us
    pallas_call x1, Pallas kernels, front(): pl.pallas_call(front_kernel, out_shape=hbm_outs + vmem_outs, in_specs=[vm...  174 us
    pallas_call x1, Pallas kernels, moe_layer(): pl.pallas_call(moe_kernel, out_shape=[stack, stack] + [jax.ShapeDtypeStru...  155 us
    pallas_call x2, Pallas kernels, weight_grads(): pl.pallas_call(functools.partial(weight_kernel, views, streamed), out_sha...  102 us
    convert_element_type x6, other arithmetic, low(): return value.astype(jnp.bfloat16)  15.1 us

profile of v4, /device:TPU:0, one launch (start us, length us, event | category | flops | bytes accessed | tf_op | source)
XLA Modules:
  0.0 683.9 jit_solution(547304523028046685)
XLA Ops:
  0.7 1.3 broadcast_in_dim.39.refs_10_.refs_12_
  2.0 1.3 broadcast_in_dim.40.refs_11_.refs_13_
  8.2 3.1 fusion.18
  11.3 174.0 %front.1 = (bf16[5,128,768]{2,1,0:T(8,128)(2,1)}, bf16[5,128,768]{2,1,0:T(8,128)(2,1)}, bf16[5,768,128]{2,1,0:T(8,128)(2,1)}, bf16[5,768,128]{2,1,0:T(8,128)(2,1...) custom-call(bf16[512,768]{1,0:T(8,128)(2,1)} %refs_7_.5, ...), custom_call_target="tpu_custom_call" | custom-call | tf_op jit(solution)/shard_map/front/pallas_call | solution.py:504
  185.2 2.8 copy.44
  188.1 154.6 %moe_layer.1 = (bf16[4,2,512,768]{3,2,1,0:T(8,128)(2,1)}, bf16[4,2,512,768]{3,2,1,0:T(8,128)(2,1)}, bf16[4096,768]{1,0:T(8,128)(2,1)}, bf16[4096,768]{1,0:T(8,12...) custom-call(s32[4096,8]{1,0:T(8,128)} %bitcast.89, ...), custom_call_target="tpu_custom_call" | custom-call | tf_op jit(solution)/shard_map/moe_layer/pallas_call | solution.py:818
  342.7 5.4 fusion.23
  348.5 1.8 fusion.22
  351.8 50.7 %expert_weight_grads.2 = (f32[5,192,768]{2,1,0:T(8,128)}, f32[5,192,768]{2,1,0:T(8,128)}, bf16[5,192,768]{2,1,0:T(8,128)(2,1)}, bf16[1,192,768]{2,1,0:T(8,128)(2...) custom-call(bf16[4,2,512,768]{3,2,1,0:T(8,128)(2,1)} %get-tuple-elem, ...), custom_call_target="tpu_custom_call" | custom-call | tf_op jit(solution)/shard_map/expert_weight_grads/pallas_call | solution.py:928
  402.5 5.4 fusion.refs_9_.refs_10_
  407.9 2.9 fusion.1
  410.8 1.3 fusion.9.refs_6_
  412.0 51.7 %expert_weight_grads.3 = (f32[5,192,768]{2,1,0:T(8,128)}, f32[5,192,768]{2,1,0:T(8,128)}, bf16[5,192,768]{2,1,0:T(8,128)(2,1)}, bf16[5,192,768]{2,1,0:T(8,128)(2...) custom-call(bf16[4,2,512,768]{3,2,1,0:T(8,128)(2,1)} %get-tuple-elem, ...), custom_call_target="tpu_custom_call" | custom-call | tf_op jit(solution)/shard_map/expert_weight_grads/pallas_call | solution.py:928
  463.7 2.6 fusion.17.refs_6_
  466.3 1.6 fusion.16
  469.0 1.5 add_convert_fusion.refs_36_
  471.4 187.8 %back.1 = (bf16[512,768]{1,0:T(8,128)(2,1)}, bf16[512,768]{1,0:T(8,128)(2,1)}, bf16[512,768]{1,0:T(8,128)(2,1)}, bf16[512,768]{1,0:T(8,128)(2,1)}, bf16[5,192,76...) custom-call(bf16[768,768]{1,0:T(8,128)(2,1)} %refs_0_.3, ...), custom_call_target="tpu_custom_call" | custom-call | tf_op jit(solution)/shard_map/back/pallas_call | solution.py:1313
  659.3 4.3 fusion.8
  664.1 3.0 fusion.14
  667.1 1.3 slice_reduce_fusion.2
  670.3 1.2 copy_select_fusion
  671.5 5.1 fusion.6
  678.8 1.4 copy.67
  682.2 1.4 copy.70
  (75 shorter events, 15.4 us)
Async XLA Ops:
  6.2 5.1 copy-start.3
  342.7 5.4 copy-start
  342.7 5.8 copy-start.1
  402.5 5.4 copy-start.5
  407.9 2.9 copy-start.20
  407.9 2.9 copy-start.21
  410.7 59.8 %copy-start.2 = (bf16[4,512,768]{2,1,0:T(8,128)(2,1)}, bf16[4,512,768]{2,1,0:T(8,128)(2,1)S(1)}, u32[]{:S(2)}) copy-start(bf16[4,512,768]{2,1,0:T(8,128)(2,1)S(1)} %fusion.1) | copy-start | bytes 9437188
  463.7 2.6 copy-start.10
  466.3 2.4 copy-start.6
  466.3 2.7 copy-start.13
  466.3 2.8 copy-start.22
  659.2 4.4 copy-start.4
  659.2 4.4 copy-start.14
  659.2 4.4 copy-start.15
  659.2 4.6 copy-start.16
  659.3 4.9 copy-start.17
  664.1 4.3 copy-start.23
  664.1 5.6 copy-start.11
  664.1 5.6 copy-start.12
  671.4 5.1 copy-start.9
  676.6 2.2 copy-start.8
  678.8 1.7 copy-start.19
  678.8 2.5 copy-start.18
  678.8 3.4 copy-start.7

commit v5 on v4

--- a/solution.py
+++ b/solution.py
@@ -1542,10 +1542,13 @@
         a, b = a.astype(jnp.float32), b.astype(jnp.float32)
         return jnp.concatenate([jnp.where(index == 0, a, b), jnp.where(index == 0, b, a)], 0)
 
-    expert_grads = in_order(
-        in_order(own_first, own_second, side), in_order(far_first, far_second, side), col
-    )
-    expert_grads = expert_grads.reshape(local, 3, -1, part)
+    def assemble(i, turned):
+        parts = []
+        for p in (own_first, own_second, far_first, far_second):
+            p = p.reshape(split, 3, -1, part)[:, i]
+            parts.append(jnp.swapaxes(p, 1, 2) if turned else p)
+        return in_order(in_order(*parts[:2], side), in_order(*parts[2:], side), col)
+
     output = middle + RESIDUAL * add_wide(moe_own[0], *moe_parts)
     return (
         output,
@@ -1557,9 +1560,9 @@
         grad_out,
         small[SUMMED],
         small[:experts].T,
-        jnp.swapaxes(expert_grads[:, 0], 1, 2),
-        jnp.swapaxes(expert_grads[:, 1], 1, 2),
-        expert_grads[:, 2],
+        assemble(0, True),
+        assemble(1, True),
+        assemble(2, False),
     )
 
 

time: 691 us -> 705 us (1.020)
  Pallas kernels: 619 us -> 629 us
    pallas_call x1, Pallas kernels: 155 us -> 165 us  [moe_layer(): pl.pallas_call(moe_kernel, out_shape=[stack, stack] + [jax.ShapeDtypeStru...]
where the time goes in v5:
time: 705 us; the launch traced here: 698 us
  Pallas kernels  629 us (89%)
  other arithmetic  34.1 us (5%)
  local copies, waits for them, and re-layouts  25.4 us (4%)
  matrix products  7.23 us (1%)
    pallas_call x1, Pallas kernels, back(): pl.pallas_call(functools.partial(back_kernel, levels, bool(grads)), out_s...  188 us
    pallas_call x1, Pallas kernels, front(): pl.pallas_call(front_kernel, out_shape=hbm_outs + vmem_outs, in_specs=[vm...  174 us
    pallas_call x1, Pallas kernels, moe_layer(): pl.pallas_call(moe_kernel, out_shape=[stack, stack] + [jax.ShapeDtypeStru...  165 us
    pallas_call x2, Pallas kernels, weight_grads(): pl.pallas_call(functools.partial(weight_kernel, views, streamed), out_sha...  102 us
    convert_element_type x6, other arithmetic, low(): return value.astype(jnp.bfloat16)  15.1 us

profile of v5, /device:TPU:0, one launch (start us, length us, event | category | flops | bytes accessed | tf_op | source)
XLA Modules:
  0.0 697.6 jit_solution(7048016212260129554)
XLA Ops:
  0.7 1.3 broadcast_in_dim.39.refs_10_.refs_12_
  2.0 1.3 broadcast_in_dim.40.refs_11_.refs_13_
  8.2 3.1 fusion.23
  11.3 173.9 %front.1 = (bf16[5,128,768]{2,1,0:T(8,128)(2,1)}, bf16[5,128,768]{2,1,0:T(8,128)(2,1)}, bf16[5,768,128]{2,1,0:T(8,128)(2,1)}, bf16[5,768,128]{2,1,0:T(8,128)(2,1...) custom-call(bf16[512,768]{1,0:T(8,128)(2,1)} %refs_7_.5, ...), custom_call_target="tpu_custom_call" | custom-call | tf_op jit(solution)/shard_map/front/pallas_call | solution.py:504
  185.2 2.8 copy.52
  188.0 165.3 %moe_layer.1 = (bf16[4,2,512,768]{3,2,1,0:T(8,128)(2,1)}, bf16[4,2,512,768]{3,2,1,0:T(8,128)(2,1)}, bf16[4096,768]{1,0:T(8,128)(2,1)}, bf16[4096,768]{1,0:T(8,12...) custom-call(s32[4096,8]{1,0:T(8,128)} %bitcast.188, ...), custom_call_target="tpu_custom_call" | custom-call | tf_op jit(solution)/shard_map/moe_layer/pallas_call | solution.py:818
  353.4 5.4 fusion.28
  359.2 1.8 fusion.27
  362.5 50.7 %expert_weight_grads.2 = (f32[5,192,768]{2,1,0:T(8,128)}, f32[5,192,768]{2,1,0:T(8,128)}, bf16[5,192,768]{2,1,0:T(8,128)(2,1)}, bf16[1,192,768]{2,1,0:T(8,128)(2...) custom-call(bf16[4,2,512,768]{3,2,1,0:T(8,128)(2,1)} %get-tuple-elem, ...), custom_call_target="tpu_custom_call" | custom-call | tf_op jit(solution)/shard_map/expert_weight_grads/pallas_call | solution.py:928
  413.2 5.4 fusion.refs_9_.refs_10_
  418.6 2.9 fusion.1
  422.7 51.7 %expert_weight_grads.3 = (f32[5,192,768]{2,1,0:T(8,128)}, f32[5,192,768]{2,1,0:T(8,128)}, bf16[5,192,768]{2,1,0:T(8,128)(2,1)}, bf16[5,192,768]{2,1,0:T(8,128)(2...) custom-call(bf16[4,2,512,768]{3,2,1,0:T(8,128)(2,1)} %get-tuple-elem, ...), custom_call_target="tpu_custom_call" | custom-call | tf_op jit(solution)/shard_map/expert_weight_grads/pallas_call | solution.py:928
  474.4 2.6 fusion.22.refs_6_
  477.0 1.6 fusion.21
  479.8 1.5 add_convert_fusion.refs_36_
  482.2 187.8 %back.1 = (bf16[512,768]{1,0:T(8,128)(2,1)}, bf16[512,768]{1,0:T(8,128)(2,1)}, bf16[512,768]{1,0:T(8,128)(2,1)}, bf16[512,768]{1,0:T(8,128)(2,1)}, bf16[5,192,76...) custom-call(bf16[768,768]{1,0:T(8,128)(2,1)} %refs_0_.3, ...), custom_call_target="tpu_custom_call" | custom-call | tf_op jit(solution)/shard_map/back/pallas_call | solution.py:1313
  670.1 2.7 convert_add_fusion.3
  673.7 3.1 fusion.13
  676.7 1.3 slice_reduce_fusion.2
  682.5 2.2 pad_maximum_fusion.2
  685.3 2.2 pad_maximum_fusion.1
  687.5 2.2 pad_maximum_fusion
  691.9 1.4 copy.89
  695.9 1.4 copy.92
  (85 shorter events, 20.7 us)
Async XLA Ops:
  6.2 5.1 copy-start.3
  353.4 5.4 copy-start
  353.4 5.8 copy-start.1
  413.2 5.4 copy-start.5
  418.6 2.9 copy-start.22
  418.6 2.9 copy-start.23
  421.5 59.8 %copy-start.2 = (bf16[4,512,768]{2,1,0:T(8,128)(2,1)}, bf16[4,512,768]{2,1,0:T(8,128)(2,1)S(1)}, u32[]{:S(2)}) copy-start(bf16[4,512,768]{2,1,0:T(8,128)(2,1)S(1)} %fusion.1) | copy-start | bytes 9437188
  474.4 2.6 copy-start.11
  477.0 2.4 copy-start.7
  477.0 2.7 copy-start.15
  477.0 2.8 copy-start.24
  670.0 2.8 copy-start.4
  670.0 2.9 copy-start.16
  670.0 3.2 copy-start.17
  670.0 3.4 copy-start.18
  670.0 3.6 copy-start.19
  673.6 4.4 copy-start.25
  673.6 5.7 copy-start.6
  673.7 5.7 copy-start.14
  679.6 1.8 copy-start.13
  687.5 2.2 copy-start.10
  689.7 2.2 copy-start.9
  691.9 2.6 copy-start.20
  693.6 2.2 copy-start.8
  (2 other events, 3.1 us)
